TPU v7x, 512 devices: a whole 4x4x16 slice. The times are simulated.
512 devices in a mesh: slab: 512 (over x, z, y, core).
Axes of the slice: x: 4, y: 4, z: 16, core: 2. Of those that a mesh axis runs over, the one named last changes fastest.
Arguments:
- load: float32 [3, 1048576], P(None, 'slab'), may hold values from -6 to 6
- element_mats: bfloat16 [12, 12, 1048576], P(None, None, 'slab'), as said below
- connect: int32 [4, 1048576], P(None, 'slab'), may hold values from 0 to 2047, as said below
- shared: int32 [2, 131072], P(None, 'slab'), may hold values from 0 to 2047, as said below
Outputs:
- accel: float32 [3, 1048576], P(None, 'slab')
- residual: float32 [3, 1048576], P(None, 'slab')
Inputs may be any that keep to these rules, and one draw needn't show every extreme that they name: `connect`: slab-local node numbers; the four nodes of an element differ, and every node of a slab belongs to some element of that slab. `shared`: within a slab the 256 numbers of row 0 and of row 1 are all distinct; entry j of a slab's row 1 and entry j of the next slab's row 0 are the same physical node. `element_mats`: each element's matrix is symmetric with a strictly dominant positive diagonal.
All inputs are finite; a program needn't handle non-finite values.
Results may differ from a plain program's by a relative error of at most 0.0003.
Values sent between devices are 32-bit elements; how exact they have to be, the bound alone decides.
No kernel may reach another device: no remote copies, remote signals or barrier semaphores. Data moves between devices by JAX's collectives and lax.ppermute only.
A program may use at most 64 MiB of HBM per device.

v0:
```python
import jax
import jax.numpy as jnp
from jax import lax
from jax.sharding import PartitionSpec as P

ITERS = 4


def extended(cells, sides, width):
    for axis, dim in sides:
        count = lax.axis_size(axis)
        ends = count - 1
        head = lax.slice_in_dim(cells, 0, width, axis=dim)
        tail = lax.slice_in_dim(cells, cells.shape[dim] - width, cells.shape[dim], axis=dim)
        cells = jnp.concatenate(
            [
                lax.ppermute(tail, axis, [(i, (i + 1) % count) for i in range(ends)]),
                cells,
                lax.ppermute(head, axis, [((i + 1) % count, i) for i in range(ends)]),
            ],
            axis=dim,
        )
    return cells


def element_apply(kblock, conn, field):
    gathered = field[:, conn]
    gathered = gathered.transpose(1, 0, 2).reshape(12, -1)
    result = kblock[:, 0, :].astype(jnp.float32) * gathered[0]
    for column in range(1, 12):
        result = result + kblock[:, column, :].astype(jnp.float32) * gathered[column]
    values = result.reshape(4, 3, -1).transpose(1, 0, 2).reshape(3, -1)
    return jnp.zeros(field.shape, jnp.float32).at[:, conn.reshape(-1)].add(values)


def diag_partial(kblock, conn, node_count):
    entries = jnp.stack([kblock[i, i, :].astype(jnp.float32) for i in range(12)])
    values = entries.reshape(4, 3, -1).transpose(1, 0, 2).reshape(3, -1)
    return jnp.zeros((3, node_count), jnp.float32).at[:, conn.reshape(-1)].add(values)


def body(load, element_mats, connect, shared):
    node_count = load.shape[1]
    slab_index = lax.axis_index("slab")
    slab_count = lax.axis_size("slab")
    left_weight = jnp.where(slab_index > 0, jnp.float32(0.5), jnp.float32(1.0))
    right_weight = jnp.where(slab_index < slab_count - 1, jnp.float32(0.5), jnp.float32(1.0))
    weights = (
        jnp.ones((node_count,), jnp.float32)
        .at[shared[0]]
        .set(left_weight)
        .at[shared[1]]
        .set(right_weight)
    )

    def local_inner(first, second):
        return jnp.sum(weights * jnp.sum(first * second, axis=0))

    def assemble(partial_value):
        packed = jnp.stack([partial_value[:, shared[0]], partial_value[:, shared[1]]])
        near = extended(packed, (("slab", 0),), 1)
        return partial_value.at[:, shared[0]].add(near[0]).at[:, shared[1]].add(near[3])

    lumped = diag_partial(element_mats, connect, node_count)
    both = assemble(jnp.concatenate([load, lumped], axis=0))
    force = both[:3]
    diagonal = both[3:]
    accel = jnp.zeros_like(force)
    residual = force

    def precond_sum(resid, prec):
        return lax.psum(local_inner(resid, prec), "slab")

    precond = residual / diagonal
    direction = precond
    gamma = precond_sum(residual, precond)
    for step in range(ITERS):
        image = assemble(element_apply(element_mats, connect, direction))
        alpha = gamma / lax.psum(local_inner(direction, image), "slab")
        accel = accel + alpha * direction
        residual = residual - alpha * image
        precond = residual / diagonal
        gamma_next = precond_sum(residual, precond)
        direction = precond + gamma_next / gamma * direction
        gamma = gamma_next
    return (accel, residual)


def solution(mesh):
    return jax.shard_map(
        body,
        mesh=mesh,
        in_specs=(P(None, "slab"), P(None, None, "slab"), P(None, "slab"), P(None, "slab")),
        out_specs=(P(None, "slab"), P(None, "slab")),
        check_vma=False,
    )
```

profile of v0, /device:TPU:1, one launch (start us, length us, event | category | flops | bytes accessed | tf_op | source)
XLA Modules:
  0.0 1196.9 jit_solution(11886055117771831770)
XLA Ops:
  2.8 2.6 copy.59
  5.8 44.6 %scatter_custom_fusion.2 = f32[3,2048]{0,1:T(8,128)S(1)} fusion(s32[8192]{0:T(1024)S(1)} %bitcast.263, f32[8192,3]{1,0:T(8,128)} %copy.59, f32[]{:T(128)} %constant.13.clone.1), kind=kCustom, calls=%fused_computation.40 | custom fusion | flops 24576 | bytes 25088 | tf_op jit(solution)/shard_map/scatter-add | solution.py:39
  51.5 4.6 collective-permute-start
  57.4 5.5 collective-permute-start.1
  62.9 6.5 convert_reduce_fusion.11
  76.4 2.3 scatter_custom_fusion.3
  78.8 2.5 scatter_custom_fusion.4
  83.6 30.4 %gather_fusion.2 = f32[8192,3]{1,0:T(8,128)} fusion(f32[3,2048]{0,1:T(8,128)S(1)} %copy.63, s32[8192]{0:T(1024)} %broadcast_clamp_fusion), kind=kCustom, calls=%fused_computation.2 | custom fusion | bytes 229376 | tf_op jit(solution)/shard_map/gather | solution.py:27
  114.0 2.8 copy.64
  117.4 2.6 copy.65
  120.0 44.5 %scatter_custom_fusion.5 = f32[3,2048]{0,1:T(8,128)S(1)} fusion(s32[8192]{0:T(1024)} %bitcast.264, f32[8192,3]{1,0:T(8,128)} %copy.65, f32[]{:T(128)} %constant.13.clone.1), kind=kCustom, calls=%fused_computation.38 | custom fusion | flops 24576 | bytes 25088 | tf_op jit(solution)/shard_map/scatter-add | solution.py:33
  166.0 1.9 collective-permute-start.2
  167.9 2.4 collective-permute-start.3
  173.4 2.5 scatter_custom_fusion.6
  175.9 2.3 scatter_custom_fusion.7
  179.2 112.5 %all-reduce = (f32[]{:T(128)}, f32[]{:T(128)}) all-reduce(f32[]{:T(128)} %get-tuple-element.27, f32[]{:T(128)} %get-tuple-element.26), channel_id=1, replica_groups=mesh['slab'=512] {'slab'}, use_global_device_ids=true, to_apply=%region_7.8 | all-reduce | flops 2 | bytes 16 | tf_op jit(solution)/shard_map/psum | solution.py:72
  293.7 98.9 %psum.58 = f32[]{:T(128)} all-reduce(f32[]{:T(128)} %multiply_reduce_fusion.13), channel_id=1, replica_groups=mesh['slab'=512] {'slab'}, use_global_device_ids=true, to_apply=%region_16.17 | all-reduce | flops 1 | bytes 8 | tf_op jit(solution)/shard_map/psum | solution.py:72
  394.3 27.7 %gather_fusion.5 = f32[8192,3]{1,0:T(8,128)} fusion(f32[3,2048]{0,1:T(8,128)S(1)} %copy.68, s32[8192]{0:T(1024)S(1)} %copy-done.10), kind=kCustom, calls=%fused_computation.5 | custom fusion | bytes 229376 | tf_op jit(solution)/shard_map/gather | solution.py:27
  422.0 2.8 copy.69
  425.3 2.6 copy.70
  427.9 44.5 %scatter_custom_fusion.8 = f32[3,2048]{0,1:T(8,128)S(1)} fusion(s32[8192]{0:T(1024)} %bitcast.265, f32[8192,3]{1,0:T(8,128)} %copy.70, f32[]{:T(128)} %constant.13.clone.1), kind=kCustom, calls=%fused_computation.36 | custom fusion | flops 24576 | bytes 25088 | tf_op jit(solution)/shard_map/scatter-add | solution.py:33
  473.9 3.3 collective-permute-start.4
  477.3 1.9 collective-permute-start.5
  479.2 2.5 scatter_custom_fusion.9
  481.7 1.9 collective-permute-done.5
  483.6 2.3 scatter_custom_fusion.10
  486.9 105.1 %psum.59 = f32[]{:T(128)} all-reduce(f32[]{:T(128)} %multiply_reduce_fusion.12), channel_id=1, replica_groups=mesh['slab'=512] {'slab'}, use_global_device_ids=true, to_apply=%region_22.23 | all-reduce | flops 1 | bytes 8 | tf_op jit(solution)/shard_map/psum | solution.py:79
  593.9 99.7 %psum.60 = f32[]{:T(128)} all-reduce(f32[]{:T(128)} %multiply_reduce_fusion.11), channel_id=1, replica_groups=mesh['slab'=512] {'slab'}, use_global_device_ids=true, to_apply=%region_25.26 | all-reduce | flops 1 | bytes 8 | tf_op jit(solution)/shard_map/psum | solution.py:72
  695.3 27.7 %gather_fusion.8 = f32[8192,3]{1,0:T(8,128)} fusion(f32[3,2048]{0,1:T(8,128)S(1)} %copy.73, s32[8192]{0:T(1024)S(1)} %copy-done.10), kind=kCustom, calls=%fused_computation.8 | custom fusion | bytes 229376 | tf_op jit(solution)/shard_map/gather | solution.py:27
  723.0 2.8 copy.74
  726.3 2.6 copy.75
  728.9 44.5 %scatter_custom_fusion.11 = f32[3,2048]{0,1:T(8,128)S(1)} fusion(s32[8192]{0:T(1024)} %bitcast.266, f32[8192,3]{1,0:T(8,128)} %copy.75, f32[]{:T(128)} %constant.13.clone.1), kind=kCustom, calls=%fused_computation.34 | custom fusion | flops 24576 | bytes 25088 | tf_op jit(solution)/shard_map/scatter-add | solution.py:33
  774.9 3.6 collective-permute-start.6
  778.5 1.9 collective-permute-start.7
  780.5 2.5 scatter_custom_fusion.12
  784.8 2.3 scatter_custom_fusion.13
  788.1 105.1 %psum.61 = f32[]{:T(128)} all-reduce(f32[]{:T(128)} %multiply_reduce_fusion.10), channel_id=1, replica_groups=mesh['slab'=512] {'slab'}, use_global_device_ids=true, to_apply=%region_31.32 | all-reduce | flops 1 | bytes 8 | tf_op jit(solution)/shard_map/psum | solution.py:79
  895.2 99.8 %psum.62 = f32[]{:T(128)} all-reduce(f32[]{:T(128)} %multiply_reduce_fusion.9), channel_id=1, replica_groups=mesh['slab'=512] {'slab'}, use_global_device_ids=true, to_apply=%region_34.35 | all-reduce | flops 1 | bytes 8 | tf_op jit(solution)/shard_map/psum | solution.py:72
  996.7 27.7 %gather_fusion.11 = f32[8192,3]{1,0:T(8,128)} fusion(f32[3,2048]{0,1:T(8,128)S(1)} %copy.78, s32[8192]{0:T(1024)S(1)} %copy-done.10), kind=kCustom, calls=%fused_computation.11 | custom fusion | bytes 229376 | tf_op jit(solution)/shard_map/gather | solution.py:27
  1024.4 2.8 copy.79
  1027.6 2.6 copy.80
  1030.3 44.5 %scatter_custom_fusion.14 = f32[3,2048]{0,1:T(8,128)S(1)} fusion(s32[8192]{0:T(1024)} %bitcast.267, f32[8192,3]{1,0:T(8,128)} %copy.80, f32[]{:T(128)} %constant.13.clone.1), kind=kCustom, calls=%fused_computation.32 | custom fusion | flops 24576 | bytes 25088 | tf_op jit(solution)/shard_map/scatter-add | solution.py:33
  1076.3 3.5 collective-permute-start.8
  1079.8 1.9 collective-permute-start.9
  1081.7 2.5 scatter_custom_fusion.15
  1084.2 1.9 collective-permute-done.9
  1086.0 2.3 scatter_custom_fusion.16
  1089.4 105.1 %psum.63 = f32[]{:T(128)} all-reduce(f32[]{:T(128)} %multiply_reduce_fusion.8), channel_id=1, replica_groups=mesh['slab'=512] {'slab'}, use_global_device_ids=true, to_apply=%region_40.41 | all-reduce | flops 1 | bytes 8 | tf_op jit(solution)/shard_map/psum | solution.py:79
  (133 shorter events, 34.1 us)
Async XLA Ops:
  0.6 4.8 copy-start.16
  0.6 5.1 copy-start.21
  1.5 4.3 copy-start.17
  5.4 64.0 %copy-start.15 = (s32[4,2048]{1,0:T(4,128)S(1)}, s32[4,2048]{1,0:T(4,128)}, u32[]{:S(2)}) copy-start(s32[4,2048]{1,0:T(4,128)} %param.6) | copy-start | bytes 98308
  5.8 70.6 %copy-start.20 = (s32[256,1]{0,1:T(1,128)}, s32[256,1]{0,1:T(1,128)S(1)}, u32[]{:S(2)}) copy-start(s32[256,1]{0,1:T(1,128)S(1)} %get-tuple-element.102) | copy-start | bytes 3076
  5.8 73.0 %copy-start.18 = (s32[256,1]{0,1:T(1,128)}, s32[256,1]{0,1:T(1,128)S(1)}, u32[]{:S(2)}) copy-start(s32[256,1]{0,1:T(1,128)S(1)} %get-tuple-element.101) | copy-start | bytes 3076
  51.5 24.9 %collective-permute-start = (f32[1,6,256]{1,2,0:T(8,128)S(1)}, f32[1,6,256]{1,2,0:T(8,128)S(1)}, u32[]{:S(2)}, u32[]{:S(2)}) collective-permute-start(f32[1,6,256]{1,2,0:T(8,128)S(1)} %bitcast.282), channel_id=1, source_target_pairs={{0,1},{1,2},{2,3},{3,4},{4,5},{5,6},{6,7},{7,8},{8,9},{9,10},{10,1... | collective-permute-start | bytes 18440 | tf_op jit(solution)/shard_map/ppermute | solution.py:17
  57.4 21.3 %collective-permute-start.1 = (f32[1,6,256]{1,2,0:T(8,128)}, f32[1,6,256]{1,2,0:T(8,128)S(1)}, u32[]{:S(2)}, u32[]{:S(2)}) collective-permute-start(f32[1,6,256]{1,2,0:T(8,128)} %bitcast.25), channel_id=1, source_target_pairs={{1,0},{2,1},{3,2},{4,3},{5,4},{6,5},{7,6},{8,7},{9,8},{10,9},{11,1... | collective-permute-start | bytes 18440 | tf_op jit(solution)/shard_map/ppermute | solution.py:19
  82.0 0.6 copy-start.11
  82.0 35.0 %copy-start = (f32[4,3,2048]{2,1,0:T(4,128)S(1)}, f32[4,3,2048]{2,1,0:T(4,128)}, u32[]{:S(2)}) copy-start(f32[4,3,2048]{2,1,0:T(4,128)} %reshape.611) | copy-start | bytes 294916
  82.0 35.0 %copy-start.1 = (f32[4,3,2048]{2,1,0:T(4,128)S(1)}, f32[4,3,2048]{2,1,0:T(4,128)}, u32[]{:S(2)}) copy-start(f32[4,3,2048]{2,1,0:T(4,128)} %reshape.610) | copy-start | bytes 294916
  82.0 35.0 %copy-start.2 = (f32[4,3,2048]{2,1,0:T(4,128)S(1)}, f32[4,3,2048]{2,1,0:T(4,128)}, u32[]{:S(2)}) copy-start(f32[4,3,2048]{2,1,0:T(4,128)} %reshape.609) | copy-start | bytes 294916
  82.0 35.0 %copy-start.3 = (f32[4,3,2048]{2,1,0:T(4,128)S(1)}, f32[4,3,2048]{2,1,0:T(4,128)}, u32[]{:S(2)}) copy-start(f32[4,3,2048]{2,1,0:T(4,128)} %reshape.608) | copy-start | bytes 294916
  82.0 35.0 %copy-start.4 = (f32[4,3,2048]{2,1,0:T(4,128)S(1)}, f32[4,3,2048]{2,1,0:T(4,128)}, u32[]{:S(2)}) copy-start(f32[4,3,2048]{2,1,0:T(4,128)} %reshape.607) | copy-start | bytes 294916
  82.0 35.0 %copy-start.5 = (f32[4,3,2048]{2,1,0:T(4,128)S(1)}, f32[4,3,2048]{2,1,0:T(4,128)}, u32[]{:S(2)}) copy-start(f32[4,3,2048]{2,1,0:T(4,128)} %reshape.606) | copy-start | bytes 294916
  82.0 35.0 %copy-start.6 = (f32[4,3,2048]{2,1,0:T(4,128)S(1)}, f32[4,3,2048]{2,1,0:T(4,128)}, u32[]{:S(2)}) copy-start(f32[4,3,2048]{2,1,0:T(4,128)} %reshape.605) | copy-start | bytes 294916
  82.0 35.0 %copy-start.7 = (f32[4,3,2048]{2,1,0:T(4,128)S(1)}, f32[4,3,2048]{2,1,0:T(4,128)}, u32[]{:S(2)}) copy-start(f32[4,3,2048]{2,1,0:T(4,128)} %reshape.604) | copy-start | bytes 294916
  82.1 35.0 %copy-start.8 = (f32[4,3,2048]{2,1,0:T(4,128)S(1)}, f32[4,3,2048]{2,1,0:T(4,128)}, u32[]{:S(2)}) copy-start(f32[4,3,2048]{2,1,0:T(4,128)} %reshape.603) | copy-start | bytes 294916
  82.6 0.6 copy-start.13
  116.8 55.1 %copy-start.19 = (s32[256,1]{0,1:T(1,128)S(1)}, s32[256,1]{0,1:T(1,128)}, u32[]{:S(2)}) copy-start(s32[256,1]{0,1:T(1,128)} %copy-done.18) | copy-start | bytes 3076
  120.0 58.6 %copy-start.14 = (f32[3,2048]{1,0:T(4,128)S(1)}, f32[3,2048]{1,0:T(4,128)}, u32[]{:S(2)}) copy-start(f32[3,2048]{1,0:T(4,128)} %copy-done.13) | copy-start | bytes 73732
  120.0 173.0 %copy-start.12 = (f32[3,2048]{1,0:T(4,128)S(1)}, f32[3,2048]{1,0:T(4,128)}, u32[]{:S(2)}) copy-start(f32[3,2048]{1,0:T(4,128)} %copy-done.11) | copy-start | bytes 73732
  120.0 274.3 %copy-start.10 = (s32[8192]{0:T(1024)S(1)}, s32[8192]{0:T(1024)}, u32[]{:S(2)}) copy-start(s32[8192]{0:T(1024)} %broadcast_clamp_fusion) | copy-start | bytes 98308
  166.0 7.4 collective-permute-start.2
  167.9 7.9 collective-permute-start.3
  178.2 246.8 %copy-start.9 = (f32[4,3,2048]{2,1,0:T(4,128)S(1)}, f32[4,3,2048]{2,1,0:T(4,128)}, u32[]{:S(2)}) copy-start(f32[4,3,2048]{2,1,0:T(4,128)} %reshape.603) | copy-start | bytes 294916
  473.9 5.3 collective-permute-start.4
  477.3 6.3 collective-permute-start.5
  774.9 5.5 collective-permute-start.6
  778.5 6.3 collective-permute-start.7
  1076.3 5.4 collective-permute-start.8
  1079.8 6.3 collective-permute-start.9
where the time goes:
time: 1210 us; the launch traced here: 1200 us
  blocking collectives  726 us (60%)
  other arithmetic  261 us (22%)
  local copies, waits for them, and re-layouts  163 us (13%)
  starting transfers between devices  30.6 us (3%)
    psum x4, blocking collectives, precond_sum(): return lax.psum(local_inner(resid, prec), 'slab')  411 us
    psum x3, blocking collectives, body(): alpha = gamma / lax.psum(local_inner(direction, image), 'slab')  315 us
    scatter-add x4, other arithmetic, element_apply(): jnp.zeros(field.shape, jnp.float32).at[:, conn.reshape(-1)].add(values)  178 us
    gather x8, local copies, waits for them, and re-layouts, element_apply(): gathered = field[:, conn]  125 us
    scatter-add x1, other arithmetic, diag_partial(): jnp.zeros((3, node_count), jnp.float32).at[:, conn.reshape(-1)].add(values)  44.6 us
  transfers between devices with their start and end apart: 10, of which 3 were waited for; matrix products, arithmetic and copies ran while one was open for 3% of the time, Pallas kernels for 0%

commit v1 on v0

v1 whole, which is shorter than its diff:
```python
import jax
import jax.numpy as jnp
from jax import lax
from jax.experimental import pallas as pl
from jax.experimental.pallas import tpu as pltpu
from jax.sharding import Mesh, PartitionSpec as P

ITERS = 4
AXES = ("x", "z", "y", "c")
GROUP = ("x", "y", "c")
NODES = 2048
ELEMS = 2048
SHARED = 256
SPLITS = 3
PIVOT_FLOOR = 1e-3
F32 = jnp.float32
BF16 = jnp.bfloat16
VMEM_LIMIT = 32 * 1024 * 1024


def iota(shape, dim):
    return lax.broadcasted_iota(jnp.int32, shape, dim)


def lane_take(table, lanes):
    return jnp.take_along_axis(table, lanes, axis=1, mode="promise_in_bounds")


def pick(parts, high):
    bit = 0
    while len(parts) > 1:
        odd = (high & (1 << bit)) != 0
        parts = [jnp.where(odd, parts[i + 1], parts[i]) for i in range(0, len(parts), 2)]
        bit += 1
    return parts[0]


def field_rows(field, block):
    high, half = block >> 1, block & 1
    return [
        jnp.broadcast_to(field[c * 8 + high : c * 8 + high + 1, half * 128 : half * 128 + 128], (8, 128))
        for c in range(3)
    ]


def by_component(rows, comp):
    return jnp.where(comp == 0, rows[0], jnp.where(comp == 1, rows[1], rows[2]))


def halos_of(field, lists):
    comp = iota((8, 128), 0) // 2
    tables = [by_component(field_rows(field, block), comp) for block in range(16)]
    out = []
    for nodes in lists:
        out.append(pick([lane_take(t, nodes & 127) for t in tables], nodes >> 7))
    return out


def assembled(field, inverse, near):
    columns = []
    for half in range(2):
        where_from = inverse[:, half * 128 : half * 128 + 128]
        lanes, code = where_from & 127, where_from >> 7
        rows = []
        for c in range(3):
            tile = field[c * 8 : c * 8 + 8, half * 128 : half * 128 + 128]
            parts = []
            for t in range(4):
                row = 2 * c + (t & 1)
                table = jnp.broadcast_to(near[t >> 1][row : row + 1, :], (8, 128))
                parts.append(lane_take(table, lanes))
            gain = pick(parts, code)
            rows.append(tile + jnp.where(code < 0, 0.0, gain))
        columns.append(jnp.concatenate(rows, axis=0))
    return jnp.concatenate(columns, axis=1)


def corner_lhs(values, conn, comps):
    width = values.shape[1]
    sub = iota((8, width), 0)
    parts = []
    rest = values
    for _ in range(SPLITS - 1):
        top = rest.astype(BF16).astype(F32)
        parts.append(top)
        rest = rest - top
    parts.append(rest)
    out = []
    for n in range(4):
        mask = jnp.broadcast_to(conn[n : n + 1, :] >> 8, (8, width)) == sub
        tiles = []
        for part in parts:
            for c in range(comps):
                row = n * comps + c
                tiles.append(jnp.where(mask, jnp.broadcast_to(part[row : row + 1, :], (8, width)), 0.0))
        if len(tiles) % 2:
            tiles.append(jnp.zeros((8, width), F32))
        out.append(jnp.concatenate(tiles, axis=0).astype(BF16))
    return out


def one_hot(nodes):
    width = nodes.shape[1]
    low = jnp.broadcast_to((nodes & 255).astype(F32), (256, width)).astype(BF16)
    rows = iota((256, width), 0).astype(F32).astype(BF16)
    return jnp.where(rows == low, jnp.ones((), BF16), jnp.zeros((), BF16))


def times_one_hot(lhs, nodes):
    return lax.dot_general(lhs, one_hot(nodes), (((1,), (1,)), ((), ())), preferred_element_type=F32)


def fold_splits(total):
    out = total[0:24]
    for s in range(1, SPLITS):
        out = out + total[24 * s : 24 * s + 24]
    return out


def scatter(values_of, conn_ref):
    total = None
    for block in range(ELEMS // 256):
        start = block * 256
        conn = conn_ref[:, start : start + 256]
        lhs = corner_lhs(values_of(start), conn, 3)
        for n in range(4):
            piece = times_one_hot(lhs[n], conn[n : n + 1, :])
            total = piece if total is None else total + piece
    return fold_splits(total)


def first_kernel(load_ref, mats_ref, conn_ref, shared_ref, load_out, lumped_out, index_out, inverse_out, lists_out, a_out, b_out):
    odd = lax.axis_index("c") == 1
    own = shared_ref[...]
    row0, row1 = own[0:1, :], own[1:2, :]
    side_a = jnp.where(odd, row0, row1)
    side_b = jnp.where(odd, row1, row0)

    sub8 = iota((8, 128), 0)
    lists = []
    for side in (side_a, side_b):
        first = jnp.broadcast_to(side[:, 0:128], (8, 128))
        second = jnp.broadcast_to(side[:, 128:256], (8, 128))
        lists.append(jnp.where((sub8 & 1) == 0, first, second))
    lists_out[0:8, :] = lists[0]
    lists_out[8:16, :] = lists[1]

    sub = iota((8, 256), 0)
    lane = iota((8, 256), 1)
    found = None
    for t, side in enumerate((side_a, side_b)):
        mask = jnp.broadcast_to(side >> 8, (8, 256)) == sub
        place = jnp.where(mask, (lane & 127).astype(F32), 0.0)
        code = jnp.where(mask, (2 * t + (lane >> 7) + 1).astype(F32), 0.0)
        piece = times_one_hot(jnp.concatenate([place, code], axis=0).astype(BF16), side)
        found = piece if found is None else found + piece
    inverse_out[...] = (found[8:16].astype(jnp.int32) - 1) * 128 + found[0:8].astype(jnp.int32)

    for c in range(3):
        for h in range(8):
            load_out[c * 8 + h : c * 8 + h + 1, :] = load_ref[c : c + 1, h * 256 : h * 256 + 256]

    for j in range(12):
        index_out[j : j + 1, :] = conn_ref[j // 3 : j // 3 + 1, :]
    index_out[12:16, :] = jnp.zeros((4, ELEMS), jnp.int32)

    row12 = iota((12, 256), 0)

    def diagonal_of(start):
        out = jnp.zeros((12, 256), F32)
        for j in range(12):
            out = jnp.where(row12 == j, mats_ref[j, :, start : start + 256].astype(F32), out)
        return out

    lumped = scatter(diagonal_of, conn_ref)
    lumped_out[...] = lumped
    load_a, load_b = halos_of(load_out[...], lists)
    lump_a, lump_b = halos_of(lumped, lists)
    a_out[0:8, :] = load_a
    a_out[8:16, :] = lump_a
    b_out[0:8, :] = load_b
    b_out[8:16, :] = lump_b


def apply_off_diagonal(field, mats_ref, conn_ref, index_ref, table_ref):
    sub = iota((8, 128), 0)
    for block in range(16):
        rows = field_rows(field, block)
        table_ref[block, 0:8, :] = by_component(rows, sub % 3)
        table_ref[block, 8:16, :] = by_component(rows, (sub + 2) % 3)
    row12 = iota((12, 128), 0)

    def product(start):
        index = index_ref[:, start : start + 128]
        gathered = []
        for t in range(2):
            nodes = index[8 * t : 8 * t + 8]
            lanes = nodes & 127
            gathered.append(pick([lane_take(table_ref[block, 8 * t : 8 * t + 8, :], lanes) for block in range(16)], nodes >> 7))
        out = jnp.zeros((12, 128), F32)
        for j in range(12):
            column = mats_ref[j, :, start : start + 128].astype(F32)
            column = jnp.where(row12 == j, 0.0, column)
            value = gathered[j // 8][j % 8 : j % 8 + 1, :]
            out = out + column * jnp.broadcast_to(value, (12, 128))
        return out

    def values_of(start):
        return jnp.concatenate([product(start), product(start + 128)], axis=1)

    return scatter(values_of, conn_ref)


def tile_sum(product):
    out = None
    for c in range(3):
        for half in range(2):
            tile = product[c * 8 : c * 8 + 8, half * 128 : half * 128 + 128]
            out = tile if out is None else out + tile
    return out


def step(basis, lumped_ref, mats_ref, conn_ref, index_ref, lists_ref, table_ref, image_out, sums_out):
    image = apply_off_diagonal(basis, mats_ref, conn_ref, index_ref, table_ref)
    image_out[...] = image
    sums_out[0:8, :] = tile_sum(basis * basis * lumped_ref[...])
    sums_out[8:16, :] = tile_sum(basis * image)
    return halos_of(image, [lists_ref[0:8, :], lists_ref[8:16, :]])


def second_kernel(
    load_ref, lumped_ref, inverse_ref, lists_ref, index_ref, conn_ref, mats_ref, near_a, near_b,
    diag_out, basis_out, image_out, sums_out, a_out, b_out, table_ref,
):
    inverse = inverse_ref[...]
    force = assembled(load_ref[...], inverse, [near_a[0:8, :], near_b[0:8, :]])
    diag = assembled(lumped_ref[...], inverse, [near_a[8:16, :], near_b[8:16, :]])
    basis = force / diag
    diag_out[...] = diag
    basis_out[...] = basis
    halos = step(basis, lumped_ref, mats_ref, conn_ref, index_ref, lists_ref, table_ref, image_out, sums_out)
    a_out[...] = halos[0]
    b_out[...] = halos[1]


def middle_kernel(
    past_ref, diag_ref, lumped_ref, inverse_ref, lists_ref, index_ref, conn_ref, mats_ref, near_a, near_b,
    basis_out, image_out, sums_out, a_out, b_out, table_ref,
):
    basis = assembled(past_ref[...], inverse_ref[...], [near_a[...], near_b[...]]) / diag_ref[...]
    basis_out[...] = basis
    halos = step(basis, lumped_ref, mats_ref, conn_ref, index_ref, lists_ref, table_ref, image_out, sums_out)
    a_out[...] = halos[0]
    b_out[...] = halos[1]


def place():
    return tuple(lax.axis_index(a) for a in AXES)


def slab_slot(slab):
    return (slab // 128) * 8 + slab % 8


def fourth_kernel(
    past_ref, diag_ref, lumped_ref, inverse_ref, lists_ref, index_ref, conn_ref, mats_ref, near_a, near_b, sums0, sums1, sums2,
    basis_out, image_out, message_out, table_ref, sums_ref,
):
    basis = assembled(past_ref[...], inverse_ref[...], [near_a[...], near_b[...]]) / diag_ref[...]
    basis_out[...] = basis
    halos = step(basis, lumped_ref, mats_ref, conn_ref, index_ref, lists_ref, table_ref, image_out, sums_ref)
    lane = iota((8, 128), 1)
    sub = iota((8, 128), 0)
    moments = jnp.zeros((8, 128), F32)
    for k, ref in enumerate((sums0, sums1, sums2, sums_ref)):
        for t in range(2):
            total = jnp.sum(ref[8 * t : 8 * t + 8, :], axis=0, keepdims=True)
            total = jnp.sum(jnp.broadcast_to(total, (8, 128)), axis=1, keepdims=True)
            moments = jnp.where(lane == 2 * k + t, total, moments)
    moments = jnp.where(sub == 6, moments, 0.0)
    message_out[...] = jnp.broadcast_to(moments[None], (32, 8, 128))
    x, z, y, c = place()
    slab = ((x * 16 + z) * 4 + y) * 2 + c
    odd = c == 1
    to_right = jnp.where(sub < 6, jnp.where(odd, halos[1], halos[0]), moments)
    to_left = jnp.where(sub < 6, jnp.where(odd, halos[0], halos[1]), moments)

    @pl.when(slab < 511)
    def _():
        message_out[slab_slot(jnp.minimum(slab + 1, 511))] = to_right

    @pl.when(slab > 0)
    def _():
        message_out[slab_slot(jnp.maximum(slab - 1, 0))] = to_left


def relay_kernel(message_ref, message_out, direct_out):
    x, z, y, c = place()
    slot = x * 8 + y * 2 + c
    first = (y == 0) & (c == 0)
    last = (y == 3) & (c == 1)
    sub = iota((8, 128), 0)
    moments = message_ref[0]
    for i in range(1, 32):
        moments = moments + message_ref[i]
    moments = jnp.where(sub == 6, moments, 0.0)
    message_out[...] = jnp.broadcast_to(moments[None], (16, 8, 128))
    source_r = jnp.where(first, jnp.where(z < 15, x * 8 + 7, jnp.maximum(x * 8 - 1, 0)), jnp.maximum(slot - 1, 0))
    source_l = jnp.where(last, jnp.where(z > 0, x * 8, jnp.minimum(x * 8 + 8, 31)), jnp.minimum(slot + 1, 31))
    from_left = message_ref[source_r]
    from_right = message_ref[source_l]
    direct_out[0:8, :] = from_left
    direct_out[8:16, :] = from_right

    @pl.when(first)
    def _():
        message_out[(z + 1) % 16] = jnp.where(sub < 6, from_left, moments)

    @pl.when(last)
    def _():
        message_out[(z + 15) % 16] = jnp.where(sub < 6, from_right, moments)


def coefficients(moment):
    zero, one = jnp.zeros((8, 128), F32), jnp.ones((8, 128), F32)
    scale = [jnp.where(moment[2 * i] > 0.0, lax.rsqrt(jnp.where(moment[2 * i] > 0.0, moment[2 * i], one)), zero) for i in range(4)]
    rows = [[moment[i + j] * scale[i] * scale[j] for j in range(4)] + [-moment[i + 4] * scale[i]] for i in range(4)]
    least = one
    inverse = []
    for i in range(4):
        pivot = rows[i][i]
        good = pivot > 1e-6
        least = jnp.minimum(least, jnp.where(good, pivot, zero))
        inverse.append(jnp.where(good, one / jnp.where(good, pivot, one), zero))
        for j in range(i + 1, 4):
            ratio = rows[j][i] * inverse[i]
            for k in range(i + 1, 5):
                rows[j][k] = rows[j][k] - ratio * rows[i][k]
    coef = [zero] * 4
    for i in (3, 2, 1, 0):
        total = rows[i][4]
        for j in range(i + 1, 4):
            total = total - rows[i][j] * coef[j]
        coef[i] = total * inverse[i]
    coef = [coef[i] * scale[i] for i in range(4)]
    at = coef[0] - coef[1] + coef[2] - coef[3] + one
    resid = [v / at for v in coef] + [one / at]
    accel = [None] * 4
    accel[3] = -resid[4]
    for i in (2, 1, 0):
        accel[i] = -resid[i + 1] - accel[i + 1]
    good = (least > PIVOT_FLOOR) & (at > 0.0)
    return accel, resid, good


def last_kernel(message_ref, direct_ref, image_ref, diag_ref, inverse_ref, b0, b1, b2, b3, accel_out, resid_out, flag_out):
    x, z, y, c = place()
    slab = ((x * 16 + z) * 4 + y) * 2 + c
    first = (y == 0) & (c == 0)
    last = (y == 3) & (c == 1)
    lane = iota((8, 128), 1)
    total = message_ref[0]
    for i in range(1, 16):
        total = total + message_ref[i]
    total = jnp.broadcast_to(total[6:7, :], (8, 128))
    moment = [
        jnp.broadcast_to(jnp.sum(jnp.where(lane == k, total, 0.0), axis=1, keepdims=True), (8, 128)) for k in range(8)
    ]
    accel_coef, resid_coef, good = coefficients(moment)
    from_left = jnp.where(first, message_ref[(z + 15) % 16], direct_ref[0:8, :])
    from_right = jnp.where(last, message_ref[(z + 1) % 16], direct_ref[8:16, :])
    from_left = jnp.where(slab > 0, from_left, 0.0)
    from_right = jnp.where(slab < 511, from_right, 0.0)
    odd = c == 1
    near = [jnp.where(odd, from_left, from_right), jnp.where(odd, from_right, from_left)]
    diag = diag_ref[...]
    image = assembled(image_ref[...], inverse_ref[...], near)
    for c_ in range(3):
        for half in range(2):
            at = (slice(c_ * 8, c_ * 8 + 8), slice(half * 128, half * 128 + 128))
            basis = [r[at] for r in (b0, b1, b2, b3)]
            accel = basis[3] * accel_coef[3]
            resid = image[at] * resid_coef[4]
            part = basis[3] * resid_coef[3]
            for k in (2, 1, 0):
                accel = accel + basis[k] * accel_coef[k]
                part = part + basis[k] * resid_coef[k]
            resid = resid + diag[at] * part
            for h in range(8):
                lanes = slice(h * 256 + half * 128, h * 256 + half * 128 + 128)
                accel_out[c_ : c_ + 1, lanes] = accel[h : h + 1, :]
                resid_out[c_ : c_ + 1, lanes] = resid[h : h + 1, :]
    flag_out[0, 0] = jnp.min(jnp.where(good, 1, 0))


def call(kernel, outs, *args, scratch=(), smem_out=None):
    vmem = pl.BlockSpec(memory_space=pltpu.VMEM)
    out_specs = [vmem] * len(outs)
    if smem_out is not None:
        out_specs[smem_out] = pl.BlockSpec(memory_space=pltpu.SMEM)
    return pl.pallas_call(
        kernel,
        out_shape=[jax.ShapeDtypeStruct(s, t) for s, t in outs],
        in_specs=[vmem] * len(args),
        out_specs=out_specs,
        scratch_shapes=list(scratch),
        compiler_params=pltpu.CompilerParams(vmem_limit_bytes=VMEM_LIMIT),
    )(*args)


def swap(side_a, side_b):
    count = 512
    from_b = lax.ppermute(side_b, AXES, [(i, ((i + 1) ^ 1) - 1) for i in range(1, count - 1)])
    from_a = lax.ppermute(side_a, AXES, [(i, i ^ 1) for i in range(count)])
    return from_a, from_b


def plain(load, element_mats, connect, shared):
    node_count = load.shape[1]
    slab_index = lax.axis_index(AXES)
    slab_count = 512
    left_weight = jnp.where(slab_index > 0, F32(0.5), F32(1.0))
    right_weight = jnp.where(slab_index < slab_count - 1, F32(0.5), F32(1.0))
    weights = jnp.ones((node_count,), F32).at[shared[0]].set(left_weight).at[shared[1]].set(right_weight)

    def inner(first, second):
        return lax.psum(jnp.sum(weights * jnp.sum(first * second, axis=0)), AXES)

    def assemble(partial_value):
        from_left = lax.ppermute(partial_value[:, shared[1]], AXES, [(i, i + 1) for i in range(slab_count - 1)])
        from_right = lax.ppermute(partial_value[:, shared[0]], AXES, [(i + 1, i) for i in range(slab_count - 1)])
        return partial_value.at[:, shared[0]].add(from_left).at[:, shared[1]].add(from_right)

    def spread(values):
        values = values.reshape(4, 3, -1).transpose(1, 0, 2).reshape(3, -1)
        return jnp.zeros((3, node_count), F32).at[:, connect.reshape(-1)].add(values)

    def element_apply(field):
        gathered = field[:, connect].transpose(1, 0, 2).reshape(12, -1)
        result = element_mats[:, 0, :].astype(F32) * gathered[0]
        for column in range(1, 12):
            result = result + element_mats[:, column, :].astype(F32) * gathered[column]
        return spread(result)

    lumped = spread(jnp.stack([element_mats[i, i, :].astype(F32) for i in range(12)]))
    both = assemble(jnp.concatenate([load, lumped], axis=0))
    residual, diagonal = both[:3], both[3:]
    direction = residual / diagonal
    accel = jnp.zeros_like(residual)
    gamma = inner(residual, direction)

    def body(_, carry):
        accel, residual, direction, gamma = carry
        image = assemble(element_apply(direction))
        alpha = gamma / inner(direction, image)
        accel = accel + alpha * direction
        residual = residual - alpha * image
        precond = residual / diagonal
        following = inner(residual, precond)
        return accel, residual, precond + following / gamma * direction, following

    accel, residual, _, _ = lax.fori_loop(0, ITERS, body, (accel, residual, direction, gamma))
    return accel, residual


def body(load, element_mats, connect, shared):
    field = ((24, 256), F32)
    halo = ((8, 128), F32)
    sums = ((16, 128), F32)
    table = pltpu.VMEM((16, 16, 128), F32)
    load_f, lumped, index, inverse, lists, a, b = call(
        first_kernel,
        [field, field, ((16, ELEMS), jnp.int32), ((8, 256), jnp.int32), ((16, 128), jnp.int32), sums, sums],
        load, element_mats, connect, shared,
    )
    a, b = swap(a, b)
    diag, b0, image, sums0, a, b = call(
        second_kernel,
        [field, field, field, sums, halo, halo],
        load_f, lumped, inverse, lists, index, connect, element_mats, a, b,
        scratch=[table],
    )
    bases, totals = [b0], [sums0]
    for _ in range(2):
        a, b = swap(a, b)
        basis, image, total, a, b = call(
            middle_kernel,
            [field, field, sums, halo, halo],
            image, diag, lumped, inverse, lists, index, connect, element_mats, a, b,
            scratch=[table],
        )
        bases.append(basis)
        totals.append(total)
    a, b = swap(a, b)
    basis, image, message = call(
        fourth_kernel,
        [field, field, ((32, 8, 128), F32)],
        image, diag, lumped, inverse, lists, index, connect, element_mats, a, b, *totals,
        scratch=[table, pltpu.VMEM((16, 128), F32)],
    )
    bases.append(basis)
    message = lax.all_to_all(message, GROUP, 0, 0, tiled=True)
    message, direct = call(relay_kernel, [((16, 8, 128), F32), sums], message)
    message = lax.all_to_all(message, "z", 0, 0, tiled=True)
    accel, residual, flag = call(
        last_kernel,
        [((3, NODES), F32), ((3, NODES), F32), ((1, 1), jnp.int32)],
        message, direct, image, diag, inverse, *bases,
        smem_out=2,
    )

    def again(carry):
        return (jnp.int32(1),) + plain(load, element_mats, connect, shared)

    _, accel, residual = lax.while_loop(lambda carry: carry[0] == 0, again, (flag.reshape(()), accel, residual))
    return accel, residual


def solution(mesh):
    parts = Mesh(mesh.devices.reshape(4, 16, 4, 2), AXES)
    return jax.shard_map(
        body,
        mesh=parts,
        in_specs=(P(None, AXES), P(None, None, AXES), P(None, AXES), P(None, AXES)),
        out_specs=(P(None, AXES), P(None, AXES)),
        check_vma=False,
    )
```

time: 1210 us -> 109 us (0.09); the launches traced: 1200 us -> 108 us
  blocking collectives: 726 us -> 29.6 us
  other arithmetic: 261 us -> 0 us
  local copies, waits for them, and re-layouts: 163 us -> 11.8 us
  waiting for transfers between devices: 5.62 us -> 20.7 us
  Pallas kernels: 0 us -> 13.8 us
    psum x7 -> x0, blocking collectives: 726 us -> none  [the longest x4 411 us: precond_sum(): return lax.psum(local_inner(resid, prec), 'slab')]
    scatter-add x15 -> x0, other arithmetic: 247 us -> none  [the longest x4 178 us: element_apply(): jnp.zeros(field.shape, jnp.float32).at[:, conn.reshape(-1)].add(values)]
    gather x18 -> x0, local copies, waits for them, and re-layouts: 133 us -> none  [the longest x8 125 us: element_apply(): gathered = field[:, conn]]
    all_to_all x0 -> x1, blocking collectives: none -> 29.6 us  [body(): message = lax.all_to_all(message, GROUP, 0, 0, tiled=True)]
    pallas_call x0 -> x7, Pallas kernels: none -> 13.8 us  [call(): pl.pallas_call(kernel, out_shape=[jax.ShapeDtypeStruct(s, t) for s, t in...]
    reshape x10 -> x0, local copies, waits for them, and re-layouts: 13.4 us -> none  [the longest x4 10.5 us: element_apply(): values = result.reshape(4, 3, -1).transpose(1, 0, 2).reshape(3, -1)]
    ppermute x10 -> x8, starting transfers between devices: 30.6 us -> 23.4 us  [the longest x4 14.5 us: swap(): from_a = lax.ppermute(side_a, AXES, [(i, i ^ 1) for i in range(count)])]
  transfers between devices with their start and end apart: 10 -> 9, of which waited for: 3 -> 5; matrix products, arithmetic and copies ran while one was open for 3% -> 2% of each run, Pallas kernels for 0% -> 0%
where the time goes in v1:
time: 109 us; the launch traced here: 108 us
  starting transfers between devices  30.4 us (28%)
  blocking collectives  29.6 us (27%)
  waiting for transfers between devices  20.7 us (19%)
  Pallas kernels  13.8 us (13%)
  local copies, waits for them, and re-layouts  11.8 us (11%)
    all_to_all x1, blocking collectives, body(): message = lax.all_to_all(message, GROUP, 0, 0, tiled=True)  29.6 us
    ppermute x4, starting transfers between devices, swap(): from_a = lax.ppermute(side_a, AXES, [(i, i ^ 1) for i in range(count)])  14.5 us
    pallas_call x7, Pallas kernels, call(): pl.pallas_call(kernel, out_shape=[jax.ShapeDtypeStruct(s, t) for s, t in...  13.8 us
    ppermute x4, waiting for transfers between devices, swap(): lax.ppermute(side_b, AXES, [(i, (i + 1 ^ 1) - 1) for i in range(1, count...  10.8 us
    all_to_all x1, waiting for transfers between devices, body(): message = lax.all_to_all(message, 'z', 0, 0, tiled=True)  9.89 us
    ppermute x4, starting transfers between devices, swap(): lax.ppermute(side_b, AXES, [(i, (i + 1 ^ 1) - 1) for i in range(1, count...  8.83 us
    unnamed x12, local copies, waits for them, and re-layouts  7.36 us
    all_to_all x1, starting transfers between devices, body(): message = lax.all_to_all(message, 'z', 0, 0, tiled=True)  7.02 us
  transfers between devices with their start and end apart: 9, of which 5 were waited for; matrix products, arithmetic and copies ran while one was open for 2% of the time, Pallas kernels for 0%

profile of v1, /device:TPU:1, one launch (start us, length us, event | category | flops | bytes accessed | tf_op | source)
XLA Modules:
  0.0 108.1 jit_solution(13221825756254414686)
XLA Ops:
  0.6 0.0 copy-start
  0.6 1.1 %copy-done = bf16[12,12,2048]{2,1,0:T(8,128)(2,1)S(1)} copy-done((bf16[12,12,2048]{2,1,0:T(8,128)(2,1)S(1)}, bf16[12,12,2048]{2,1,0:T(8,128)(2,1)}, u32[]{:S(2)}) %copy-start) | copy-done | bytes 589848
  1.8 0.0 copy-start.3
  1.8 0.8 copy-done.3
  2.5 0.0 copy-start.4
  2.5 0.0 copy-start.2
  2.5 2.5 %shard_map.59 = (f32[24,256]{1,0:T(8,128)S(1)}, f32[24,256]{1,0:T(8,128)S(1)}, s32[16,2048]{1,0:T(8,128)S(1)}, s32[8,256]{1,0:T(8,128)S(1)}, s32[16,128]{1,0:T(8...) custom-call(f32[3,2048]{1,0:T(4,128)S(1)} %copy-done.3, bf16[12,12,2048]{2,1,0:T(8,128)(2,1)S(1)} %copy-done, ...), custom_call_target="tpu_custom_call" | custom-call | tf_op jit(solution)/shard_map/pallas_call | solution.py:401
  5.0 8.8 %collective-permute-start.4 = (f32[16,128]{1,0:T(8,128)S(1)}, f32[16,128]{1,0:T(8,128)S(1)}, u32[]{:S(2)}, u32[]{:S(2)}) collective-permute-start(f32[16,128]{1,0:T(8,128)S(1)} %get-tuple-element.151), channel_id=1, source_target_pairs={{0,1},{1,0},{2,3},{3,2},{4,5},{5,4},{6,7},{7,6},{8,9},{9,8},{10,11... | collective-permute-start | bytes 24584 | tf_op jit(solution)/shard_map/ppermute | solution.py:414
  13.8 1.9 %collective-permute-start.5 = (f32[16,128]{1,0:T(8,128)S(1)}, f32[16,128]{1,0:T(8,128)S(1)}, u32[]{:S(2)}, u32[]{:S(2)}) collective-permute-start(f32[16,128]{1,0:T(8,128)S(1)} %get-tuple-element.152), channel_id=1, source_target_pairs={{1,2},{2,1},{3,4},{4,3},{5,6},{6,5},{7,8},{8,7},{9,10},{10,9},{11,... | collective-permute-start | bytes 24584 | tf_op jit(solution)/shard_map/ppermute | solution.py:413
  15.7 0.0 collective-permute-done.4.near_a
  15.7 3.0 %collective-permute-done.5.near_b = f32[16,128]{1,0:T(8,128)S(1)} collective-permute-done((f32[16,128]{1,0:T(8,128)S(1)}, f32[16,128]{1,0:T(8,128)S(1)}, u32[]{:S(2)}, u32[]{:S(2)}) %collective-permute-start.5) | collective-permute-done | bytes 8224 | tf_op jit(solution)/shard_map/ppermute | solution.py:413
  18.8 0.0 copy-start.1
  18.8 1.1 %copy-done.1 = bf16[12,12,2048]{2,1,0:T(8,128)(2,1)S(1)} copy-done((bf16[12,12,2048]{2,1,0:T(8,128)(2,1)S(1)}, bf16[12,12,2048]{2,1,0:T(8,128)(2,1)}, u32[]{:S(2)}) %copy-start.1) | copy-done | bytes 589848
  19.9 2.5 %shard_map.60 = (f32[24,256]{1,0:T(8,128)S(1)}, f32[24,256]{1,0:T(8,128)S(1)}, f32[24,256]{1,0:T(8,128)S(1)}, f32[16,128]{1,0:T(8,128)S(1)}, f32[8,128]{1,0:T(8,128)S(1)}, /*index=5*/f32[8,128]{1,0:T(8,128)S(1)}) custom-call(f32[24,256]{1,0:T(8,128)S(1)} %get-tuple-element.146.load_ref, f32[24,256]{1,0:T(8,128)S(1)} %get-tuple-element.147.lumped_ref, ...), custom_call_target="tpu_custom_call" | custom-call | tf_op jit(solution)/shard_map/pallas_call | solution.py:401
  22.4 1.9 %collective-permute-start.6 = (f32[8,128]{1,0:T(8,128)S(1)}, f32[8,128]{1,0:T(8,128)S(1)}, u32[]{:S(2)}, u32[]{:S(2)}) collective-permute-start(f32[8,128]{1,0:T(8,128)S(1)} %get-tuple-element.155), channel_id=1, source_target_pairs={{0,1},{1,0},{2,3},{3,2},{4,5},{5,4},{6,7},{7,6},{8,9},{9,8},{10,11... | collective-permute-start | bytes 12296 | tf_op jit(solution)/shard_map/ppermute | solution.py:414
  24.3 1.9 %collective-permute-start.7 = (f32[8,128]{1,0:T(8,128)S(1)}, f32[8,128]{1,0:T(8,128)S(1)}, u32[]{:S(2)}, u32[]{:S(2)}) collective-permute-start(f32[8,128]{1,0:T(8,128)S(1)} %get-tuple-element.156), channel_id=1, source_target_pairs={{1,2},{2,1},{3,4},{4,3},{5,6},{6,5},{7,8},{8,7},{9,10},{10,9},{11,... | collective-permute-start | bytes 12296 | tf_op jit(solution)/shard_map/ppermute | solution.py:413
  26.3 0.0 collective-permute-done.6.near_a
  26.3 3.0 %collective-permute-done.7.near_b = f32[8,128]{1,0:T(8,128)S(1)} collective-permute-done((f32[8,128]{1,0:T(8,128)S(1)}, f32[8,128]{1,0:T(8,128)S(1)}, u32[]{:S(2)}, u32[]{:S(2)}) %collective-permute-start.7) | collective-permute-done | bytes 4128 | tf_op jit(solution)/shard_map/ppermute | solution.py:413
  29.3 2.5 %shard_map.61 = (f32[24,256]{1,0:T(8,128)S(1)}, f32[24,256]{1,0:T(8,128)S(1)}, f32[16,128]{1,0:T(8,128)S(1)}, f32[8,128]{1,0:T(8,128)S(1)}, f32[8,128]{1,0:T(8,128)S(1)}) custom-call(f32[24,256]{1,0:T(8,128)S(1)} %get-tuple-element.153.past_ref, f32[24,256]{1,0:T(8,128)S(1)} %get-tuple-element.154.diag_ref, f32[24,256]{1,0:T(8,128)S(1)} %get-tuple-element.147.lumped_ref, ...), custom_call_target="tpu_custom_call" | custom-call | tf_op jit(solution)/shard_map/pallas_call | solution.py:401
  31.8 1.9 %collective-permute-start.8 = (f32[8,128]{1,0:T(8,128)S(1)}, f32[8,128]{1,0:T(8,128)S(1)}, u32[]{:S(2)}, u32[]{:S(2)}) collective-permute-start(f32[8,128]{1,0:T(8,128)S(1)} %get-tuple-element.158), channel_id=1, source_target_pairs={{0,1},{1,0},{2,3},{3,2},{4,5},{5,4},{6,7},{7,6},{8,9},{9,8},{10,11... | collective-permute-start | bytes 12296 | tf_op jit(solution)/shard_map/ppermute | solution.py:414
  33.7 2.4 %collective-permute-start.9 = (f32[8,128]{1,0:T(8,128)S(1)}, f32[8,128]{1,0:T(8,128)S(1)}, u32[]{:S(2)}, u32[]{:S(2)}) collective-permute-start(f32[8,128]{1,0:T(8,128)S(1)} %get-tuple-element.159), channel_id=1, source_target_pairs={{1,2},{2,1},{3,4},{4,3},{5,6},{6,5},{7,8},{8,7},{9,10},{10,9},{11,... | collective-permute-start | bytes 12296 | tf_op jit(solution)/shard_map/ppermute | solution.py:413
  36.1 0.0 collective-permute-done.8.near_a
  36.1 2.5 %collective-permute-done.9.near_b = f32[8,128]{1,0:T(8,128)S(1)} collective-permute-done((f32[8,128]{1,0:T(8,128)S(1)}, f32[8,128]{1,0:T(8,128)S(1)}, u32[]{:S(2)}, u32[]{:S(2)}) %collective-permute-start.9) | collective-permute-done | bytes 4128 | tf_op jit(solution)/shard_map/ppermute | solution.py:413
  38.6 2.5 %shard_map.62 = (f32[24,256]{1,0:T(8,128)S(1)}, f32[24,256]{1,0:T(8,128)S(1)}, f32[16,128]{1,0:T(8,128)S(1)}, f32[8,128]{1,0:T(8,128)S(1)}, f32[8,128]{1,0:T(8,128)S(1)}) custom-call(f32[24,256]{1,0:T(8,128)S(1)} %get-tuple-element.157.past_ref, f32[24,256]{1,0:T(8,128)S(1)} %get-tuple-element.154.diag_ref, f32[24,256]{1,0:T(8,128)S(1)} %get-tuple-element.147.lumped_ref, ...), custom_call_target="tpu_custom_call" | custom-call | tf_op jit(solution)/shard_map/pallas_call | solution.py:401
  41.1 1.9 %collective-permute-start.10 = (f32[8,128]{1,0:T(8,128)S(1)}, f32[8,128]{1,0:T(8,128)S(1)}, u32[]{:S(2)}, u32[]{:S(2)}) collective-permute-start(f32[8,128]{1,0:T(8,128)S(1)} %get-tuple-element.161), channel_id=1, source_target_pairs={{0,1},{1,0},{2,3},{3,2},{4,5},{5,4},{6,7},{7,6},{8,9},{9,8},{10,11... | collective-permute-start | bytes 12296 | tf_op jit(solution)/shard_map/ppermute | solution.py:414
  43.0 2.5 %collective-permute-start.11 = (f32[8,128]{1,0:T(8,128)S(1)}, f32[8,128]{1,0:T(8,128)S(1)}, u32[]{:S(2)}, u32[]{:S(2)}) collective-permute-start(f32[8,128]{1,0:T(8,128)S(1)} %get-tuple-element.162), channel_id=1, source_target_pairs={{1,2},{2,1},{3,4},{4,3},{5,6},{6,5},{7,8},{8,7},{9,10},{10,9},{11,... | collective-permute-start | bytes 12296 | tf_op jit(solution)/shard_map/ppermute | solution.py:413
  45.6 0.0 collective-permute-done.10.near_a
  45.6 2.4 %collective-permute-done.11.near_b = f32[8,128]{1,0:T(8,128)S(1)} collective-permute-done((f32[8,128]{1,0:T(8,128)S(1)}, f32[8,128]{1,0:T(8,128)S(1)}, u32[]{:S(2)}, u32[]{:S(2)}) %collective-permute-start.11) | collective-permute-done | bytes 4128 | tf_op jit(solution)/shard_map/ppermute | solution.py:413
  48.0 2.5 %shard_map.63 = (f32[24,256]{1,0:T(8,128)S(1)}, f32[24,256]{1,0:T(8,128)S(1)}, f32[32,8,128]{2,1,0:T(8,128)S(1)}) custom-call(f32[24,256]{1,0:T(8,128)S(1)} %get-tuple-element.160.past_ref, f32[24,256]{1,0:T(8,128)S(1)} %get-tuple-element.154.diag_ref, f32[24,256]{1,0:T(8,128)S(1)} %get-tuple-element.147.lumped_ref, ...), custom_call_target="tpu_custom_call" | custom-call | tf_op jit(solution)/shard_map/pallas_call | solution.py:401
  50.5 29.6 %all_to_all.10.message_ref = f32[32,8,128]{2,1,0:T(8,128)S(1)} all-to-all(f32[32,8,128]{2,1,0:T(8,128)S(1)} %get-tuple-element.166), channel_id=1, replica_groups=mesh['x'=4,'z'=16,'y'=4,'c'=2] {'x','y','c'}, dimensions={0} | all-to-all | bytes 262144 | tf_op jit(solution)/shard_map/all_to_all | solution.py:502
  80.1 0.7 shard_map.64
  80.8 7.0 %all-to-all-start.1 = ((f32[16,8,128]{2,1,0:T(8,128)}), f32[16,8,128]{2,1,0:T(8,128)S(1)}, u32[]{:S(2)}, u32[]{:S(2)}) async-start(f32[16,8,128]{2,1,0:T(8,128)} %get-tuple-element.167), calls=%async_computation.1 | async-start | bytes 131072 | tf_op jit(solution)/shard_map/all_to_all | solution.py:504
  87.8 0.0 copy-done.4
  87.8 1.3 %copy.46 = f32[3,2048]{0,1:T(8,128)} copy(f32[3,2048]{1,0:T(4,128)S(1)} %copy-done.4) | data formatting | bytes 49152 | tf_op jit(solution)/shard_map/while | solution.py:515
  89.1 0.0 copy-done.2
  89.1 0.3 copy.45
  89.5 9.9 %all-to-all-done.1.message_ref = f32[16,8,128]{2,1,0:T(8,128)S(1)} async-done(((f32[16,8,128]{2,1,0:T(8,128)}), f32[16,8,128]{2,1,0:T(8,128)S(1)}, u32[]{:S(2)}, u32[]{:S(2)}) %all-to-all-start.1) | async-done | bytes 65568 | tf_op jit(solution)/shard_map/all_to_all | solution.py:504
  99.4 0.7 shard_map.65
  100.1 1.4 %copy.43 = f32[3,2048]{0,1:T(8,128)} copy(f32[3,2048]{1,0:T(4,128)S(1)} %get-tuple-element.249) | data formatting | bytes 49152 | tf_op jit(solution)/shard_map/while | solution.py:515
  101.5 1.3 %copy.44 = f32[3,2048]{0,1:T(8,128)} copy(f32[3,2048]{1,0:T(4,128)S(1)} %get-tuple-element.250) | data formatting | bytes 49152 | tf_op jit(solution)/shard_map/while | solution.py:515
  102.8 0.9 while.28
  103.8 2.2 %copy.47 = f32[3,2048]{1,0:T(4,128)} copy(f32[3,2048]{0,1:T(8,128)} %get-tuple-element.255) | data formatting | bytes 49152
  105.9 2.2 %copy.48 = f32[3,2048]{1,0:T(4,128)} copy(f32[3,2048]{0,1:T(8,128)} %get-tuple-element.256) | data formatting | bytes 49152
Async XLA Ops:
  0.6 1.1 %copy-start = (bf16[12,12,2048]{2,1,0:T(8,128)(2,1)S(1)}, bf16[12,12,2048]{2,1,0:T(8,128)(2,1)}, u32[]{:S(2)}) copy-start(bf16[12,12,2048]{2,1,0:T(8,128)(2,1)} %mats_ref.9) | copy-start | bytes 1769476
  1.8 0.8 copy-start.3
  2.5 85.3 %copy-start.4 = (f32[3,2048]{1,0:T(4,128)S(1)}, f32[3,2048]{1,0:T(4,128)}, u32[]{:S(2)}) copy-start(f32[3,2048]{1,0:T(4,128)} %load_ref.1) | copy-start | bytes 73732
  2.5 86.6 %copy-start.2 = (bf16[12,12,2048]{2,1,0:T(8,128)(2,1)S(1)}, bf16[12,12,2048]{2,1,0:T(8,128)(2,1)}, u32[]{:S(2)}) copy-start(bf16[12,12,2048]{2,1,0:T(8,128)(2,1)} %mats_ref.9) | copy-start | bytes 1769476
  5.0 10.7 %collective-permute-start.4 = (f32[16,128]{1,0:T(8,128)S(1)}, f32[16,128]{1,0:T(8,128)S(1)}, u32[]{:S(2)}, u32[]{:S(2)}) collective-permute-start(f32[16,128]{1,0:T(8,128)S(1)} %get-tuple-element.151), channel_id=1, source_target_pairs={{0,1},{1,0},{2,3},{3,2},{4,5},{5,4},{6,7},{7,6},{8,9},{9,8},{10,11... | collective-permute-start | bytes 24584 | tf_op jit(solution)/shard_map/ppermute | solution.py:414
  13.8 5.0 %collective-permute-start.5 = (f32[16,128]{1,0:T(8,128)S(1)}, f32[16,128]{1,0:T(8,128)S(1)}, u32[]{:S(2)}, u32[]{:S(2)}) collective-permute-start(f32[16,128]{1,0:T(8,128)S(1)} %get-tuple-element.152), channel_id=1, source_target_pairs={{1,2},{2,1},{3,4},{4,3},{5,6},{6,5},{7,8},{8,7},{9,10},{10,9},{11,... | collective-permute-start | bytes 24584 | tf_op jit(solution)/shard_map/ppermute | solution.py:413
  18.8 1.1 %copy-start.1 = (bf16[12,12,2048]{2,1,0:T(8,128)(2,1)S(1)}, bf16[12,12,2048]{2,1,0:T(8,128)(2,1)}, u32[]{:S(2)}) copy-start(bf16[12,12,2048]{2,1,0:T(8,128)(2,1)} %mats_ref.9) | copy-start | bytes 1769476
  22.4 3.9 %collective-permute-start.6 = (f32[8,128]{1,0:T(8,128)S(1)}, f32[8,128]{1,0:T(8,128)S(1)}, u32[]{:S(2)}, u32[]{:S(2)}) collective-permute-start(f32[8,128]{1,0:T(8,128)S(1)} %get-tuple-element.155), channel_id=1, source_target_pairs={{0,1},{1,0},{2,3},{3,2},{4,5},{5,4},{6,7},{7,6},{8,9},{9,8},{10,11... | collective-permute-start | bytes 12296 | tf_op jit(solution)/shard_map/ppermute | solution.py:414
  24.3 4.9 %collective-permute-start.7 = (f32[8,128]{1,0:T(8,128)S(1)}, f32[8,128]{1,0:T(8,128)S(1)}, u32[]{:S(2)}, u32[]{:S(2)}) collective-permute-start(f32[8,128]{1,0:T(8,128)S(1)} %get-tuple-element.156), channel_id=1, source_target_pairs={{1,2},{2,1},{3,4},{4,3},{5,6},{6,5},{7,8},{8,7},{9,10},{10,9},{11,... | collective-permute-start | bytes 12296 | tf_op jit(solution)/shard_map/ppermute | solution.py:413
  31.8 4.4 %collective-permute-start.8 = (f32[8,128]{1,0:T(8,128)S(1)}, f32[8,128]{1,0:T(8,128)S(1)}, u32[]{:S(2)}, u32[]{:S(2)}) collective-permute-start(f32[8,128]{1,0:T(8,128)S(1)} %get-tuple-element.158), channel_id=1, source_target_pairs={{0,1},{1,0},{2,3},{3,2},{4,5},{5,4},{6,7},{7,6},{8,9},{9,8},{10,11... | collective-permute-start | bytes 12296 | tf_op jit(solution)/shard_map/ppermute | solution.py:414
  33.7 4.9 %collective-permute-start.9 = (f32[8,128]{1,0:T(8,128)S(1)}, f32[8,128]{1,0:T(8,128)S(1)}, u32[]{:S(2)}, u32[]{:S(2)}) collective-permute-start(f32[8,128]{1,0:T(8,128)S(1)} %get-tuple-element.159), channel_id=1, source_target_pairs={{1,2},{2,1},{3,4},{4,3},{5,6},{6,5},{7,8},{8,7},{9,10},{10,9},{11,... | collective-permute-start | bytes 12296 | tf_op jit(solution)/shard_map/ppermute | solution.py:413
  41.1 4.5 %collective-permute-start.10 = (f32[8,128]{1,0:T(8,128)S(1)}, f32[8,128]{1,0:T(8,128)S(1)}, u32[]{:S(2)}, u32[]{:S(2)}) collective-permute-start(f32[8,128]{1,0:T(8,128)S(1)} %get-tuple-element.161), channel_id=1, source_target_pairs={{0,1},{1,0},{2,3},{3,2},{4,5},{5,4},{6,7},{7,6},{8,9},{9,8},{10,11... | collective-permute-start | bytes 12296 | tf_op jit(solution)/shard_map/ppermute | solution.py:414
  43.0 4.9 %collective-permute-start.11 = (f32[8,128]{1,0:T(8,128)S(1)}, f32[8,128]{1,0:T(8,128)S(1)}, u32[]{:S(2)}, u32[]{:S(2)}) collective-permute-start(f32[8,128]{1,0:T(8,128)S(1)} %get-tuple-element.162), channel_id=1, source_target_pairs={{1,2},{2,1},{3,4},{4,3},{5,6},{6,5},{7,8},{8,7},{9,10},{10,9},{11,... | collective-permute-start | bytes 12296 | tf_op jit(solution)/shard_map/ppermute | solution.py:413
  80.8 18.6 %all-to-all-start.1 = ((f32[16,8,128]{2,1,0:T(8,128)}), f32[16,8,128]{2,1,0:T(8,128)S(1)}, u32[]{:S(2)}, u32[]{:S(2)}) async-start(f32[16,8,128]{2,1,0:T(8,128)} %get-tuple-element.167), calls=%async_computation.1 | async-start | bytes 131072 | tf_op jit(solution)/shard_map/all_to_all | solution.py:504

commit v2 on v1

--- a/solution.py
+++ b/solution.py
@@ -36,11 +36,7 @@
 
 
 def field_rows(field, block):
-    high, half = block >> 1, block & 1
-    return [
-        jnp.broadcast_to(field[c * 8 + high : c * 8 + high + 1, half * 128 : half * 128 + 128], (8, 128))
-        for c in range(3)
-    ]
+    return [jnp.broadcast_to(field[c * 16 + block : c * 16 + block + 1, :], (8, 128)) for c in range(3)]
 
 
 def by_component(rows, comp):
@@ -57,27 +53,35 @@
 
 
 def assembled(field, inverse, near):
-    columns = []
-    for half in range(2):
-        where_from = inverse[:, half * 128 : half * 128 + 128]
-        lanes, code = where_from & 127, where_from >> 7
-        rows = []
-        for c in range(3):
-            tile = field[c * 8 : c * 8 + 8, half * 128 : half * 128 + 128]
+    tiles = []
+    for c in range(3):
+        for half in range(2):
+            place = inverse[half * 8 : half * 8 + 8, :]
+            lanes, code = place & 127, place >> 7
             parts = []
             for t in range(4):
                 row = 2 * c + (t & 1)
                 table = jnp.broadcast_to(near[t >> 1][row : row + 1, :], (8, 128))
                 parts.append(lane_take(table, lanes))
-            gain = pick(parts, code)
-            rows.append(tile + jnp.where(code < 0, 0.0, gain))
-        columns.append(jnp.concatenate(rows, axis=0))
-    return jnp.concatenate(columns, axis=1)
-
-
-def corner_lhs(values, conn, comps):
-    width = values.shape[1]
-    sub = iota((8, width), 0)
+            start = c * 16 + half * 8
+            tiles.append(field[start : start + 8, :] + jnp.where(code < 0, 0.0, pick(parts, code)))
+    return jnp.concatenate(tiles, axis=0)
+
+
+def bf16_rows(row, count):
+    return jnp.broadcast_to(row.astype(F32), (count, row.shape[1])).astype(BF16)
+
+
+def bf16_iota(shape):
+    return iota(shape, 0).astype(F32).astype(BF16)
+
+
+def high_mask(nodes):
+    return bf16_rows(nodes >> 7, 16) == bf16_iota((16, nodes.shape[1]))
+
+
+def corner_lhs(values, conn):
+    zero = jnp.zeros((), BF16)
     parts = []
     rest = values
     for _ in range(SPLITS - 1):
@@ -87,34 +91,16 @@
     parts.append(rest)
     out = []
     for n in range(4):
-        mask = jnp.broadcast_to(conn[n : n + 1, :] >> 8, (8, width)) == sub
-        tiles = []
-        for part in parts:
-            for c in range(comps):
-                row = n * comps + c
-                tiles.append(jnp.where(mask, jnp.broadcast_to(part[row : row + 1, :], (8, width)), 0.0))
-        if len(tiles) % 2:
-            tiles.append(jnp.zeros((8, width), F32))
-        out.append(jnp.concatenate(tiles, axis=0).astype(BF16))
+        mask = high_mask(conn[n : n + 1, :])
+        rows = [part[3 * n + c : 3 * n + c + 1, :] for part in parts for c in range(3)]
+        out.append(jnp.concatenate([jnp.where(mask, bf16_rows(row, 16), zero) for row in rows], axis=0))
     return out
 
 
-def one_hot(nodes):
-    width = nodes.shape[1]
-    low = jnp.broadcast_to((nodes & 255).astype(F32), (256, width)).astype(BF16)
-    rows = iota((256, width), 0).astype(F32).astype(BF16)
-    return jnp.where(rows == low, jnp.ones((), BF16), jnp.zeros((), BF16))
-
-
 def times_one_hot(lhs, nodes):
-    return lax.dot_general(lhs, one_hot(nodes), (((1,), (1,)), ((), ())), preferred_element_type=F32)
-
-
-def fold_splits(total):
-    out = total[0:24]
-    for s in range(1, SPLITS):
-        out = out + total[24 * s : 24 * s + 24]
-    return out
+    shape = (128, nodes.shape[1])
+    hot = jnp.where(bf16_rows(nodes & 127, 128) == bf16_iota(shape), jnp.ones((), BF16), jnp.zeros((), BF16))
+    return lax.dot_general(lhs, hot, (((1,), (1,)), ((), ())), preferred_element_type=F32)
 
 
 def scatter(values_of, conn_ref):
@@ -122,14 +108,32 @@
     for block in range(ELEMS // 256):
         start = block * 256
         conn = conn_ref[:, start : start + 256]
-        lhs = corner_lhs(values_of(start), conn, 3)
+        lhs = corner_lhs(values_of(start), conn)
         for n in range(4):
             piece = times_one_hot(lhs[n], conn[n : n + 1, :])
             total = piece if total is None else total + piece
-    return fold_splits(total)
-
-
-def first_kernel(load_ref, mats_ref, conn_ref, shared_ref, load_out, lumped_out, index_out, inverse_out, lists_out, a_out, b_out):
+    out = total[0:48]
+    for t in range(1, SPLITS):
+        out = out + total[48 * t : 48 * t + 48]
+    return out
+
+
+def first_kernel(
+    load_hbm, mats_hbm, conn_hbm, shared_hbm,
+    load_out, lumped_out, mats_ref, conn_ref, index_out, inverse_out, lists_out, a_out, b_out,
+    load_ref, shared_ref, sems,
+):
+    small = [
+        pltpu.make_async_copy(shared_hbm, shared_ref, sems.at[0]),
+        pltpu.make_async_copy(conn_hbm, conn_ref, sems.at[1]),
+        pltpu.make_async_copy(load_hbm, load_ref, sems.at[2]),
+    ]
+    large = [
+        pltpu.make_async_copy(mats_hbm.at[pl.ds(3 * i, 3)], mats_ref.at[pl.ds(3 * i, 3)], sems.at[3 + i]) for i in range(4)
+    ]
+    for copy in small + large:
+        copy.start()
+    small[0].wait()
     odd = lax.axis_index("c") == 1
     own = shared_ref[...]
     row0, row1 = own[0:1, :], own[1:2, :]
@@ -145,40 +149,46 @@
     lists_out[0:8, :] = lists[0]
     lists_out[8:16, :] = lists[1]
 
-    sub = iota((8, 256), 0)
-    lane = iota((8, 256), 1)
+    lane = iota((16, 256), 1)
+    zero = jnp.zeros((), BF16)
     found = None
     for t, side in enumerate((side_a, side_b)):
-        mask = jnp.broadcast_to(side >> 8, (8, 256)) == sub
-        place = jnp.where(mask, (lane & 127).astype(F32), 0.0)
-        code = jnp.where(mask, (2 * t + (lane >> 7) + 1).astype(F32), 0.0)
-        piece = times_one_hot(jnp.concatenate([place, code], axis=0).astype(BF16), side)
+        mask = high_mask(side)
+        place = jnp.where(mask, (lane & 127).astype(F32).astype(BF16), zero)
+        code = jnp.where(mask, (2 * t + (lane >> 7) + 1).astype(F32).astype(BF16), zero)
+        piece = times_one_hot(jnp.concatenate([place, code], axis=0), side)
         found = piece if found is None else found + piece
-    inverse_out[...] = (found[8:16].astype(jnp.int32) - 1) * 128 + found[0:8].astype(jnp.int32)
-
-    for c in range(3):
-        for h in range(8):
-            load_out[c * 8 + h : c * 8 + h + 1, :] = load_ref[c : c + 1, h * 256 : h * 256 + 256]
-
+    inverse_out[...] = (found[16:32].astype(jnp.int32) - 1) * 128 + found[0:16].astype(jnp.int32)
+
+    small[1].wait()
     for j in range(12):
         index_out[j : j + 1, :] = conn_ref[j // 3 : j // 3 + 1, :]
     index_out[12:16, :] = jnp.zeros((4, ELEMS), jnp.int32)
 
+    small[2].wait()
+    for c in range(3):
+        for h in range(16):
+            load_out[c * 16 + h : c * 16 + h + 1, :] = load_ref[c : c + 1, h * 128 : h * 128 + 128]
+    load_a, load_b = halos_of(load_out[...], lists)
+    a_out[0:8, :] = load_a
+    b_out[0:8, :] = load_b
+
+    for copy in large:
+        copy.wait()
     row12 = iota((12, 256), 0)
 
     def diagonal_of(start):
         out = jnp.zeros((12, 256), F32)
         for j in range(12):
-            out = jnp.where(row12 == j, mats_ref[j, :, start : start + 256].astype(F32), out)
+            column = mats_ref[j, :, start : start + 256].astype(F32)
+            out = jnp.where(row12 == j, column, out)
+            mats_ref[j, :, start : start + 256] = jnp.where(row12 == j, 0.0, column).astype(BF16)
         return out
 
     lumped = scatter(diagonal_of, conn_ref)
     lumped_out[...] = lumped
-    load_a, load_b = halos_of(load_out[...], lists)
     lump_a, lump_b = halos_of(lumped, lists)
-    a_out[0:8, :] = load_a
     a_out[8:16, :] = lump_a
-    b_out[0:8, :] = load_b
     b_out[8:16, :] = lump_b
 
 
@@ -188,7 +198,6 @@
         rows = field_rows(field, block)
         table_ref[block, 0:8, :] = by_component(rows, sub % 3)
         table_ref[block, 8:16, :] = by_component(rows, (sub + 2) % 3)
-    row12 = iota((12, 128), 0)
 
     def product(start):
         index = index_ref[:, start : start + 128]
@@ -200,7 +209,6 @@
         out = jnp.zeros((12, 128), F32)
         for j in range(12):
             column = mats_ref[j, :, start : start + 128].astype(F32)
-            column = jnp.where(row12 == j, 0.0, column)
             value = gathered[j // 8][j % 8 : j % 8 + 1, :]
             out = out + column * jnp.broadcast_to(value, (12, 128))
         return out
@@ -212,11 +220,9 @@
 
 
 def tile_sum(product):
-    out = None
-    for c in range(3):
-        for half in range(2):
-            tile = product[c * 8 : c * 8 + 8, half * 128 : half * 128 + 128]
-            out = tile if out is None else out + tile
+    out = product[0:8, :]
+    for i in range(1, 6):
+        out = out + product[8 * i : 8 * i + 8, :]
     return out
 
 
@@ -229,7 +235,7 @@
 
 
 def second_kernel(
-    load_ref, lumped_ref, inverse_ref, lists_ref, index_ref, conn_ref, mats_ref, near_a, near_b,
+    load_ref, lumped_ref, inverse_ref, lists_ref, index_ref, conn_ref, mats_ref, near_b, near_a,
     diag_out, basis_out, image_out, sums_out, a_out, b_out, table_ref,
 ):
     inverse = inverse_ref[...]
@@ -244,7 +250,7 @@
 
 
 def middle_kernel(
-    past_ref, diag_ref, lumped_ref, inverse_ref, lists_ref, index_ref, conn_ref, mats_ref, near_a, near_b,
+    past_ref, diag_ref, lumped_ref, inverse_ref, lists_ref, index_ref, conn_ref, mats_ref, near_b, near_a,
     basis_out, image_out, sums_out, a_out, b_out, table_ref,
 ):
     basis = assembled(past_ref[...], inverse_ref[...], [near_a[...], near_b[...]]) / diag_ref[...]
@@ -263,7 +269,7 @@
 
 
 def fourth_kernel(
-    past_ref, diag_ref, lumped_ref, inverse_ref, lists_ref, index_ref, conn_ref, mats_ref, near_a, near_b, sums0, sums1, sums2,
+    past_ref, diag_ref, lumped_ref, inverse_ref, lists_ref, index_ref, conn_ref, mats_ref, near_b, near_a, sums0, sums1, sums2,
     basis_out, image_out, message_out, table_ref, sums_ref,
 ):
     basis = assembled(past_ref[...], inverse_ref[...], [near_a[...], near_b[...]]) / diag_ref[...]
@@ -377,35 +383,41 @@
     image = assembled(image_ref[...], inverse_ref[...], near)
     for c_ in range(3):
         for half in range(2):
-            at = (slice(c_ * 8, c_ * 8 + 8), slice(half * 128, half * 128 + 128))
-            basis = [r[at] for r in (b0, b1, b2, b3)]
+            rows = slice(c_ * 16 + half * 8, c_ * 16 + half * 8 + 8)
+            basis = [r[rows, :] for r in (b0, b1, b2, b3)]
             accel = basis[3] * accel_coef[3]
-            resid = image[at] * resid_coef[4]
             part = basis[3] * resid_coef[3]
             for k in (2, 1, 0):
                 accel = accel + basis[k] * accel_coef[k]
                 part = part + basis[k] * resid_coef[k]
-            resid = resid + diag[at] * part
+            resid = image[rows, :] * resid_coef[4] + diag[rows, :] * part
             for h in range(8):
-                lanes = slice(h * 256 + half * 128, h * 256 + half * 128 + 128)
-                accel_out[c_ : c_ + 1, lanes] = accel[h : h + 1, :]
-                resid_out[c_ : c_ + 1, lanes] = resid[h : h + 1, :]
+                start = (half * 8 + h) * 128
+                accel_out[c_ : c_ + 1, start : start + 128] = accel[h : h + 1, :]
+                resid_out[c_ : c_ + 1, start : start + 128] = resid[h : h + 1, :]
     flag_out[0, 0] = jnp.min(jnp.where(good, 1, 0))
 
 
-def call(kernel, outs, *args, scratch=(), smem_out=None):
-    vmem = pl.BlockSpec(memory_space=pltpu.VMEM)
-    out_specs = [vmem] * len(outs)
+def call(kernel, outs, *args, scratch=(), smem_out=None, space=pltpu.VMEM):
+    out_specs = [pl.BlockSpec(memory_space=pltpu.VMEM)] * len(outs)
     if smem_out is not None:
         out_specs[smem_out] = pl.BlockSpec(memory_space=pltpu.SMEM)
     return pl.pallas_call(
         kernel,
         out_shape=[jax.ShapeDtypeStruct(s, t) for s, t in outs],
-        in_specs=[vmem] * len(args),
+        in_specs=[pl.BlockSpec(memory_space=space)] * len(args),
         out_specs=out_specs,
         scratch_shapes=list(scratch),
         compiler_params=pltpu.CompilerParams(vmem_limit_bytes=VMEM_LIMIT),
     )(*args)
+
+
+def same(*args):
+    def kernel(*refs):
+        for src, dst in zip(refs[: len(args)], refs[len(args) :]):
+            dst[...] = src[...]
+
+    return call(kernel, [(a.shape, a.dtype) for a in args], *args)
 
 
 def swap(side_a, side_b):
@@ -464,20 +476,24 @@
 
 
 def body(load, element_mats, connect, shared):
-    field = ((24, 256), F32)
+    field = ((48, 128), F32)
     halo = ((8, 128), F32)
     sums = ((16, 128), F32)
+    index = ((16, ELEMS), jnp.int32)
+    inverse = ((16, 128), jnp.int32)
     table = pltpu.VMEM((16, 16, 128), F32)
-    load_f, lumped, index, inverse, lists, a, b = call(
+    load_f, lumped, mats, conn, index, inverse, lists, a, b = call(
         first_kernel,
-        [field, field, ((16, ELEMS), jnp.int32), ((8, 256), jnp.int32), ((16, 128), jnp.int32), sums, sums],
+        [field, field, ((12, 12, ELEMS), BF16), ((4, ELEMS), jnp.int32), index, inverse, inverse, sums, sums],
         load, element_mats, connect, shared,
+        scratch=[pltpu.VMEM((3, NODES), F32), pltpu.VMEM((2, SHARED), jnp.int32), pltpu.SemaphoreType.DMA((7,))],
+        space=pltpu.HBM,
     )
     a, b = swap(a, b)
     diag, b0, image, sums0, a, b = call(
         second_kernel,
         [field, field, field, sums, halo, halo],
-        load_f, lumped, inverse, lists, index, connect, element_mats, a, b,
+        load_f, lumped, inverse, lists, index, conn, mats, b, a,
         scratch=[table],
     )
     bases, totals = [b0], [sums0]
@@ -486,7 +502,7 @@
         basis, image, total, a, b = call(
             middle_kernel,
             [field, field, sums, halo, halo],
-            image, diag, lumped, inverse, lists, index, connect, element_mats, a, b,
+            image, diag, lumped, inverse, lists, index, conn, mats, b, a,
             scratch=[table],
         )
         bases.append(basis)
@@ -495,7 +511,7 @@
     basis, image, message = call(
         fourth_kernel,
         [field, field, ((32, 8, 128), F32)],
-        image, diag, lumped, inverse, lists, index, connect, element_mats, a, b, *totals,
+        image, diag, lumped, inverse, lists, index, conn, mats, b, a, *totals,
         scratch=[table, pltpu.VMEM((16, 128), F32)],
     )
     bases.append(basis)
@@ -510,7 +526,8 @@
     )
 
     def again(carry):
-        return (jnp.int32(1),) + plain(load, element_mats, connect, shared)
+        args = same(load, element_mats, connect, shared)
+        return (jnp.int32(1),) + tuple(same(*plain(*args)))
 
     _, accel, residual = lax.while_loop(lambda carry: carry[0] == 0, again, (flag.reshape(()), accel, residual))
     return accel, residual

time: 109 us -> 85 us (0.78)
  blocking collectives: 29.6 us -> 47 us
  waiting for transfers between devices: 20.7 us -> 4.18 us
  local copies, waits for them, and re-layouts: 11.8 us -> 0 us
  starting transfers between devices: 30.4 us -> 22.7 us
  Pallas kernels: 13.8 us -> 8.92 us
    all_to_all x0 -> x1, blocking collectives: none -> 16.7 us  [body(): message = lax.all_to_all(message, 'z', 0, 0, tiled=True)]
    all_to_all x1 -> x0, waiting for transfers between devices: 9.89 us -> none  [body(): message = lax.all_to_all(message, 'z', 0, 0, tiled=True)]
    ppermute x4, waiting for transfers between devices: 10.8 us -> 2.14 us  [swap(): lax.ppermute(side_b, AXES, [(i, (i + 1 ^ 1) - 1) for i in range(1, count...]
    unnamed x12 -> x0, local copies, waits for them, and re-layouts: 7.36 us -> none
    all_to_all x1 -> x0, starting transfers between devices: 7.02 us -> none  [body(): message = lax.all_to_all(message, 'z', 0, 0, tiled=True)]
    pallas_call x7, Pallas kernels: 13.8 us -> 8.92 us  [call(): pl.pallas_call(kernel, out_shape=[jax.ShapeDtypeStruct(s, t) for s, t in...]
    while x4 -> x0, local copies, waits for them, and re-layouts: 4.41 us -> none  [body(): lax.while_loop(lambda carry: carry[0] == 0, again, (flag.reshape(()), acc...]
    ppermute x4, starting transfers between devices: 14.5 us -> 10.6 us  [swap(): from_a = lax.ppermute(side_a, AXES, [(i, i ^ 1) for i in range(count)])]
  transfers between devices with their start and end apart: 9 -> 8, of which waited for: 5 -> 6; matrix products, arithmetic and copies ran while one was open for 2% -> 0% of each run, Pallas kernels for 0% -> 0%
where the time goes in v2:
time: 85 us; the launch traced here: 84.6 us
  blocking collectives  47 us (55%)
  starting transfers between devices  22.7 us (27%)
  Pallas kernels  8.92 us (10%)
  waiting for transfers between devices  4.18 us (5%)
  between operations  0.94 us (1%)
    all_to_all x1, blocking collectives, body(): message = lax.all_to_all(message, GROUP, 0, 0, tiled=True)  30.4 us
    all_to_all x1, blocking collectives, body(): message = lax.all_to_all(message, 'z', 0, 0, tiled=True)  16.7 us
    ppermute x4, starting transfers between devices, swap(): lax.ppermute(side_b, AXES, [(i, (i + 1 ^ 1) - 1) for i in range(1, count...  12.1 us
    ppermute x4, starting transfers between devices, swap(): from_a = lax.ppermute(side_a, AXES, [(i, i ^ 1) for i in range(count)])  10.6 us
    pallas_call x7, Pallas kernels, call(): pl.pallas_call(kernel, out_shape=[jax.ShapeDtypeStruct(s, t) for s, t in...  8.92 us
    ppermute x4, waiting for transfers between devices, swap(): lax.ppermute(side_b, AXES, [(i, (i + 1 ^ 1) - 1) for i in range(1, count...  2.14 us
    ppermute x4, waiting for transfers between devices, swap(): from_a = lax.ppermute(side_a, AXES, [(i, i ^ 1) for i in range(count)])  2.05 us
  transfers between devices with their start and end apart: 8, of which 6 were waited for; matrix products, arithmetic and copies ran while one was open for 0% of the time, Pallas kernels for 0%

profile of v2, /device:TPU:1, one launch (start us, length us, event | category | flops | bytes accessed | tf_op | source)
XLA Modules:
  0.0 84.6 jit_solution(5647439723110727027)
XLA Ops:
  0.6 2.3 %shard_map.59 = (f32[48,128]{1,0:T(8,128)S(1)}, f32[48,128]{1,0:T(8,128)S(1)}, bf16[12,12,2048]{2,1,0:T(8,128)(2,1)S(1)}, s32[4,2048]{1,0:T(4,128)S(1)}, s32[16,...) custom-call(f32[3,2048]{1,0:T(4,128)} %load_hbm.1, ...), custom_call_target="tpu_custom_call" | custom-call | tf_op jit(solution)/shard_map/pallas_call | solution.py:405
  3.0 4.6 %collective-permute-start.4 = (f32[16,128]{1,0:T(8,128)S(1)}, f32[16,128]{1,0:T(8,128)S(1)}, u32[]{:S(2)}, u32[]{:S(2)}) collective-permute-start(f32[16,128]{1,0:T(8,128)S(1)} %get-tuple-element.161), channel_id=1, source_target_pairs={{1,2},{2,1},{3,4},{4,3},{5,6},{6,5},{7,8},{8,7},{9,10},{10,9},{11,... | collective-permute-start | bytes 24584 | tf_op jit(solution)/shard_map/ppermute | solution.py:425
  7.6 4.8 %collective-permute-start.5 = (f32[16,128]{1,0:T(8,128)S(1)}, f32[16,128]{1,0:T(8,128)S(1)}, u32[]{:S(2)}, u32[]{:S(2)}) collective-permute-start(f32[16,128]{1,0:T(8,128)S(1)} %get-tuple-element.162), channel_id=1, source_target_pairs={{0,1},{1,0},{2,3},{3,2},{4,5},{5,4},{6,7},{7,6},{8,9},{9,8},{10,11... | collective-permute-start | bytes 24584 | tf_op jit(solution)/shard_map/ppermute | solution.py:426
  12.4 0.0 collective-permute-done.4.near_b
  12.4 0.8 collective-permute-done.5.near_a
  13.2 1.5 %shard_map.60 = (f32[48,128]{1,0:T(8,128)S(1)}, f32[48,128]{1,0:T(8,128)S(1)}, f32[48,128]{1,0:T(8,128)S(1)}, f32[16,128]{1,0:T(8,128)S(1)}, f32[8,128]{1,0:T(8,128)S(1)}, /*index=5*/f32[8,128]{1,0:T(8,128)S(1)}) custom-call(f32[48,128]{1,0:T(8,128)S(1)} %get-tuple-element.154.load_ref, f32[48,128]{1,0:T(8,128)S(1)} %get-tuple-element.155.lumped_ref, ...), custom_call_target="tpu_custom_call" | custom-call | tf_op jit(solution)/shard_map/pallas_call | solution.py:405
  14.7 1.9 %collective-permute-start.6 = (f32[8,128]{1,0:T(8,128)S(1)}, f32[8,128]{1,0:T(8,128)S(1)}, u32[]{:S(2)}, u32[]{:S(2)}) collective-permute-start(f32[8,128]{1,0:T(8,128)S(1)} %get-tuple-element.165), channel_id=1, source_target_pairs={{1,2},{2,1},{3,4},{4,3},{5,6},{6,5},{7,8},{8,7},{9,10},{10,9},{11,... | collective-permute-start | bytes 12296 | tf_op jit(solution)/shard_map/ppermute | solution.py:425
  16.6 1.9 %collective-permute-start.7 = (f32[8,128]{1,0:T(8,128)S(1)}, f32[8,128]{1,0:T(8,128)S(1)}, u32[]{:S(2)}, u32[]{:S(2)}) collective-permute-start(f32[8,128]{1,0:T(8,128)S(1)} %get-tuple-element.166), channel_id=1, source_target_pairs={{0,1},{1,0},{2,3},{3,2},{4,5},{5,4},{6,7},{7,6},{8,9},{9,8},{10,11... | collective-permute-start | bytes 12296 | tf_op jit(solution)/shard_map/ppermute | solution.py:426
  18.6 1.1 %collective-permute-done.6.near_b = f32[8,128]{1,0:T(8,128)S(1)} collective-permute-done((f32[8,128]{1,0:T(8,128)S(1)}, f32[8,128]{1,0:T(8,128)S(1)}, u32[]{:S(2)}, u32[]{:S(2)}) %collective-permute-start.6) | collective-permute-done | bytes 4128 | tf_op jit(solution)/shard_map/ppermute | solution.py:425
  19.6 0.1 collective-permute-done.7.near_a
  19.7 1.4 %shard_map.61 = (f32[48,128]{1,0:T(8,128)S(1)}, f32[48,128]{1,0:T(8,128)S(1)}, f32[16,128]{1,0:T(8,128)S(1)}, f32[8,128]{1,0:T(8,128)S(1)}, f32[8,128]{1,0:T(8,128)S(1)}) custom-call(f32[48,128]{1,0:T(8,128)S(1)} %get-tuple-element.163.past_ref, f32[48,128]{1,0:T(8,128)S(1)} %get-tuple-element.164.diag_ref, f32[48,128]{1,0:T(8,128)S(1)} %get-tuple-element.155.lumped_ref, ...), custom_call_target="tpu_custom_call" | custom-call | tf_op jit(solution)/shard_map/pallas_call | solution.py:405
  21.1 3.6 %collective-permute-start.8 = (f32[8,128]{1,0:T(8,128)S(1)}, f32[8,128]{1,0:T(8,128)S(1)}, u32[]{:S(2)}, u32[]{:S(2)}) collective-permute-start(f32[8,128]{1,0:T(8,128)S(1)} %get-tuple-element.168), channel_id=1, source_target_pairs={{1,2},{2,1},{3,4},{4,3},{5,6},{6,5},{7,8},{8,7},{9,10},{10,9},{11,... | collective-permute-start | bytes 12296 | tf_op jit(solution)/shard_map/ppermute | solution.py:425
  24.7 1.9 %collective-permute-start.9 = (f32[8,128]{1,0:T(8,128)S(1)}, f32[8,128]{1,0:T(8,128)S(1)}, u32[]{:S(2)}, u32[]{:S(2)}) collective-permute-start(f32[8,128]{1,0:T(8,128)S(1)} %get-tuple-element.169), channel_id=1, source_target_pairs={{0,1},{1,0},{2,3},{3,2},{4,5},{5,4},{6,7},{7,6},{8,9},{9,8},{10,11... | collective-permute-start | bytes 12296 | tf_op jit(solution)/shard_map/ppermute | solution.py:426
  26.7 0.0 collective-permute-done.8.near_b
  26.7 1.1 %collective-permute-done.9.near_a = f32[8,128]{1,0:T(8,128)S(1)} collective-permute-done((f32[8,128]{1,0:T(8,128)S(1)}, f32[8,128]{1,0:T(8,128)S(1)}, u32[]{:S(2)}, u32[]{:S(2)}) %collective-permute-start.9) | collective-permute-done | bytes 4128 | tf_op jit(solution)/shard_map/ppermute | solution.py:426
  27.8 1.4 %shard_map.62 = (f32[48,128]{1,0:T(8,128)S(1)}, f32[48,128]{1,0:T(8,128)S(1)}, f32[16,128]{1,0:T(8,128)S(1)}, f32[8,128]{1,0:T(8,128)S(1)}, f32[8,128]{1,0:T(8,128)S(1)}) custom-call(f32[48,128]{1,0:T(8,128)S(1)} %get-tuple-element.167.past_ref, f32[48,128]{1,0:T(8,128)S(1)} %get-tuple-element.164.diag_ref, f32[48,128]{1,0:T(8,128)S(1)} %get-tuple-element.155.lumped_ref, ...), custom_call_target="tpu_custom_call" | custom-call | tf_op jit(solution)/shard_map/pallas_call | solution.py:405
  29.2 1.9 %collective-permute-start.10 = (f32[8,128]{1,0:T(8,128)S(1)}, f32[8,128]{1,0:T(8,128)S(1)}, u32[]{:S(2)}, u32[]{:S(2)}) collective-permute-start(f32[8,128]{1,0:T(8,128)S(1)} %get-tuple-element.171), channel_id=1, source_target_pairs={{1,2},{2,1},{3,4},{4,3},{5,6},{6,5},{7,8},{8,7},{9,10},{10,9},{11,... | collective-permute-start | bytes 12296 | tf_op jit(solution)/shard_map/ppermute | solution.py:425
  31.1 1.9 %collective-permute-start.11 = (f32[8,128]{1,0:T(8,128)S(1)}, f32[8,128]{1,0:T(8,128)S(1)}, u32[]{:S(2)}, u32[]{:S(2)}) collective-permute-start(f32[8,128]{1,0:T(8,128)S(1)} %get-tuple-element.172), channel_id=1, source_target_pairs={{0,1},{1,0},{2,3},{3,2},{4,5},{5,4},{6,7},{7,6},{8,9},{9,8},{10,11... | collective-permute-start | bytes 12296 | tf_op jit(solution)/shard_map/ppermute | solution.py:426
  33.1 1.1 %collective-permute-done.10.near_b = f32[8,128]{1,0:T(8,128)S(1)} collective-permute-done((f32[8,128]{1,0:T(8,128)S(1)}, f32[8,128]{1,0:T(8,128)S(1)}, u32[]{:S(2)}, u32[]{:S(2)}) %collective-permute-start.10) | collective-permute-done | bytes 4128 | tf_op jit(solution)/shard_map/ppermute | solution.py:425
  34.1 0.1 collective-permute-done.11.near_a
  34.2 1.5 %shard_map.63 = (f32[48,128]{1,0:T(8,128)S(1)}, f32[48,128]{1,0:T(8,128)S(1)}, f32[32,8,128]{2,1,0:T(8,128)S(1)}) custom-call(f32[48,128]{1,0:T(8,128)S(1)} %get-tuple-element.170.past_ref, f32[48,128]{1,0:T(8,128)S(1)} %get-tuple-element.164.diag_ref, f32[48,128]{1,0:T(8,128)S(1)} %get-tuple-element.155.lumped_ref, ...), custom_call_target="tpu_custom_call" | custom-call | tf_op jit(solution)/shard_map/pallas_call | solution.py:405
  35.7 30.4 %all_to_all.10.message_ref = f32[32,8,128]{2,1,0:T(8,128)S(1)} all-to-all(f32[32,8,128]{2,1,0:T(8,128)S(1)} %get-tuple-element.176), channel_id=1, replica_groups=mesh['x'=4,'z'=16,'y'=4,'c'=2] {'x','y','c'}, dimensions={0} | all-to-all | bytes 262144 | tf_op jit(solution)/shard_map/all_to_all | solution.py:518
  66.1 16.7 %all_to_all.11.message_ref = f32[16,8,128]{2,1,0:T(8,128)S(1)} all-to-all(f32[16,8,128]{2,1,0:T(8,128)S(1)} %get-tuple-element.177), channel_id=1, replica_groups=mesh['x'=4,'z'=16,'y'=4,'c'=2] {'z'}, dimensions={0} | all-to-all | bytes 131072 | tf_op jit(solution)/shard_map/all_to_all | solution.py:520
  82.7 0.8 %shard_map.65 = (f32[3,2048]{1,0:T(4,128)}, f32[3,2048]{1,0:T(4,128)}, s32[1,1]{1,0:T(1,128)}) custom-call(f32[16,8,128]{2,1,0:T(8,128)S(1)} %all_to_all.11.message_ref, f32[16,128]{1,0:T(8,128)S(1)} %get-tuple-element.178.direct_ref, f32[48,128]{1,0:T(8,128)S(1)} %get-tuple-element.179.image_ref, f32[48,128]{1,0:T(8,128)S(1)} %get-tuple-element.164.diag_ref, ...), custom_call_target="tpu_custom_call" | custom-call | tf_op jit(solution)/shard_map/pallas_call | solution.py:405
  83.6 0.8 while.28
  (1 shorter events, 0.0 us)
Async XLA Ops:
  3.0 9.5 %collective-permute-start.4 = (f32[16,128]{1,0:T(8,128)S(1)}, f32[16,128]{1,0:T(8,128)S(1)}, u32[]{:S(2)}, u32[]{:S(2)}) collective-permute-start(f32[16,128]{1,0:T(8,128)S(1)} %get-tuple-element.161), channel_id=1, source_target_pairs={{1,2},{2,1},{3,4},{4,3},{5,6},{6,5},{7,8},{8,7},{9,10},{10,9},{11,... | collective-permute-start | bytes 24584 | tf_op jit(solution)/shard_map/ppermute | solution.py:425
  7.6 5.7 %collective-permute-start.5 = (f32[16,128]{1,0:T(8,128)S(1)}, f32[16,128]{1,0:T(8,128)S(1)}, u32[]{:S(2)}, u32[]{:S(2)}) collective-permute-start(f32[16,128]{1,0:T(8,128)S(1)} %get-tuple-element.162), channel_id=1, source_target_pairs={{0,1},{1,0},{2,3},{3,2},{4,5},{5,4},{6,7},{7,6},{8,9},{9,8},{10,11... | collective-permute-start | bytes 24584 | tf_op jit(solution)/shard_map/ppermute | solution.py:426
  14.7 4.9 %collective-permute-start.6 = (f32[8,128]{1,0:T(8,128)S(1)}, f32[8,128]{1,0:T(8,128)S(1)}, u32[]{:S(2)}, u32[]{:S(2)}) collective-permute-start(f32[8,128]{1,0:T(8,128)S(1)} %get-tuple-element.165), channel_id=1, source_target_pairs={{1,2},{2,1},{3,4},{4,3},{5,6},{6,5},{7,8},{8,7},{9,10},{10,9},{11,... | collective-permute-start | bytes 12296 | tf_op jit(solution)/shard_map/ppermute | solution.py:425
  16.6 3.1 %collective-permute-start.7 = (f32[8,128]{1,0:T(8,128)S(1)}, f32[8,128]{1,0:T(8,128)S(1)}, u32[]{:S(2)}, u32[]{:S(2)}) collective-permute-start(f32[8,128]{1,0:T(8,128)S(1)} %get-tuple-element.166), channel_id=1, source_target_pairs={{0,1},{1,0},{2,3},{3,2},{4,5},{5,4},{6,7},{7,6},{8,9},{9,8},{10,11... | collective-permute-start | bytes 12296 | tf_op jit(solution)/shard_map/ppermute | solution.py:426
  21.1 5.6 %collective-permute-start.8 = (f32[8,128]{1,0:T(8,128)S(1)}, f32[8,128]{1,0:T(8,128)S(1)}, u32[]{:S(2)}, u32[]{:S(2)}) collective-permute-start(f32[8,128]{1,0:T(8,128)S(1)} %get-tuple-element.168), channel_id=1, source_target_pairs={{1,2},{2,1},{3,4},{4,3},{5,6},{6,5},{7,8},{8,7},{9,10},{10,9},{11,... | collective-permute-start | bytes 12296 | tf_op jit(solution)/shard_map/ppermute | solution.py:425
  24.7 3.1 %collective-permute-start.9 = (f32[8,128]{1,0:T(8,128)S(1)}, f32[8,128]{1,0:T(8,128)S(1)}, u32[]{:S(2)}, u32[]{:S(2)}) collective-permute-start(f32[8,128]{1,0:T(8,128)S(1)} %get-tuple-element.169), channel_id=1, source_target_pairs={{0,1},{1,0},{2,3},{3,2},{4,5},{5,4},{6,7},{7,6},{8,9},{9,8},{10,11... | collective-permute-start | bytes 12296 | tf_op jit(solution)/shard_map/ppermute | solution.py:426
  29.2 4.9 %collective-permute-start.10 = (f32[8,128]{1,0:T(8,128)S(1)}, f32[8,128]{1,0:T(8,128)S(1)}, u32[]{:S(2)}, u32[]{:S(2)}) collective-permute-start(f32[8,128]{1,0:T(8,128)S(1)} %get-tuple-element.171), channel_id=1, source_target_pairs={{1,2},{2,1},{3,4},{4,3},{5,6},{6,5},{7,8},{8,7},{9,10},{10,9},{11,... | collective-permute-start | bytes 12296 | tf_op jit(solution)/shard_map/ppermute | solution.py:425
  31.1 3.1 %collective-permute-start.11 = (f32[8,128]{1,0:T(8,128)S(1)}, f32[8,128]{1,0:T(8,128)S(1)}, u32[]{:S(2)}, u32[]{:S(2)}) collective-permute-start(f32[8,128]{1,0:T(8,128)S(1)} %get-tuple-element.172), channel_id=1, source_target_pairs={{0,1},{1,0},{2,3},{3,2},{4,5},{5,4},{6,7},{7,6},{8,9},{9,8},{10,11... | collective-permute-start | bytes 12296 | tf_op jit(solution)/shard_map/ppermute | solution.py:426

commit v3 on v2

--- a/solution.py
+++ b/solution.py
@@ -12,7 +12,7 @@
 ELEMS = 2048
 SHARED = 256
 SPLITS = 3
-PIVOT_FLOOR = 1e-3
+PIVOT_FLOOR = 0.02
 F32 = jnp.float32
 BF16 = jnp.bfloat16
 VMEM_LIMIT = 32 * 1024 * 1024
@@ -131,9 +131,10 @@
     large = [
         pltpu.make_async_copy(mats_hbm.at[pl.ds(3 * i, 3)], mats_ref.at[pl.ds(3 * i, 3)], sems.at[3 + i]) for i in range(4)
     ]
-    for copy in small + large:
+    for copy in small[:2] + large + small[2:]:
         copy.start()
-    small[0].wait()
+    for copy in small:
+        copy.wait()
     odd = lax.axis_index("c") == 1
     own = shared_ref[...]
     row0, row1 = own[0:1, :], own[1:2, :]
@@ -160,12 +161,10 @@
         found = piece if found is None else found + piece
     inverse_out[...] = (found[16:32].astype(jnp.int32) - 1) * 128 + found[0:16].astype(jnp.int32)
 
-    small[1].wait()
     for j in range(12):
         index_out[j : j + 1, :] = conn_ref[j // 3 : j // 3 + 1, :]
     index_out[12:16, :] = jnp.zeros((4, ELEMS), jnp.int32)
 
-    small[2].wait()
     for c in range(3):
         for h in range(16):
             load_out[c * 16 + h : c * 16 + h + 1, :] = load_ref[c : c + 1, h * 128 : h * 128 + 128]
@@ -173,19 +172,23 @@
     a_out[0:8, :] = load_a
     b_out[0:8, :] = load_b
 
+    row12 = iota((12, 256), 0)
+    zero16 = jnp.zeros((), BF16)
+    lumped = None
     for copy in large:
         copy.wait()
-    row12 = iota((12, 256), 0)
-
-    def diagonal_of(start):
-        out = jnp.zeros((12, 256), F32)
-        for j in range(12):
-            column = mats_ref[j, :, start : start + 256].astype(F32)
-            out = jnp.where(row12 == j, column, out)
-            mats_ref[j, :, start : start + 256] = jnp.where(row12 == j, 0.0, column).astype(BF16)
-        return out
-
-    lumped = scatter(diagonal_of, conn_ref)
+    for block in range(ELEMS // 256):
+        for n in range(4):
+            span = slice(block * 256, block * 256 + 256)
+            nodes = conn_ref[n : n + 1, span]
+            mask = high_mask(nodes)
+            rows = []
+            for j in range(3 * n, 3 * n + 3):
+                column = mats_ref[j, :, span].astype(F32)
+                rows.append(jnp.where(mask, bf16_rows(column[j : j + 1, :], 16), zero16))
+                mats_ref[j, :, span] = jnp.where(row12 == j, 0.0, column).astype(BF16)
+            piece = times_one_hot(jnp.concatenate(rows, axis=0), nodes)
+            lumped = piece if lumped is None else lumped + piece
     lumped_out[...] = lumped
     lump_a, lump_b = halos_of(lumped, lists)
     a_out[8:16, :] = lump_a

time: 85 us -> 85.1 us (level)
  no operation moved by 1% of the time
where the time goes in v3:
time: 85.1 us; the launch traced here: 84.7 us
  blocking collectives  47 us (55%)
  starting transfers between devices  22.7 us (27%)
  Pallas kernels  9.03 us (11%)
  waiting for transfers between devices  4.18 us (5%)
  between operations  0.94 us (1%)
    all_to_all x1, blocking collectives, body(): message = lax.all_to_all(message, GROUP, 0, 0, tiled=True)  30.4 us
    all_to_all x1, blocking collectives, body(): message = lax.all_to_all(message, 'z', 0, 0, tiled=True)  16.7 us
    ppermute x4, starting transfers between devices, swap(): lax.ppermute(side_b, AXES, [(i, (i + 1 ^ 1) - 1) for i in range(1, count...  12.1 us
    ppermute x4, starting transfers between devices, swap(): from_a = lax.ppermute(side_a, AXES, [(i, i ^ 1) for i in range(count)])  10.6 us
    pallas_call x7, Pallas kernels, call(): pl.pallas_call(kernel, out_shape=[jax.ShapeDtypeStruct(s, t) for s, t in...  9.03 us
    ppermute x4, waiting for transfers between devices, swap(): lax.ppermute(side_b, AXES, [(i, (i + 1 ^ 1) - 1) for i in range(1, count...  2.14 us
    ppermute x4, waiting for transfers between devices, swap(): from_a = lax.ppermute(side_a, AXES, [(i, i ^ 1) for i in range(count)])  2.04 us
  transfers between devices with their start and end apart: 8, of which 6 were waited for; matrix products, arithmetic and copies ran while one was open for 0% of the time, Pallas kernels for 0%

profile of v3, /device:TPU:1, one launch (start us, length us, event | category | flops | bytes accessed | tf_op | source)
XLA Modules:
  0.0 84.7 jit_solution(861180583177815065)
XLA Ops:
  0.6 2.4 %shard_map.59 = (f32[48,128]{1,0:T(8,128)S(1)}, f32[48,128]{1,0:T(8,128)S(1)}, bf16[12,12,2048]{2,1,0:T(8,128)(2,1)S(1)}, s32[4,2048]{1,0:T(4,128)S(1)}, s32[16,...) custom-call(f32[3,2048]{1,0:T(4,128)} %load_hbm.1, ...), custom_call_target="tpu_custom_call" | custom-call | tf_op jit(solution)/shard_map/pallas_call | solution.py:408
  3.1 4.6 %collective-permute-start.4 = (f32[16,128]{1,0:T(8,128)S(1)}, f32[16,128]{1,0:T(8,128)S(1)}, u32[]{:S(2)}, u32[]{:S(2)}) collective-permute-start(f32[16,128]{1,0:T(8,128)S(1)} %get-tuple-element.161), channel_id=1, source_target_pairs={{1,2},{2,1},{3,4},{4,3},{5,6},{6,5},{7,8},{8,7},{9,10},{10,9},{11,... | collective-permute-start | bytes 24584 | tf_op jit(solution)/shard_map/ppermute | solution.py:428
  7.7 4.9 %collective-permute-start.5 = (f32[16,128]{1,0:T(8,128)S(1)}, f32[16,128]{1,0:T(8,128)S(1)}, u32[]{:S(2)}, u32[]{:S(2)}) collective-permute-start(f32[16,128]{1,0:T(8,128)S(1)} %get-tuple-element.162), channel_id=1, source_target_pairs={{0,1},{1,0},{2,3},{3,2},{4,5},{5,4},{6,7},{7,6},{8,9},{9,8},{10,11... | collective-permute-start | bytes 24584 | tf_op jit(solution)/shard_map/ppermute | solution.py:429
  12.5 0.0 collective-permute-done.4.near_b
  12.5 0.8 collective-permute-done.5.near_a
  13.3 1.5 %shard_map.60 = (f32[48,128]{1,0:T(8,128)S(1)}, f32[48,128]{1,0:T(8,128)S(1)}, f32[48,128]{1,0:T(8,128)S(1)}, f32[16,128]{1,0:T(8,128)S(1)}, f32[8,128]{1,0:T(8,128)S(1)}, /*index=5*/f32[8,128]{1,0:T(8,128)S(1)}) custom-call(f32[48,128]{1,0:T(8,128)S(1)} %get-tuple-element.154.load_ref, f32[48,128]{1,0:T(8,128)S(1)} %get-tuple-element.155.lumped_ref, ...), custom_call_target="tpu_custom_call" | custom-call | tf_op jit(solution)/shard_map/pallas_call | solution.py:408
  14.8 1.9 %collective-permute-start.6 = (f32[8,128]{1,0:T(8,128)S(1)}, f32[8,128]{1,0:T(8,128)S(1)}, u32[]{:S(2)}, u32[]{:S(2)}) collective-permute-start(f32[8,128]{1,0:T(8,128)S(1)} %get-tuple-element.165), channel_id=1, source_target_pairs={{1,2},{2,1},{3,4},{4,3},{5,6},{6,5},{7,8},{8,7},{9,10},{10,9},{11,... | collective-permute-start | bytes 12296 | tf_op jit(solution)/shard_map/ppermute | solution.py:428
  16.7 1.9 %collective-permute-start.7 = (f32[8,128]{1,0:T(8,128)S(1)}, f32[8,128]{1,0:T(8,128)S(1)}, u32[]{:S(2)}, u32[]{:S(2)}) collective-permute-start(f32[8,128]{1,0:T(8,128)S(1)} %get-tuple-element.166), channel_id=1, source_target_pairs={{0,1},{1,0},{2,3},{3,2},{4,5},{5,4},{6,7},{7,6},{8,9},{9,8},{10,11... | collective-permute-start | bytes 12296 | tf_op jit(solution)/shard_map/ppermute | solution.py:429
  18.7 1.1 %collective-permute-done.6.near_b = f32[8,128]{1,0:T(8,128)S(1)} collective-permute-done((f32[8,128]{1,0:T(8,128)S(1)}, f32[8,128]{1,0:T(8,128)S(1)}, u32[]{:S(2)}, u32[]{:S(2)}) %collective-permute-start.6) | collective-permute-done | bytes 4128 | tf_op jit(solution)/shard_map/ppermute | solution.py:428
  19.7 0.1 collective-permute-done.7.near_a
  19.8 1.4 %shard_map.61 = (f32[48,128]{1,0:T(8,128)S(1)}, f32[48,128]{1,0:T(8,128)S(1)}, f32[16,128]{1,0:T(8,128)S(1)}, f32[8,128]{1,0:T(8,128)S(1)}, f32[8,128]{1,0:T(8,128)S(1)}) custom-call(f32[48,128]{1,0:T(8,128)S(1)} %get-tuple-element.163.past_ref, f32[48,128]{1,0:T(8,128)S(1)} %get-tuple-element.164.diag_ref, f32[48,128]{1,0:T(8,128)S(1)} %get-tuple-element.155.lumped_ref, ...), custom_call_target="tpu_custom_call" | custom-call | tf_op jit(solution)/shard_map/pallas_call | solution.py:408
  21.2 3.6 %collective-permute-start.8 = (f32[8,128]{1,0:T(8,128)S(1)}, f32[8,128]{1,0:T(8,128)S(1)}, u32[]{:S(2)}, u32[]{:S(2)}) collective-permute-start(f32[8,128]{1,0:T(8,128)S(1)} %get-tuple-element.168), channel_id=1, source_target_pairs={{1,2},{2,1},{3,4},{4,3},{5,6},{6,5},{7,8},{8,7},{9,10},{10,9},{11,... | collective-permute-start | bytes 12296 | tf_op jit(solution)/shard_map/ppermute | solution.py:428
  24.9 1.9 %collective-permute-start.9 = (f32[8,128]{1,0:T(8,128)S(1)}, f32[8,128]{1,0:T(8,128)S(1)}, u32[]{:S(2)}, u32[]{:S(2)}) collective-permute-start(f32[8,128]{1,0:T(8,128)S(1)} %get-tuple-element.169), channel_id=1, source_target_pairs={{0,1},{1,0},{2,3},{3,2},{4,5},{5,4},{6,7},{7,6},{8,9},{9,8},{10,11... | collective-permute-start | bytes 12296 | tf_op jit(solution)/shard_map/ppermute | solution.py:429
  26.8 0.0 collective-permute-done.8.near_b
  26.8 1.1 %collective-permute-done.9.near_a = f32[8,128]{1,0:T(8,128)S(1)} collective-permute-done((f32[8,128]{1,0:T(8,128)S(1)}, f32[8,128]{1,0:T(8,128)S(1)}, u32[]{:S(2)}, u32[]{:S(2)}) %collective-permute-start.9) | collective-permute-done | bytes 4128 | tf_op jit(solution)/shard_map/ppermute | solution.py:429
  27.9 1.4 %shard_map.62 = (f32[48,128]{1,0:T(8,128)S(1)}, f32[48,128]{1,0:T(8,128)S(1)}, f32[16,128]{1,0:T(8,128)S(1)}, f32[8,128]{1,0:T(8,128)S(1)}, f32[8,128]{1,0:T(8,128)S(1)}) custom-call(f32[48,128]{1,0:T(8,128)S(1)} %get-tuple-element.167.past_ref, f32[48,128]{1,0:T(8,128)S(1)} %get-tuple-element.164.diag_ref, f32[48,128]{1,0:T(8,128)S(1)} %get-tuple-element.155.lumped_ref, ...), custom_call_target="tpu_custom_call" | custom-call | tf_op jit(solution)/shard_map/pallas_call | solution.py:408
  29.3 1.9 %collective-permute-start.10 = (f32[8,128]{1,0:T(8,128)S(1)}, f32[8,128]{1,0:T(8,128)S(1)}, u32[]{:S(2)}, u32[]{:S(2)}) collective-permute-start(f32[8,128]{1,0:T(8,128)S(1)} %get-tuple-element.171), channel_id=1, source_target_pairs={{1,2},{2,1},{3,4},{4,3},{5,6},{6,5},{7,8},{8,7},{9,10},{10,9},{11,... | collective-permute-start | bytes 12296 | tf_op jit(solution)/shard_map/ppermute | solution.py:428
  31.3 1.9 %collective-permute-start.11 = (f32[8,128]{1,0:T(8,128)S(1)}, f32[8,128]{1,0:T(8,128)S(1)}, u32[]{:S(2)}, u32[]{:S(2)}) collective-permute-start(f32[8,128]{1,0:T(8,128)S(1)} %get-tuple-element.172), channel_id=1, source_target_pairs={{0,1},{1,0},{2,3},{3,2},{4,5},{5,4},{6,7},{7,6},{8,9},{9,8},{10,11... | collective-permute-start | bytes 12296 | tf_op jit(solution)/shard_map/ppermute | solution.py:429
  33.2 1.1 %collective-permute-done.10.near_b = f32[8,128]{1,0:T(8,128)S(1)} collective-permute-done((f32[8,128]{1,0:T(8,128)S(1)}, f32[8,128]{1,0:T(8,128)S(1)}, u32[]{:S(2)}, u32[]{:S(2)}) %collective-permute-start.10) | collective-permute-done | bytes 4128 | tf_op jit(solution)/shard_map/ppermute | solution.py:428
  34.2 0.1 collective-permute-done.11.near_a
  34.3 1.5 %shard_map.63 = (f32[48,128]{1,0:T(8,128)S(1)}, f32[48,128]{1,0:T(8,128)S(1)}, f32[32,8,128]{2,1,0:T(8,128)S(1)}) custom-call(f32[48,128]{1,0:T(8,128)S(1)} %get-tuple-element.170.past_ref, f32[48,128]{1,0:T(8,128)S(1)} %get-tuple-element.164.diag_ref, f32[48,128]{1,0:T(8,128)S(1)} %get-tuple-element.155.lumped_ref, ...), custom_call_target="tpu_custom_call" | custom-call | tf_op jit(solution)/shard_map/pallas_call | solution.py:408
  35.8 30.4 %all_to_all.10.message_ref = f32[32,8,128]{2,1,0:T(8,128)S(1)} all-to-all(f32[32,8,128]{2,1,0:T(8,128)S(1)} %get-tuple-element.176), channel_id=1, replica_groups=mesh['x'=4,'z'=16,'y'=4,'c'=2] {'x','y','c'}, dimensions={0} | all-to-all | bytes 262144 | tf_op jit(solution)/shard_map/all_to_all | solution.py:521
  66.2 16.7 %all_to_all.11.message_ref = f32[16,8,128]{2,1,0:T(8,128)S(1)} all-to-all(f32[16,8,128]{2,1,0:T(8,128)S(1)} %get-tuple-element.177), channel_id=1, replica_groups=mesh['x'=4,'z'=16,'y'=4,'c'=2] {'z'}, dimensions={0} | all-to-all | bytes 131072 | tf_op jit(solution)/shard_map/all_to_all | solution.py:523
  82.8 0.8 shard_map.65
  83.7 0.8 while.28
  (1 shorter events, 0.0 us)
Async XLA Ops:
  3.1 9.5 %collective-permute-start.4 = (f32[16,128]{1,0:T(8,128)S(1)}, f32[16,128]{1,0:T(8,128)S(1)}, u32[]{:S(2)}, u32[]{:S(2)}) collective-permute-start(f32[16,128]{1,0:T(8,128)S(1)} %get-tuple-element.161), channel_id=1, source_target_pairs={{1,2},{2,1},{3,4},{4,3},{5,6},{6,5},{7,8},{8,7},{9,10},{10,9},{11,... | collective-permute-start | bytes 24584 | tf_op jit(solution)/shard_map/ppermute | solution.py:428
  7.7 5.7 %collective-permute-start.5 = (f32[16,128]{1,0:T(8,128)S(1)}, f32[16,128]{1,0:T(8,128)S(1)}, u32[]{:S(2)}, u32[]{:S(2)}) collective-permute-start(f32[16,128]{1,0:T(8,128)S(1)} %get-tuple-element.162), channel_id=1, source_target_pairs={{0,1},{1,0},{2,3},{3,2},{4,5},{5,4},{6,7},{7,6},{8,9},{9,8},{10,11... | collective-permute-start | bytes 24584 | tf_op jit(solution)/shard_map/ppermute | solution.py:429
  14.8 4.9 %collective-permute-start.6 = (f32[8,128]{1,0:T(8,128)S(1)}, f32[8,128]{1,0:T(8,128)S(1)}, u32[]{:S(2)}, u32[]{:S(2)}) collective-permute-start(f32[8,128]{1,0:T(8,128)S(1)} %get-tuple-element.165), channel_id=1, source_target_pairs={{1,2},{2,1},{3,4},{4,3},{5,6},{6,5},{7,8},{8,7},{9,10},{10,9},{11,... | collective-permute-start | bytes 12296 | tf_op jit(solution)/shard_map/ppermute | solution.py:428
  16.7 3.1 %collective-permute-start.7 = (f32[8,128]{1,0:T(8,128)S(1)}, f32[8,128]{1,0:T(8,128)S(1)}, u32[]{:S(2)}, u32[]{:S(2)}) collective-permute-start(f32[8,128]{1,0:T(8,128)S(1)} %get-tuple-element.166), channel_id=1, source_target_pairs={{0,1},{1,0},{2,3},{3,2},{4,5},{5,4},{6,7},{7,6},{8,9},{9,8},{10,11... | collective-permute-start | bytes 12296 | tf_op jit(solution)/shard_map/ppermute | solution.py:429
  21.2 5.6 %collective-permute-start.8 = (f32[8,128]{1,0:T(8,128)S(1)}, f32[8,128]{1,0:T(8,128)S(1)}, u32[]{:S(2)}, u32[]{:S(2)}) collective-permute-start(f32[8,128]{1,0:T(8,128)S(1)} %get-tuple-element.168), channel_id=1, source_target_pairs={{1,2},{2,1},{3,4},{4,3},{5,6},{6,5},{7,8},{8,7},{9,10},{10,9},{11,... | collective-permute-start | bytes 12296 | tf_op jit(solution)/shard_map/ppermute | solution.py:428
  24.9 3.1 %collective-permute-start.9 = (f32[8,128]{1,0:T(8,128)S(1)}, f32[8,128]{1,0:T(8,128)S(1)}, u32[]{:S(2)}, u32[]{:S(2)}) collective-permute-start(f32[8,128]{1,0:T(8,128)S(1)} %get-tuple-element.169), channel_id=1, source_target_pairs={{0,1},{1,0},{2,3},{3,2},{4,5},{5,4},{6,7},{7,6},{8,9},{9,8},{10,11... | collective-permute-start | bytes 12296 | tf_op jit(solution)/shard_map/ppermute | solution.py:429
  29.3 4.9 %collective-permute-start.10 = (f32[8,128]{1,0:T(8,128)S(1)}, f32[8,128]{1,0:T(8,128)S(1)}, u32[]{:S(2)}, u32[]{:S(2)}) collective-permute-start(f32[8,128]{1,0:T(8,128)S(1)} %get-tuple-element.171), channel_id=1, source_target_pairs={{1,2},{2,1},{3,4},{4,3},{5,6},{6,5},{7,8},{8,7},{9,10},{10,9},{11,... | collective-permute-start | bytes 12296 | tf_op jit(solution)/shard_map/ppermute | solution.py:428
  31.3 3.1 %collective-permute-start.11 = (f32[8,128]{1,0:T(8,128)S(1)}, f32[8,128]{1,0:T(8,128)S(1)}, u32[]{:S(2)}, u32[]{:S(2)}) collective-permute-start(f32[8,128]{1,0:T(8,128)S(1)} %get-tuple-element.172), channel_id=1, source_target_pairs={{0,1},{1,0},{2,3},{3,2},{4,5},{5,4},{6,7},{7,6},{8,9},{9,8},{10,11... | collective-permute-start | bytes 12296 | tf_op jit(solution)/shard_map/ppermute | solution.py:429

commit v4 on v3

--- a/solution.py
+++ b/solution.py
@@ -15,6 +15,7 @@
 PIVOT_FLOOR = 0.02
 F32 = jnp.float32
 BF16 = jnp.bfloat16
+EARLY_WORK = pl.CostEstimate(flops=2_000_000, bytes_accessed=400_000, transcendentals=0)
 VMEM_LIMIT = 32 * 1024 * 1024
 
 
@@ -52,19 +53,20 @@
     return out
 
 
-def assembled(field, inverse, near):
+def assembled(field, inverse, near, blocks=range(4)):
     tiles = []
     for c in range(3):
         for half in range(2):
             place = inverse[half * 8 : half * 8 + 8, :]
             lanes, code = place & 127, place >> 7
             parts = []
-            for t in range(4):
+            for t in blocks:
                 row = 2 * c + (t & 1)
                 table = jnp.broadcast_to(near[t >> 1][row : row + 1, :], (8, 128))
                 parts.append(lane_take(table, lanes))
             start = c * 16 + half * 8
-            tiles.append(field[start : start + 8, :] + jnp.where(code < 0, 0.0, pick(parts, code)))
+            here = (code >= blocks[0]) & (code <= blocks[-1])
+            tiles.append(field[start : start + 8, :] + jnp.where(here, pick(parts, code), 0.0))
     return jnp.concatenate(tiles, axis=0)
 
 
@@ -120,7 +122,7 @@
 
 def first_kernel(
     load_hbm, mats_hbm, conn_hbm, shared_hbm,
-    load_out, lumped_out, mats_ref, conn_ref, index_out, inverse_out, lists_out, a_out, b_out,
+    load_out, lumped_out, mats_ref, conn_ref, lists_out, a_out, b_out,
     load_ref, shared_ref, sems,
 ):
     small = [
@@ -149,21 +151,6 @@
         lists.append(jnp.where((sub8 & 1) == 0, first, second))
     lists_out[0:8, :] = lists[0]
     lists_out[8:16, :] = lists[1]
-
-    lane = iota((16, 256), 1)
-    zero = jnp.zeros((), BF16)
-    found = None
-    for t, side in enumerate((side_a, side_b)):
-        mask = high_mask(side)
-        place = jnp.where(mask, (lane & 127).astype(F32).astype(BF16), zero)
-        code = jnp.where(mask, (2 * t + (lane >> 7) + 1).astype(F32).astype(BF16), zero)
-        piece = times_one_hot(jnp.concatenate([place, code], axis=0), side)
-        found = piece if found is None else found + piece
-    inverse_out[...] = (found[16:32].astype(jnp.int32) - 1) * 128 + found[0:16].astype(jnp.int32)
-
-    for j in range(12):
-        index_out[j : j + 1, :] = conn_ref[j // 3 : j // 3 + 1, :]
-    index_out[12:16, :] = jnp.zeros((4, ELEMS), jnp.int32)
 
     for c in range(3):
         for h in range(16):
@@ -195,31 +182,108 @@
     b_out[8:16, :] = lump_b
 
 
-def apply_off_diagonal(field, mats_ref, conn_ref, index_ref, table_ref):
-    sub = iota((8, 128), 0)
-    for block in range(16):
-        rows = field_rows(field, block)
-        table_ref[block, 0:8, :] = by_component(rows, sub % 3)
-        table_ref[block, 8:16, :] = by_component(rows, (sub + 2) % 3)
-
+def at_corners(tables_of, index_ref, out_ref):
+    for t in range(2):
+        tables = tables_of(t)
+        for start in range(0, ELEMS, 128):
+            nodes = index_ref[8 * t : 8 * t + 8, start : start + 128]
+            lanes = nodes & 127
+            out_ref[8 * t : 8 * t + 8, start : start + 128] = pick([lane_take(table, lanes) for table in tables], nodes >> 7)
+
+
+def component_of_row(t):
+    return (iota((8, 128), 0) + 2 * t) % 3
+
+
+def corner_tables(field):
+    rows = [field_rows(field, block) for block in range(16)]
+    return lambda t: [by_component(r, component_of_row(t)) for r in rows]
+
+
+def list_kernel(conn_ref, lists_ref, index_out, inverse_out, place_out):
+    lane = iota((16, 256), 1)
+    zero = jnp.zeros((), BF16)
+    found = None
+    for t in range(2):
+        side = jnp.concatenate([lists_ref[8 * t : 8 * t + 1, :], lists_ref[8 * t + 1 : 8 * t + 2, :]], axis=1)
+        mask = high_mask(side)
+        place = jnp.where(mask, (lane & 127).astype(F32).astype(BF16), zero)
+        code = jnp.where(mask, (2 * t + (lane >> 7) + 1).astype(F32).astype(BF16), zero)
+        piece = times_one_hot(jnp.concatenate([place, code], axis=0), side)
+        found = piece if found is None else found + piece
+    inverse = (found[16:32].astype(jnp.int32) - 1) * 128 + found[0:16].astype(jnp.int32)
+    inverse_out[...] = inverse
+    for j in range(12):
+        index_out[j : j + 1, :] = conn_ref[j // 3 : j // 3 + 1, :]
+    index_out[12:16, :] = jnp.zeros((4, ELEMS), jnp.int32)
+    tables = [jnp.broadcast_to(inverse[block : block + 1, :], (8, 128)) for block in range(16)]
+    at_corners(lambda t: tables, index_out, place_out)
+
+
+def early_kernel(past_ref, index_ref, *rest):
+    if len(rest) == 3:
+        diag_ref, corner_out, scale_out = rest
+        at_corners(corner_tables(1.0 / diag_ref[...]), index_ref, scale_out)
+    else:
+        (corner_out,) = rest
+    at_corners(corner_tables(past_ref[...]), index_ref, corner_out)
+
+
+def apply_off_diagonal(corner, mats_ref, conn_ref):
     def product(start):
+        gathered = corner(start)
+        out = jnp.zeros((12, 128), F32)
+        for j in range(12):
+            column = mats_ref[j, :, start : start + 128].astype(F32)
+            value = gathered[j // 8][j % 8 : j % 8 + 1, :]
+            out = out + column * jnp.broadcast_to(value, (12, 128))
+        return out
+
+    def values_of(start):
+        return jnp.concatenate([product(start), product(start + 128)], axis=1)
+
+    return scatter(values_of, conn_ref)
+
+
+def full_corner(field, index_ref, table_ref):
+    of = corner_tables(field)
+    for t in range(2):
+        for block, table in enumerate(of(t)):
+            table_ref[block, 8 * t : 8 * t + 8, :] = table
+
+    def corner(start):
         index = index_ref[:, start : start + 128]
         gathered = []
         for t in range(2):
             nodes = index[8 * t : 8 * t + 8]
             lanes = nodes & 127
             gathered.append(pick([lane_take(table_ref[block, 8 * t : 8 * t + 8, :], lanes) for block in range(16)], nodes >> 7))
-        out = jnp.zeros((12, 128), F32)
-        for j in range(12):
-            column = mats_ref[j, :, start : start + 128].astype(F32)
-            value = gathered[j // 8][j % 8 : j % 8 + 1, :]
-            out = out + column * jnp.broadcast_to(value, (12, 128))
-        return out
-
-    def values_of(start):
-        return jnp.concatenate([product(start), product(start + 128)], axis=1)
-
-    return scatter(values_of, conn_ref)
+        return gathered
+
+    return corner
+
+
+def late_corner(corner_ref, scale_ref, place_ref, near):
+    tables = []
+    for t in range(2):
+        comp = component_of_row(t)
+        tables.append([])
+        for block in range(4):
+            k, values = block & 1, near[block >> 1]
+            rows = [jnp.broadcast_to(values[2 * c + k : 2 * c + k + 1, :], (8, 128)) for c in range(3)]
+            tables[t].append(by_component(rows, comp))
+
+    def corner(start):
+        gathered = []
+        for t in range(2):
+            at = (slice(8 * t, 8 * t + 8), slice(start, start + 128))
+            place = place_ref[at]
+            lanes, code = place & 127, place >> 7
+            extra = pick([lane_take(table, lanes) for table in tables[t]], code)
+            gathered.append((corner_ref[at] + jnp.where(code >= 0, extra, 0.0)) * scale_ref[at])
+        return gathered
+
+    return corner
 
 
 def tile_sum(product):
@@ -229,8 +293,8 @@
     return out
 
 
-def step(basis, lumped_ref, mats_ref, conn_ref, index_ref, lists_ref, table_ref, image_out, sums_out):
-    image = apply_off_diagonal(basis, mats_ref, conn_ref, index_ref, table_ref)
+def step(basis, corner, lumped_ref, mats_ref, conn_ref, lists_ref, image_out, sums_out):
+    image = apply_off_diagonal(corner, mats_ref, conn_ref)
     image_out[...] = image
     sums_out[0:8, :] = tile_sum(basis * basis * lumped_ref[...])
     sums_out[8:16, :] = tile_sum(basis * image)
@@ -247,18 +311,28 @@
     basis = force / diag
     diag_out[...] = diag
     basis_out[...] = basis
-    halos = step(basis, lumped_ref, mats_ref, conn_ref, index_ref, lists_ref, table_ref, image_out, sums_out)
+    corner = full_corner(basis, index_ref, table_ref)
+    halos = step(basis, corner, lumped_ref, mats_ref, conn_ref, lists_ref, image_out, sums_out)
     a_out[...] = halos[0]
     b_out[...] = halos[1]
 
 
+def late_step(past_ref, corner_ref, scale_ref, place_ref, diag_ref, lumped_ref, inverse_ref, lists_ref, conn_ref, mats_ref, near_b, near_a, basis_out, image_out, sums_out):
+    near = [near_a[...], near_b[...]]
+    basis = assembled(past_ref[...], inverse_ref[...], near) / diag_ref[...]
+    basis_out[...] = basis
+    corner = late_corner(corner_ref, scale_ref, place_ref, near)
+    return step(basis, corner, lumped_ref, mats_ref, conn_ref, lists_ref, image_out, sums_out)
+
+
 def middle_kernel(
-    past_ref, diag_ref, lumped_ref, inverse_ref, lists_ref, index_ref, conn_ref, mats_ref, near_b, near_a,
-    basis_out, image_out, sums_out, a_out, b_out, table_ref,
+    past_ref, corner_ref, scale_ref, place_ref, diag_ref, lumped_ref, inverse_ref, lists_ref, conn_ref, mats_ref, near_b, near_a,
+    basis_out, image_out, sums_out, a_out, b_out,
 ):
-    basis = assembled(past_ref[...], inverse_ref[...], [near_a[...], near_b[...]]) / diag_ref[...]
-    basis_out[...] = basis
-    halos = step(basis, lumped_ref, mats_ref, conn_ref, index_ref, lists_ref, table_ref, image_out, sums_out)
+    halos = late_step(
+        past_ref, corner_ref, scale_ref, place_ref, diag_ref, lumped_ref, inverse_ref, lists_ref, conn_ref, mats_ref, near_b, near_a,
+        basis_out, image_out, sums_out,
+    )
     a_out[...] = halos[0]
     b_out[...] = halos[1]
 
@@ -272,12 +346,14 @@
 
 
 def fourth_kernel(
-    past_ref, diag_ref, lumped_ref, inverse_ref, lists_ref, index_ref, conn_ref, mats_ref, near_b, near_a, sums0, sums1, sums2,
-    basis_out, image_out, message_out, table_ref, sums_ref,
+    past_ref, corner_ref, scale_ref, place_ref, diag_ref, lumped_ref, inverse_ref, lists_ref, conn_ref, mats_ref, near_b, near_a,
+    sums0, sums1, sums2,
+    basis_out, image_out, message_out, sums_ref,
 ):
-    basis = assembled(past_ref[...], inverse_ref[...], [near_a[...], near_b[...]]) / diag_ref[...]
-    basis_out[...] = basis
-    halos = step(basis, lumped_ref, mats_ref, conn_ref, index_ref, lists_ref, table_ref, image_out, sums_ref)
+    halos = late_step(
+        past_ref, corner_ref, scale_ref, place_ref, diag_ref, lumped_ref, inverse_ref, lists_ref, conn_ref, mats_ref, near_b, near_a,
+        basis_out, image_out, sums_ref,
+    )
     lane = iota((8, 128), 1)
     sub = iota((8, 128), 0)
     moments = jnp.zeros((8, 128), F32)
@@ -401,7 +477,7 @@
     flag_out[0, 0] = jnp.min(jnp.where(good, 1, 0))
 
 
-def call(kernel, outs, *args, scratch=(), smem_out=None, space=pltpu.VMEM):
+def call(kernel, outs, *args, scratch=(), smem_out=None, space=pltpu.VMEM, work=None):
     out_specs = [pl.BlockSpec(memory_space=pltpu.VMEM)] * len(outs)
     if smem_out is not None:
         out_specs[smem_out] = pl.BlockSpec(memory_space=pltpu.SMEM)
@@ -412,6 +488,7 @@
         out_specs=out_specs,
         scratch_shapes=list(scratch),
         compiler_params=pltpu.CompilerParams(vmem_limit_bytes=VMEM_LIMIT),
+        cost_estimate=work,
     )(*args)
 
 
@@ -482,40 +559,41 @@
     field = ((48, 128), F32)
     halo = ((8, 128), F32)
     sums = ((16, 128), F32)
+    corners = ((16, ELEMS), F32)
     index = ((16, ELEMS), jnp.int32)
     inverse = ((16, 128), jnp.int32)
-    table = pltpu.VMEM((16, 16, 128), F32)
-    load_f, lumped, mats, conn, index, inverse, lists, a, b = call(
+    load_f, lumped, mats, conn, lists, a, b = call(
         first_kernel,
-        [field, field, ((12, 12, ELEMS), BF16), ((4, ELEMS), jnp.int32), index, inverse, inverse, sums, sums],
+        [field, field, ((12, 12, ELEMS), BF16), ((4, ELEMS), jnp.int32), inverse, sums, sums],
         load, element_mats, connect, shared,
         scratch=[pltpu.VMEM((3, NODES), F32), pltpu.VMEM((2, SHARED), jnp.int32), pltpu.SemaphoreType.DMA((7,))],
         space=pltpu.HBM,
     )
     a, b = swap(a, b)
-    diag, b0, image, sums0, a, b = call(
+    index, inverse, places = call(list_kernel, [index, inverse, index], conn, lists, work=EARLY_WORK)
+    diag, b0, image, total, a, b = call(
         second_kernel,
         [field, field, field, sums, halo, halo],
         load_f, lumped, inverse, lists, index, conn, mats, b, a,
-        scratch=[table],
+        scratch=[pltpu.VMEM((16, 16, 128), F32)],
     )
-    bases, totals = [b0], [sums0]
-    for _ in range(2):
+    bases, totals = [b0], [total]
+    for round_ in range(3):
         a, b = swap(a, b)
-        basis, image, total, a, b = call(
-            middle_kernel,
-            [field, field, sums, halo, halo],
-            image, diag, lumped, inverse, lists, index, conn, mats, b, a,
-            scratch=[table],
-        )
-        bases.append(basis)
-        totals.append(total)
-    a, b = swap(a, b)
+        if round_ == 0:
+            corner, scale = call(early_kernel, [corners, corners], image, index, diag, work=EARLY_WORK)
+        else:
+            (corner,) = call(early_kernel, [corners], image, index, work=EARLY_WORK)
+        args = (image, corner, scale, places, diag, lumped, inverse, lists, conn, mats, b, a)
+        if round_ < 2:
+            basis, image, total, a, b = call(middle_kernel, [field, field, sums, halo, halo], *args)
+            bases.append(basis)
+            totals.append(total)
     basis, image, message = call(
         fourth_kernel,
         [field, field, ((32, 8, 128), F32)],
-        image, diag, lumped, inverse, lists, index, conn, mats, b, a, *totals,
-        scratch=[table, pltpu.VMEM((16, 128), F32)],
+        *args, *totals,
+        scratch=[pltpu.VMEM((16, 128), F32)],
     )
     bases.append(basis)
     message = lax.all_to_all(message, GROUP, 0, 0, tiled=True)

time: 85.1 us -> 84.1 us (0.988)
  waiting for transfers between devices: 4.18 us -> 0.83 us
  Pallas kernels: 9.03 us -> 11.7 us
    pallas_call x7 -> x11, Pallas kernels: 9.03 us -> 11.7 us  [call(): pl.pallas_call(kernel, out_shape=[jax.ShapeDtypeStruct(s, t) for s, t in...]
    ppermute x4, waiting for transfers between devices: 2.14 us -> 0.2 us  [swap(): lax.ppermute(side_b, AXES, [(i, (i + 1 ^ 1) - 1) for i in range(1, count...]
    ppermute x4, waiting for transfers between devices: 2.04 us -> 0.64 us  [swap(): from_a = lax.ppermute(side_a, AXES, [(i, i ^ 1) for i in range(count)])]
  transfers between devices with their start and end apart: 8 -> 8, of which waited for: 6 -> 3; matrix products, arithmetic and copies ran while one was open for 0% -> 0% of each run, Pallas kernels for 0% -> 4%
where the time goes in v4:
time: 84.1 us; the launch traced here: 83.6 us
  blocking collectives  46.5 us (55%)
  starting transfers between devices  22.9 us (27%)
  Pallas kernels  11.7 us (14%)
  between operations  0.99 us (1%)
    all_to_all x1, blocking collectives, body(): message = lax.all_to_all(message, GROUP, 0, 0, tiled=True)  30.1 us
    all_to_all x1, blocking collectives, body(): message = lax.all_to_all(message, 'z', 0, 0, tiled=True)  16.4 us
    ppermute x4, starting transfers between devices, swap(): lax.ppermute(side_b, AXES, [(i, (i + 1 ^ 1) - 1) for i in range(1, count...  12.2 us
    pallas_call x11, Pallas kernels, call(): pl.pallas_call(kernel, out_shape=[jax.ShapeDtypeStruct(s, t) for s, t in...  11.7 us
    ppermute x4, starting transfers between devices, swap(): from_a = lax.ppermute(side_a, AXES, [(i, i ^ 1) for i in range(count)])  10.6 us
  transfers between devices with their start and end apart: 8, of which 3 were waited for; matrix products, arithmetic and copies ran while one was open for 0% of the time, Pallas kernels for 4%

profile of v4, /device:TPU:1, one launch (start us, length us, event | category | flops | bytes accessed | tf_op | source)
XLA Modules:
  0.0 83.6 jit_solution(7947127481812562364)
XLA Ops:
  0.6 2.3 %shard_map.59 = (f32[48,128]{1,0:T(8,128)S(1)}, f32[48,128]{1,0:T(8,128)S(1)}, bf16[12,12,2048]{2,1,0:T(8,128)(2,1)S(1)}, s32[4,2048]{1,0:T(4,128)S(1)}, s32[16,...) custom-call(f32[3,2048]{1,0:T(4,128)} %load_hbm.1, bf16[12,12,2048]{2,1,0:T(8,128)(2,1)} %mats_hbm.1, ...), custom_call_target="tpu_custom_call" | custom-call | tf_op jit(solution)/shard_map/pallas_call | solution.py:484
  2.9 4.6 %collective-permute-start.4 = (f32[16,128]{1,0:T(8,128)S(1)}, f32[16,128]{1,0:T(8,128)S(1)}, u32[]{:S(2)}, u32[]{:S(2)}) collective-permute-start(f32[16,128]{1,0:T(8,128)S(1)} %get-tuple-element.164), channel_id=1, source_target_pairs={{1,2},{2,1},{3,4},{4,3},{5,6},{6,5},{7,8},{8,7},{9,10},{10,9},{11,... | collective-permute-start | bytes 24584 | tf_op jit(solution)/shard_map/ppermute | solution.py:505
  7.5 4.9 %collective-permute-start.5 = (f32[16,128]{1,0:T(8,128)S(1)}, f32[16,128]{1,0:T(8,128)S(1)}, u32[]{:S(2)}, u32[]{:S(2)}) collective-permute-start(f32[16,128]{1,0:T(8,128)S(1)} %get-tuple-element.165), channel_id=1, source_target_pairs={{0,1},{1,0},{2,3},{3,2},{4,5},{5,4},{6,7},{7,6},{8,9},{9,8},{10,11... | collective-permute-start | bytes 24584 | tf_op jit(solution)/shard_map/ppermute | solution.py:506
  12.4 0.9 %shard_map.60 = (s32[16,2048]{1,0:T(8,128)S(1)}, s32[16,128]{1,0:T(8,128)S(1)}, s32[16,2048]{1,0:T(8,128)S(1)}) custom-call(s32[4,2048]{1,0:T(4,128)S(1)} %get-tuple-element.159.conn_ref, s32[16,128]{1,0:T(8,128)S(1)} %get-tuple-element.160.lists_ref), custom_call_target="tpu_custom_call" | custom-call | flops 2000000 | bytes 400000 | tf_op jit(solution)/shard_map/pallas_call | solution.py:484
  13.3 0.0 collective-permute-done.4.near_b
  13.3 0.0 collective-permute-done.5.near_a
  13.3 1.5 %shard_map.61 = (f32[48,128]{1,0:T(8,128)S(1)}, f32[48,128]{1,0:T(8,128)S(1)}, f32[48,128]{1,0:T(8,128)S(1)}, f32[16,128]{1,0:T(8,128)S(1)}, f32[8,128]{1,0:T(8,128)S(1)}, /*index=5*/f32[8,128]{1,0:T(8,128)S(1)}) custom-call(f32[48,128]{1,0:T(8,128)S(1)} %get-tuple-element.157.load_ref, f32[48,128]{1,0:T(8,128)S(1)} %get-tuple-element.158.lumped_ref, ...), custom_call_target="tpu_custom_call" | custom-call | tf_op jit(solution)/shard_map/pallas_call | solution.py:484
  14.8 1.9 %collective-permute-start.6 = (f32[8,128]{1,0:T(8,128)S(1)}, f32[8,128]{1,0:T(8,128)S(1)}, u32[]{:S(2)}, u32[]{:S(2)}) collective-permute-start(f32[8,128]{1,0:T(8,128)S(1)} %get-tuple-element.171), channel_id=1, source_target_pairs={{1,2},{2,1},{3,4},{4,3},{5,6},{6,5},{7,8},{8,7},{9,10},{10,9},{11,... | collective-permute-start | bytes 12296 | tf_op jit(solution)/shard_map/ppermute | solution.py:505
  16.7 1.9 %collective-permute-start.7 = (f32[8,128]{1,0:T(8,128)S(1)}, f32[8,128]{1,0:T(8,128)S(1)}, u32[]{:S(2)}, u32[]{:S(2)}) collective-permute-start(f32[8,128]{1,0:T(8,128)S(1)} %get-tuple-element.172), channel_id=1, source_target_pairs={{0,1},{1,0},{2,3},{3,2},{4,5},{5,4},{6,7},{7,6},{8,9},{9,8},{10,11... | collective-permute-start | bytes 12296 | tf_op jit(solution)/shard_map/ppermute | solution.py:506
  18.6 1.4 %shard_map.62 = (f32[16,2048]{1,0:T(8,128)S(1)}, f32[16,2048]{1,0:T(8,128)S(1)}) custom-call(f32[48,128]{1,0:T(8,128)S(1)} %get-tuple-element.166.past_ref, s32[16,2048]{1,0:T(8,128)S(1)} %get-tuple-element.162.index_ref, f32[48,128]{1,0:T(8,128)S(1)} %get-tuple-element.167.rest_0_.diag_ref), custom_call_target="tpu_custom_call" | custom-call | flops 2000000 | bytes 400000 | tf_op jit(solution)/shard_map/pallas_call | solution.py:484
  20.0 0.0 collective-permute-done.6.near_b
  20.0 0.0 collective-permute-done.7.near_a
  20.0 1.1 %shard_map.63 = (f32[48,128]{1,0:T(8,128)S(1)}, f32[48,128]{1,0:T(8,128)S(1)}, f32[16,128]{1,0:T(8,128)S(1)}, f32[8,128]{1,0:T(8,128)S(1)}, f32[8,128]{1,0:T(8,128)S(1)}) custom-call(f32[48,128]{1,0:T(8,128)S(1)} %get-tuple-element.166.past_ref, f32[16,2048]{1,0:T(8,128)S(1)} %get-tuple-element.168.corner_ref, f32[16,2048]{1,0:T(8,128)S(1)} %get-tuple-element.169.scale_ref, ...), custom_call_target="tpu_custom_call" | custom-call | tf_op jit(solution)/shard_map/pallas_call | solution.py:484
  21.1 3.6 %collective-permute-start.8 = (f32[8,128]{1,0:T(8,128)S(1)}, f32[8,128]{1,0:T(8,128)S(1)}, u32[]{:S(2)}, u32[]{:S(2)}) collective-permute-start(f32[8,128]{1,0:T(8,128)S(1)} %get-tuple-element.174), channel_id=1, source_target_pairs={{1,2},{2,1},{3,4},{4,3},{5,6},{6,5},{7,8},{8,7},{9,10},{10,9},{11,... | collective-permute-start | bytes 12296 | tf_op jit(solution)/shard_map/ppermute | solution.py:505
  24.8 1.9 %collective-permute-start.9 = (f32[8,128]{1,0:T(8,128)S(1)}, f32[8,128]{1,0:T(8,128)S(1)}, u32[]{:S(2)}, u32[]{:S(2)}) collective-permute-start(f32[8,128]{1,0:T(8,128)S(1)} %get-tuple-element.175), channel_id=1, source_target_pairs={{0,1},{1,0},{2,3},{3,2},{4,5},{5,4},{6,7},{7,6},{8,9},{9,8},{10,11... | collective-permute-start | bytes 12296 | tf_op jit(solution)/shard_map/ppermute | solution.py:506
  26.7 0.7 shard_map.64.corner_ref
  27.4 0.0 collective-permute-done.8.near_b
  27.4 0.4 collective-permute-done.9.near_a
  27.8 1.1 %shard_map.65 = (f32[48,128]{1,0:T(8,128)S(1)}, f32[48,128]{1,0:T(8,128)S(1)}, f32[16,128]{1,0:T(8,128)S(1)}, f32[8,128]{1,0:T(8,128)S(1)}, f32[8,128]{1,0:T(8,128)S(1)}) custom-call(f32[48,128]{1,0:T(8,128)S(1)} %get-tuple-element.173.past_ref, f32[16,2048]{1,0:T(8,128)S(1)} %shard_map.64.corner_ref, f32[16,2048]{1,0:T(8,128)S(1)} %get-tuple-element.169.scale_ref, ...), custom_call_target="tpu_custom_call" | custom-call | tf_op jit(solution)/shard_map/pallas_call | solution.py:484
  29.0 2.1 %collective-permute-start.10 = (f32[8,128]{1,0:T(8,128)S(1)}, f32[8,128]{1,0:T(8,128)S(1)}, u32[]{:S(2)}, u32[]{:S(2)}) collective-permute-start(f32[8,128]{1,0:T(8,128)S(1)} %get-tuple-element.177), channel_id=1, source_target_pairs={{1,2},{2,1},{3,4},{4,3},{5,6},{6,5},{7,8},{8,7},{9,10},{10,9},{11,... | collective-permute-start | bytes 12296 | tf_op jit(solution)/shard_map/ppermute | solution.py:505
  31.0 1.9 %collective-permute-start.11 = (f32[8,128]{1,0:T(8,128)S(1)}, f32[8,128]{1,0:T(8,128)S(1)}, u32[]{:S(2)}, u32[]{:S(2)}) collective-permute-start(f32[8,128]{1,0:T(8,128)S(1)} %get-tuple-element.178), channel_id=1, source_target_pairs={{0,1},{1,0},{2,3},{3,2},{4,5},{5,4},{6,7},{7,6},{8,9},{9,8},{10,11... | collective-permute-start | bytes 12296 | tf_op jit(solution)/shard_map/ppermute | solution.py:506
  33.0 0.7 shard_map.66.corner_ref
  33.7 0.2 collective-permute-done.10.near_b
  33.9 0.2 collective-permute-done.11.near_a
  34.1 1.2 %shard_map.67 = (f32[48,128]{1,0:T(8,128)S(1)}, f32[48,128]{1,0:T(8,128)S(1)}, f32[32,8,128]{2,1,0:T(8,128)S(1)}) custom-call(f32[48,128]{1,0:T(8,128)S(1)} %get-tuple-element.176.past_ref, f32[16,2048]{1,0:T(8,128)S(1)} %shard_map.66.corner_ref, f32[16,2048]{1,0:T(8,128)S(1)} %get-tuple-element.169.scale_ref, s32[16,2048]{1,0:T(8,128)S(1)} %get-tuple-element.170.place_ref, ...), custom_call_target="tpu_custom_call" | custom-call | tf_op jit(solution)/shard_map/pallas_call | solution.py:484
  35.3 30.1 %all_to_all.10.message_ref = f32[32,8,128]{2,1,0:T(8,128)S(1)} all-to-all(f32[32,8,128]{2,1,0:T(8,128)S(1)} %get-tuple-element.182), channel_id=1, replica_groups=mesh['x'=4,'z'=16,'y'=4,'c'=2] {'x','y','c'}, dimensions={0} | all-to-all | bytes 262144 | tf_op jit(solution)/shard_map/all_to_all | solution.py:599
  65.4 16.4 %all_to_all.11.message_ref = f32[16,8,128]{2,1,0:T(8,128)S(1)} all-to-all(f32[16,8,128]{2,1,0:T(8,128)S(1)} %get-tuple-element.183), channel_id=1, replica_groups=mesh['x'=4,'z'=16,'y'=4,'c'=2] {'z'}, dimensions={0} | all-to-all | bytes 131072 | tf_op jit(solution)/shard_map/all_to_all | solution.py:601
  81.8 0.8 %shard_map.69 = (f32[3,2048]{1,0:T(4,128)}, f32[3,2048]{1,0:T(4,128)}, s32[1,1]{1,0:T(1,128)}) custom-call(f32[16,8,128]{2,1,0:T(8,128)S(1)} %all_to_all.11.message_ref, f32[16,128]{1,0:T(8,128)S(1)} %get-tuple-element.184.direct_ref, f32[48,128]{1,0:T(8,128)S(1)} %get-tuple-element.185.image_ref, f32[48,128]{1,0:T(8,128)S(1)} %get-tuple-element.167.rest_0_.diag_ref, ...), custom_call_target="tpu_custom_call" | custom-call | tf_op jit(solution)/shard_map/pallas_call | solution.py:484
  82.7 0.8 while.28
  (1 shorter events, 0.0 us)
Async XLA Ops:
  2.9 10.4 %collective-permute-start.4 = (f32[16,128]{1,0:T(8,128)S(1)}, f32[16,128]{1,0:T(8,128)S(1)}, u32[]{:S(2)}, u32[]{:S(2)}) collective-permute-start(f32[16,128]{1,0:T(8,128)S(1)} %get-tuple-element.164), channel_id=1, source_target_pairs={{1,2},{2,1},{3,4},{4,3},{5,6},{6,5},{7,8},{8,7},{9,10},{10,9},{11,... | collective-permute-start | bytes 24584 | tf_op jit(solution)/shard_map/ppermute | solution.py:505
  7.5 5.8 %collective-permute-start.5 = (f32[16,128]{1,0:T(8,128)S(1)}, f32[16,128]{1,0:T(8,128)S(1)}, u32[]{:S(2)}, u32[]{:S(2)}) collective-permute-start(f32[16,128]{1,0:T(8,128)S(1)} %get-tuple-element.165), channel_id=1, source_target_pairs={{0,1},{1,0},{2,3},{3,2},{4,5},{5,4},{6,7},{7,6},{8,9},{9,8},{10,11... | collective-permute-start | bytes 24584 | tf_op jit(solution)/shard_map/ppermute | solution.py:506
  14.8 5.2 %collective-permute-start.6 = (f32[8,128]{1,0:T(8,128)S(1)}, f32[8,128]{1,0:T(8,128)S(1)}, u32[]{:S(2)}, u32[]{:S(2)}) collective-permute-start(f32[8,128]{1,0:T(8,128)S(1)} %get-tuple-element.171), channel_id=1, source_target_pairs={{1,2},{2,1},{3,4},{4,3},{5,6},{6,5},{7,8},{8,7},{9,10},{10,9},{11,... | collective-permute-start | bytes 12296 | tf_op jit(solution)/shard_map/ppermute | solution.py:505
  16.7 3.3 %collective-permute-start.7 = (f32[8,128]{1,0:T(8,128)S(1)}, f32[8,128]{1,0:T(8,128)S(1)}, u32[]{:S(2)}, u32[]{:S(2)}) collective-permute-start(f32[8,128]{1,0:T(8,128)S(1)} %get-tuple-element.172), channel_id=1, source_target_pairs={{0,1},{1,0},{2,3},{3,2},{4,5},{5,4},{6,7},{7,6},{8,9},{9,8},{10,11... | collective-permute-start | bytes 12296 | tf_op jit(solution)/shard_map/ppermute | solution.py:506
  21.1 6.3 %collective-permute-start.8 = (f32[8,128]{1,0:T(8,128)S(1)}, f32[8,128]{1,0:T(8,128)S(1)}, u32[]{:S(2)}, u32[]{:S(2)}) collective-permute-start(f32[8,128]{1,0:T(8,128)S(1)} %get-tuple-element.174), channel_id=1, source_target_pairs={{1,2},{2,1},{3,4},{4,3},{5,6},{6,5},{7,8},{8,7},{9,10},{10,9},{11,... | collective-permute-start | bytes 12296 | tf_op jit(solution)/shard_map/ppermute | solution.py:505
  24.8 3.1 %collective-permute-start.9 = (f32[8,128]{1,0:T(8,128)S(1)}, f32[8,128]{1,0:T(8,128)S(1)}, u32[]{:S(2)}, u32[]{:S(2)}) collective-permute-start(f32[8,128]{1,0:T(8,128)S(1)} %get-tuple-element.175), channel_id=1, source_target_pairs={{0,1},{1,0},{2,3},{3,2},{4,5},{5,4},{6,7},{7,6},{8,9},{9,8},{10,11... | collective-permute-start | bytes 12296 | tf_op jit(solution)/shard_map/ppermute | solution.py:506
  29.0 4.9 %collective-permute-start.10 = (f32[8,128]{1,0:T(8,128)S(1)}, f32[8,128]{1,0:T(8,128)S(1)}, u32[]{:S(2)}, u32[]{:S(2)}) collective-permute-start(f32[8,128]{1,0:T(8,128)S(1)} %get-tuple-element.177), channel_id=1, source_target_pairs={{1,2},{2,1},{3,4},{4,3},{5,6},{6,5},{7,8},{8,7},{9,10},{10,9},{11,... | collective-permute-start | bytes 12296 | tf_op jit(solution)/shard_map/ppermute | solution.py:505
  31.0 3.1 %collective-permute-start.11 = (f32[8,128]{1,0:T(8,128)S(1)}, f32[8,128]{1,0:T(8,128)S(1)}, u32[]{:S(2)}, u32[]{:S(2)}) collective-permute-start(f32[8,128]{1,0:T(8,128)S(1)} %get-tuple-element.178), channel_id=1, source_target_pairs={{0,1},{1,0},{2,3},{3,2},{4,5},{5,4},{6,7},{7,6},{8,9},{9,8},{10,11... | collective-permute-start | bytes 12296 | tf_op jit(solution)/shard_map/ppermute | solution.py:506

commit v5 on v4

--- a/solution.py
+++ b/solution.py
@@ -105,14 +105,13 @@
     return lax.dot_general(lhs, hot, (((1,), (1,)), ((), ())), preferred_element_type=F32)
 
 
-def scatter(values_of, conn_ref):
+def scatter(values_of, conn_ref, hot_ref):
     total = None
     for block in range(ELEMS // 256):
         start = block * 256
-        conn = conn_ref[:, start : start + 256]
-        lhs = corner_lhs(values_of(start), conn)
+        lhs = corner_lhs(values_of(start), conn_ref[:, start : start + 256])
         for n in range(4):
-            piece = times_one_hot(lhs[n], conn[n : n + 1, :])
+            piece = jnp.dot(lhs[n], hot_ref[n, start : start + 256, :], preferred_element_type=F32)
             total = piece if total is None else total + piece
     out = total[0:48]
     for t in range(1, SPLITS):
@@ -131,7 +130,7 @@
         pltpu.make_async_copy(load_hbm, load_ref, sems.at[2]),
     ]
     large = [
-        pltpu.make_async_copy(mats_hbm.at[pl.ds(3 * i, 3)], mats_ref.at[pl.ds(3 * i, 3)], sems.at[3 + i]) for i in range(4)
+        pltpu.make_async_copy(mats_hbm.at[i], mats_ref.at[i], sems.at[3 + i]) for i in range(12)
     ]
     for copy in small[:2] + large + small[2:]:
         copy.start()
@@ -200,7 +199,7 @@
     return lambda t: [by_component(r, component_of_row(t)) for r in rows]
 
 
-def list_kernel(conn_ref, lists_ref, index_out, inverse_out, place_out):
+def list_kernel(conn_ref, lists_ref, index_out, inverse_out, place_out, hot_out):
     lane = iota((16, 256), 1)
     zero = jnp.zeros((), BF16)
     found = None
@@ -218,6 +217,13 @@
     index_out[12:16, :] = jnp.zeros((4, ELEMS), jnp.int32)
     tables = [jnp.broadcast_to(inverse[block : block + 1, :], (8, 128)) for block in range(16)]
     at_corners(lambda t: tables, index_out, place_out)
+    lane128 = iota((128, 128), 1).astype(F32)
+    for start in range(0, ELEMS, 128):
+        low = (conn_ref[:, start : start + 128] & 127).astype(F32)
+        columns = jnp.concatenate([low, low], axis=0).T
+        for n in range(4):
+            same_low = jnp.broadcast_to(columns[:, n : n + 1], (128, 128)) == lane128
+            hot_out[n, start : start + 128, :] = jnp.where(same_low, 1.0, 0.0).astype(BF16)
 
 
 def early_kernel(past_ref, index_ref, *rest):
@@ -229,7 +235,7 @@
     at_corners(corner_tables(past_ref[...]), index_ref, corner_out)
 
 
-def apply_off_diagonal(corner, mats_ref, conn_ref):
+def apply_off_diagonal(corner, mats_ref, conn_ref, hot_ref):
     def product(start):
         gathered = corner(start)
         out = jnp.zeros((12, 128), F32)
@@ -242,7 +248,7 @@
     def values_of(start):
         return jnp.concatenate([product(start), product(start + 128)], axis=1)
 
-    return scatter(values_of, conn_ref)
+    return scatter(values_of, conn_ref, hot_ref)
 
 
 def full_corner(field, index_ref, table_ref):
@@ -293,8 +299,8 @@
     return out
 
 
-def step(basis, corner, lumped_ref, mats_ref, conn_ref, lists_ref, image_out, sums_out):
-    image = apply_off_diagonal(corner, mats_ref, conn_ref)
+def step(basis, corner, lumped_ref, mats_ref, conn_ref, hot_ref, lists_ref, image_out, sums_out):
+    image = apply_off_diagonal(corner, mats_ref, conn_ref, hot_ref)
     image_out[...] = image
     sums_out[0:8, :] = tile_sum(basis * basis * lumped_ref[...])
     sums_out[8:16, :] = tile_sum(basis * image)
@@ -302,7 +308,7 @@
 
 
 def second_kernel(
-    load_ref, lumped_ref, inverse_ref, lists_ref, index_ref, conn_ref, mats_ref, near_b, near_a,
+    load_ref, lumped_ref, inverse_ref, lists_ref, index_ref, conn_ref, hot_ref, mats_ref, near_b, near_a,
     diag_out, basis_out, image_out, sums_out, a_out, b_out, table_ref,
 ):
     inverse = inverse_ref[...]
@@ -312,25 +318,25 @@
     diag_out[...] = diag
     basis_out[...] = basis
     corner = full_corner(basis, index_ref, table_ref)
-    halos = step(basis, corner, lumped_ref, mats_ref, conn_ref, lists_ref, image_out, sums_out)
+    halos = step(basis, corner, lumped_ref, mats_ref, conn_ref, hot_ref, lists_ref, image_out, sums_out)
     a_out[...] = halos[0]
     b_out[...] = halos[1]
 
 
-def late_step(past_ref, corner_ref, scale_ref, place_ref, diag_ref, lumped_ref, inverse_ref, lists_ref, conn_ref, mats_ref, near_b, near_a, basis_out, image_out, sums_out):
+def late_step(past_ref, corner_ref, scale_ref, place_ref, diag_ref, lumped_ref, inverse_ref, lists_ref, conn_ref, hot_ref, mats_ref, near_b, near_a, basis_out, image_out, sums_out):
     near = [near_a[...], near_b[...]]
     basis = assembled(past_ref[...], inverse_ref[...], near) / diag_ref[...]
     basis_out[...] = basis
     corner = late_corner(corner_ref, scale_ref, place_ref, near)
-    return step(basis, corner, lumped_ref, mats_ref, conn_ref, lists_ref, image_out, sums_out)
+    return step(basis, corner, lumped_ref, mats_ref, conn_ref, hot_ref, lists_ref, image_out, sums_out)
 
 
 def middle_kernel(
-    past_ref, corner_ref, scale_ref, place_ref, diag_ref, lumped_ref, inverse_ref, lists_ref, conn_ref, mats_ref, near_b, near_a,
+    past_ref, corner_ref, scale_ref, place_ref, diag_ref, lumped_ref, inverse_ref, lists_ref, conn_ref, hot_ref, mats_ref, near_b, near_a,
     basis_out, image_out, sums_out, a_out, b_out,
 ):
     halos = late_step(
-        past_ref, corner_ref, scale_ref, place_ref, diag_ref, lumped_ref, inverse_ref, lists_ref, conn_ref, mats_ref, near_b, near_a,
+        past_ref, corner_ref, scale_ref, place_ref, diag_ref, lumped_ref, inverse_ref, lists_ref, conn_ref, hot_ref, mats_ref, near_b, near_a,
         basis_out, image_out, sums_out,
     )
     a_out[...] = halos[0]
@@ -346,12 +352,12 @@
 
 
 def fourth_kernel(
-    past_ref, corner_ref, scale_ref, place_ref, diag_ref, lumped_ref, inverse_ref, lists_ref, conn_ref, mats_ref, near_b, near_a,
+    past_ref, corner_ref, scale_ref, place_ref, diag_ref, lumped_ref, inverse_ref, lists_ref, conn_ref, hot_ref, mats_ref, near_b, near_a,
     sums0, sums1, sums2,
     basis_out, image_out, message_out, sums_ref,
 ):
     halos = late_step(
-        past_ref, corner_ref, scale_ref, place_ref, diag_ref, lumped_ref, inverse_ref, lists_ref, conn_ref, mats_ref, near_b, near_a,
+        past_ref, corner_ref, scale_ref, place_ref, diag_ref, lumped_ref, inverse_ref, lists_ref, conn_ref, hot_ref, mats_ref, near_b, near_a,
         basis_out, image_out, sums_ref,
     )
     lane = iota((8, 128), 1)
@@ -566,15 +572,17 @@
         first_kernel,
         [field, field, ((12, 12, ELEMS), BF16), ((4, ELEMS), jnp.int32), inverse, sums, sums],
         load, element_mats, connect, shared,
-        scratch=[pltpu.VMEM((3, NODES), F32), pltpu.VMEM((2, SHARED), jnp.int32), pltpu.SemaphoreType.DMA((7,))],
+        scratch=[pltpu.VMEM((3, NODES), F32), pltpu.VMEM((2, SHARED), jnp.int32), pltpu.SemaphoreType.DMA((15,))],
         space=pltpu.HBM,
     )
     a, b = swap(a, b)
-    index, inverse, places = call(list_kernel, [index, inverse, index], conn, lists, work=EARLY_WORK)
+    index, inverse, places, hot = call(
+        list_kernel, [index, inverse, index, ((4, ELEMS, 128), BF16)], conn, lists, work=EARLY_WORK
+    )
     diag, b0, image, total, a, b = call(
         second_kernel,
         [field, field, field, sums, halo, halo],
-        load_f, lumped, inverse, lists, index, conn, mats, b, a,
+        load_f, lumped, inverse, lists, index, conn, hot, mats, b, a,
         scratch=[pltpu.VMEM((16, 16, 128), F32)],
     )
     bases, totals = [b0], [total]
@@ -584,7 +592,7 @@
             corner, scale = call(early_kernel, [corners, corners], image, index, diag, work=EARLY_WORK)
         else:
             (corner,) = call(early_kernel, [corners], image, index, work=EARLY_WORK)
-        args = (image, corner, scale, places, diag, lumped, inverse, lists, conn, mats, b, a)
+        args = (image, corner, scale, places, diag, lumped, inverse, lists, conn, hot, mats, b, a)
         if round_ < 2:
             basis, image, total, a, b = call(middle_kernel, [field, field, sums, halo, halo], *args)
             bases.append(basis)

time: 84.1 us -> 84.1 us (level)
  Pallas kernels: 11.7 us -> 13 us
  blocking collectives: 46.5 us -> 45.2 us
    pallas_call x11, Pallas kernels: 11.7 us -> 13 us  [call(): pl.pallas_call(kernel, out_shape=[jax.ShapeDtypeStruct(s, t) for s, t in...]
  transfers between devices with their start and end apart: 8 -> 8, of which waited for: 3 -> 3; matrix products, arithmetic and copies ran while one was open for 0% -> 0% of each run, Pallas kernels for 4% -> 6%
where the time goes in v5:
time: 84.1 us; the launch traced here: 83.7 us
  blocking collectives  45.2 us (54%)
  starting transfers between devices  22.8 us (27%)
  Pallas kernels  13 us (15%)
  between operations  0.99 us (1%)
    all_to_all x1, blocking collectives, body(): message = lax.all_to_all(message, GROUP, 0, 0, tiled=True)  29.6 us
    all_to_all x1, blocking collectives, body(): message = lax.all_to_all(message, 'z', 0, 0, tiled=True)  15.6 us
    pallas_call x11, Pallas kernels, call(): pl.pallas_call(kernel, out_shape=[jax.ShapeDtypeStruct(s, t) for s, t in...  13 us
    ppermute x4, starting transfers between devices, swap(): lax.ppermute(side_b, AXES, [(i, (i + 1 ^ 1) - 1) for i in range(1, count...  12.2 us
    ppermute x4, starting transfers between devices, swap(): from_a = lax.ppermute(side_a, AXES, [(i, i ^ 1) for i in range(count)])  10.6 us
  transfers between devices with their start and end apart: 8, of which 3 were waited for; matrix products, arithmetic and copies ran while one was open for 0% of the time, Pallas kernels for 6%

profile of v5, /device:TPU:1, one launch (start us, length us, event | category | flops | bytes accessed | tf_op | source)
XLA Modules:
  0.0 83.7 jit_solution(2746801148181495154)
XLA Ops:
  0.6 2.4 %shard_map.59 = (f32[48,128]{1,0:T(8,128)S(1)}, f32[48,128]{1,0:T(8,128)S(1)}, bf16[12,12,2048]{2,1,0:T(8,128)(2,1)S(1)}, s32[4,2048]{1,0:T(4,128)S(1)}, s32[16,...) custom-call(f32[3,2048]{1,0:T(4,128)} %load_hbm.1, bf16[12,12,2048]{2,1,0:T(8,128)(2,1)} %mats_hbm.1, ...), custom_call_target="tpu_custom_call" | custom-call | tf_op jit(solution)/shard_map/pallas_call | solution.py:490
  3.0 4.6 %collective-permute-start.4 = (f32[16,128]{1,0:T(8,128)S(1)}, f32[16,128]{1,0:T(8,128)S(1)}, u32[]{:S(2)}, u32[]{:S(2)}) collective-permute-start(f32[16,128]{1,0:T(8,128)S(1)} %get-tuple-element.166), channel_id=1, source_target_pairs={{1,2},{2,1},{3,4},{4,3},{5,6},{6,5},{7,8},{8,7},{9,10},{10,9},{11,... | collective-permute-start | bytes 24584 | tf_op jit(solution)/shard_map/ppermute | solution.py:511
  7.6 4.9 %collective-permute-start.5 = (f32[16,128]{1,0:T(8,128)S(1)}, f32[16,128]{1,0:T(8,128)S(1)}, u32[]{:S(2)}, u32[]{:S(2)}) collective-permute-start(f32[16,128]{1,0:T(8,128)S(1)} %get-tuple-element.167), channel_id=1, source_target_pairs={{0,1},{1,0},{2,3},{3,2},{4,5},{5,4},{6,7},{7,6},{8,9},{9,8},{10,11... | collective-permute-start | bytes 24584 | tf_op jit(solution)/shard_map/ppermute | solution.py:512
  12.4 2.2 %shard_map.60 = (s32[16,2048]{1,0:T(8,128)S(1)}, s32[16,128]{1,0:T(8,128)S(1)}, s32[16,2048]{1,0:T(8,128)S(1)}, bf16[4,2048,128]{2,1,0:T(8,128)(2,1)S(1)}) custom-call(s32[4,2048]{1,0:T(4,128)S(1)} %get-tuple-element.160.conn_ref, s32[16,128]{1,0:T(8,128)S(1)} %get-tuple-element.161.lists_ref), custom_call_target="tpu_custom_call" | custom-call | flops 2000000 | bytes 400000 | tf_op jit(solution)/shard_map/pallas_call | solution.py:490
  14.6 0.0 collective-permute-done.4.near_b
  14.7 0.0 collective-permute-done.5.near_a
  14.7 1.4 %shard_map.61 = (f32[48,128]{1,0:T(8,128)S(1)}, f32[48,128]{1,0:T(8,128)S(1)}, f32[48,128]{1,0:T(8,128)S(1)}, f32[16,128]{1,0:T(8,128)S(1)}, f32[8,128]{1,0:T(8,128)S(1)}, /*index=5*/f32[8,128]{1,0:T(8,128)S(1)}) custom-call(f32[48,128]{1,0:T(8,128)S(1)} %get-tuple-element.158.load_ref, f32[48,128]{1,0:T(8,128)S(1)} %get-tuple-element.159.lumped_ref, ...), custom_call_target="tpu_custom_call" | custom-call | tf_op jit(solution)/shard_map/pallas_call | solution.py:490
  16.1 1.9 %collective-permute-start.6 = (f32[8,128]{1,0:T(8,128)S(1)}, f32[8,128]{1,0:T(8,128)S(1)}, u32[]{:S(2)}, u32[]{:S(2)}) collective-permute-start(f32[8,128]{1,0:T(8,128)S(1)} %get-tuple-element.173), channel_id=1, source_target_pairs={{1,2},{2,1},{3,4},{4,3},{5,6},{6,5},{7,8},{8,7},{9,10},{10,9},{11,... | collective-permute-start | bytes 12296 | tf_op jit(solution)/shard_map/ppermute | solution.py:511
  18.0 1.9 %collective-permute-start.7 = (f32[8,128]{1,0:T(8,128)S(1)}, f32[8,128]{1,0:T(8,128)S(1)}, u32[]{:S(2)}, u32[]{:S(2)}) collective-permute-start(f32[8,128]{1,0:T(8,128)S(1)} %get-tuple-element.174), channel_id=1, source_target_pairs={{0,1},{1,0},{2,3},{3,2},{4,5},{5,4},{6,7},{7,6},{8,9},{9,8},{10,11... | collective-permute-start | bytes 12296 | tf_op jit(solution)/shard_map/ppermute | solution.py:512
  19.9 1.4 %shard_map.62 = (f32[16,2048]{1,0:T(8,128)S(1)}, f32[16,2048]{1,0:T(8,128)S(1)}) custom-call(f32[48,128]{1,0:T(8,128)S(1)} %get-tuple-element.168.past_ref, s32[16,2048]{1,0:T(8,128)S(1)} %get-tuple-element.163.index_ref, f32[48,128]{1,0:T(8,128)S(1)} %get-tuple-element.169.rest_0_.diag_ref), custom_call_target="tpu_custom_call" | custom-call | flops 2000000 | bytes 400000 | tf_op jit(solution)/shard_map/pallas_call | solution.py:490
  21.3 0.0 collective-permute-done.6.near_b
  21.3 0.0 collective-permute-done.7.near_a
  21.3 1.1 %shard_map.63 = (f32[48,128]{1,0:T(8,128)S(1)}, f32[48,128]{1,0:T(8,128)S(1)}, f32[16,128]{1,0:T(8,128)S(1)}, f32[8,128]{1,0:T(8,128)S(1)}, f32[8,128]{1,0:T(8,128)S(1)}) custom-call(f32[48,128]{1,0:T(8,128)S(1)} %get-tuple-element.168.past_ref, f32[16,2048]{1,0:T(8,128)S(1)} %get-tuple-element.170.corner_ref, f32[16,2048]{1,0:T(8,128)S(1)} %get-tuple-element.171.scale_ref, ...), custom_call_target="tpu_custom_call" | custom-call | tf_op jit(solution)/shard_map/pallas_call | solution.py:490
  22.5 3.6 %collective-permute-start.8 = (f32[8,128]{1,0:T(8,128)S(1)}, f32[8,128]{1,0:T(8,128)S(1)}, u32[]{:S(2)}, u32[]{:S(2)}) collective-permute-start(f32[8,128]{1,0:T(8,128)S(1)} %get-tuple-element.176), channel_id=1, source_target_pairs={{1,2},{2,1},{3,4},{4,3},{5,6},{6,5},{7,8},{8,7},{9,10},{10,9},{11,... | collective-permute-start | bytes 12296 | tf_op jit(solution)/shard_map/ppermute | solution.py:511
  26.1 1.9 %collective-permute-start.9 = (f32[8,128]{1,0:T(8,128)S(1)}, f32[8,128]{1,0:T(8,128)S(1)}, u32[]{:S(2)}, u32[]{:S(2)}) collective-permute-start(f32[8,128]{1,0:T(8,128)S(1)} %get-tuple-element.177), channel_id=1, source_target_pairs={{0,1},{1,0},{2,3},{3,2},{4,5},{5,4},{6,7},{7,6},{8,9},{9,8},{10,11... | collective-permute-start | bytes 12296 | tf_op jit(solution)/shard_map/ppermute | solution.py:512
  28.0 0.7 shard_map.64.corner_ref
  28.7 0.0 collective-permute-done.8.near_b
  28.8 0.4 collective-permute-done.9.near_a
  29.2 1.1 %shard_map.65 = (f32[48,128]{1,0:T(8,128)S(1)}, f32[48,128]{1,0:T(8,128)S(1)}, f32[16,128]{1,0:T(8,128)S(1)}, f32[8,128]{1,0:T(8,128)S(1)}, f32[8,128]{1,0:T(8,128)S(1)}) custom-call(f32[48,128]{1,0:T(8,128)S(1)} %get-tuple-element.175.past_ref, f32[16,2048]{1,0:T(8,128)S(1)} %shard_map.64.corner_ref, f32[16,2048]{1,0:T(8,128)S(1)} %get-tuple-element.171.scale_ref, ...), custom_call_target="tpu_custom_call" | custom-call | tf_op jit(solution)/shard_map/pallas_call | solution.py:490
  30.3 2.1 %collective-permute-start.10 = (f32[8,128]{1,0:T(8,128)S(1)}, f32[8,128]{1,0:T(8,128)S(1)}, u32[]{:S(2)}, u32[]{:S(2)}) collective-permute-start(f32[8,128]{1,0:T(8,128)S(1)} %get-tuple-element.179), channel_id=1, source_target_pairs={{1,2},{2,1},{3,4},{4,3},{5,6},{6,5},{7,8},{8,7},{9,10},{10,9},{11,... | collective-permute-start | bytes 12296 | tf_op jit(solution)/shard_map/ppermute | solution.py:511
  32.4 1.9 %collective-permute-start.11 = (f32[8,128]{1,0:T(8,128)S(1)}, f32[8,128]{1,0:T(8,128)S(1)}, u32[]{:S(2)}, u32[]{:S(2)}) collective-permute-start(f32[8,128]{1,0:T(8,128)S(1)} %get-tuple-element.180), channel_id=1, source_target_pairs={{0,1},{1,0},{2,3},{3,2},{4,5},{5,4},{6,7},{7,6},{8,9},{9,8},{10,11... | collective-permute-start | bytes 12296 | tf_op jit(solution)/shard_map/ppermute | solution.py:512
  34.3 0.7 shard_map.66.corner_ref
  35.0 0.2 collective-permute-done.10.near_b
  35.2 0.2 collective-permute-done.11.near_a
  35.5 1.2 %shard_map.67 = (f32[48,128]{1,0:T(8,128)S(1)}, f32[48,128]{1,0:T(8,128)S(1)}, f32[32,8,128]{2,1,0:T(8,128)S(1)}) custom-call(f32[48,128]{1,0:T(8,128)S(1)} %get-tuple-element.178.past_ref, f32[16,2048]{1,0:T(8,128)S(1)} %shard_map.66.corner_ref, f32[16,2048]{1,0:T(8,128)S(1)} %get-tuple-element.171.scale_ref, s32[16,2048]{1,0:T(8,128)S(1)} %get-tuple-element.172.place_ref, ...), custom_call_target="tpu_custom_call" | custom-call | tf_op jit(solution)/shard_map/pallas_call | solution.py:490
  36.6 29.6 %all_to_all.10.message_ref = f32[32,8,128]{2,1,0:T(8,128)S(1)} all-to-all(f32[32,8,128]{2,1,0:T(8,128)S(1)} %get-tuple-element.184), channel_id=1, replica_groups=mesh['x'=4,'z'=16,'y'=4,'c'=2] {'x','y','c'}, dimensions={0} | all-to-all | bytes 262144 | tf_op jit(solution)/shard_map/all_to_all | solution.py:607
  66.3 15.6 %all_to_all.11.message_ref = f32[16,8,128]{2,1,0:T(8,128)S(1)} all-to-all(f32[16,8,128]{2,1,0:T(8,128)S(1)} %get-tuple-element.185), channel_id=1, replica_groups=mesh['x'=4,'z'=16,'y'=4,'c'=2] {'z'}, dimensions={0} | all-to-all | bytes 131072 | tf_op jit(solution)/shard_map/all_to_all | solution.py:609
  81.9 0.8 %shard_map.69 = (f32[3,2048]{1,0:T(4,128)}, f32[3,2048]{1,0:T(4,128)}, s32[1,1]{1,0:T(1,128)}) custom-call(f32[16,8,128]{2,1,0:T(8,128)S(1)} %all_to_all.11.message_ref, f32[16,128]{1,0:T(8,128)S(1)} %get-tuple-element.186.direct_ref, f32[48,128]{1,0:T(8,128)S(1)} %get-tuple-element.187.image_ref, f32[48,128]{1,0:T(8,128)S(1)} %get-tuple-element.169.rest_0_.diag_ref, ...), custom_call_target="tpu_custom_call" | custom-call | tf_op jit(solution)/shard_map/pallas_call | solution.py:490
  82.7 0.8 while.28
  (1 shorter events, 0.0 us)
Async XLA Ops:
  3.0 11.7 %collective-permute-start.4 = (f32[16,128]{1,0:T(8,128)S(1)}, f32[16,128]{1,0:T(8,128)S(1)}, u32[]{:S(2)}, u32[]{:S(2)}) collective-permute-start(f32[16,128]{1,0:T(8,128)S(1)} %get-tuple-element.166), channel_id=1, source_target_pairs={{1,2},{2,1},{3,4},{4,3},{5,6},{6,5},{7,8},{8,7},{9,10},{10,9},{11,... | collective-permute-start | bytes 24584 | tf_op jit(solution)/shard_map/ppermute | solution.py:511
  7.6 7.1 %collective-permute-start.5 = (f32[16,128]{1,0:T(8,128)S(1)}, f32[16,128]{1,0:T(8,128)S(1)}, u32[]{:S(2)}, u32[]{:S(2)}) collective-permute-start(f32[16,128]{1,0:T(8,128)S(1)} %get-tuple-element.167), channel_id=1, source_target_pairs={{0,1},{1,0},{2,3},{3,2},{4,5},{5,4},{6,7},{7,6},{8,9},{9,8},{10,11... | collective-permute-start | bytes 24584 | tf_op jit(solution)/shard_map/ppermute | solution.py:512
  16.1 5.2 %collective-permute-start.6 = (f32[8,128]{1,0:T(8,128)S(1)}, f32[8,128]{1,0:T(8,128)S(1)}, u32[]{:S(2)}, u32[]{:S(2)}) collective-permute-start(f32[8,128]{1,0:T(8,128)S(1)} %get-tuple-element.173), channel_id=1, source_target_pairs={{1,2},{2,1},{3,4},{4,3},{5,6},{6,5},{7,8},{8,7},{9,10},{10,9},{11,... | collective-permute-start | bytes 12296 | tf_op jit(solution)/shard_map/ppermute | solution.py:511
  18.0 3.3 %collective-permute-start.7 = (f32[8,128]{1,0:T(8,128)S(1)}, f32[8,128]{1,0:T(8,128)S(1)}, u32[]{:S(2)}, u32[]{:S(2)}) collective-permute-start(f32[8,128]{1,0:T(8,128)S(1)} %get-tuple-element.174), channel_id=1, source_target_pairs={{0,1},{1,0},{2,3},{3,2},{4,5},{5,4},{6,7},{7,6},{8,9},{9,8},{10,11... | collective-permute-start | bytes 12296 | tf_op jit(solution)/shard_map/ppermute | solution.py:512
  22.5 6.3 %collective-permute-start.8 = (f32[8,128]{1,0:T(8,128)S(1)}, f32[8,128]{1,0:T(8,128)S(1)}, u32[]{:S(2)}, u32[]{:S(2)}) collective-permute-start(f32[8,128]{1,0:T(8,128)S(1)} %get-tuple-element.176), channel_id=1, source_target_pairs={{1,2},{2,1},{3,4},{4,3},{5,6},{6,5},{7,8},{8,7},{9,10},{10,9},{11,... | collective-permute-start | bytes 12296 | tf_op jit(solution)/shard_map/ppermute | solution.py:511
  26.1 3.1 %collective-permute-start.9 = (f32[8,128]{1,0:T(8,128)S(1)}, f32[8,128]{1,0:T(8,128)S(1)}, u32[]{:S(2)}, u32[]{:S(2)}) collective-permute-start(f32[8,128]{1,0:T(8,128)S(1)} %get-tuple-element.177), channel_id=1, source_target_pairs={{0,1},{1,0},{2,3},{3,2},{4,5},{5,4},{6,7},{7,6},{8,9},{9,8},{10,11... | collective-permute-start | bytes 12296 | tf_op jit(solution)/shard_map/ppermute | solution.py:512
  30.3 4.9 %collective-permute-start.10 = (f32[8,128]{1,0:T(8,128)S(1)}, f32[8,128]{1,0:T(8,128)S(1)}, u32[]{:S(2)}, u32[]{:S(2)}) collective-permute-start(f32[8,128]{1,0:T(8,128)S(1)} %get-tuple-element.179), channel_id=1, source_target_pairs={{1,2},{2,1},{3,4},{4,3},{5,6},{6,5},{7,8},{8,7},{9,10},{10,9},{11,... | collective-permute-start | bytes 12296 | tf_op jit(solution)/shard_map/ppermute | solution.py:511
  32.4 3.1 %collective-permute-start.11 = (f32[8,128]{1,0:T(8,128)S(1)}, f32[8,128]{1,0:T(8,128)S(1)}, u32[]{:S(2)}, u32[]{:S(2)}) collective-permute-start(f32[8,128]{1,0:T(8,128)S(1)} %get-tuple-element.180), channel_id=1, source_target_pairs={{0,1},{1,0},{2,3},{3,2},{4,5},{5,4},{6,7},{7,6},{8,9},{9,8},{10,11... | collective-permute-start | bytes 12296 | tf_op jit(solution)/shard_map/ppermute | solution.py:512

commit v6 on v4

--- a/solution.py
+++ b/solution.py
@@ -135,7 +135,7 @@
     ]
     for copy in small[:2] + large + small[2:]:
         copy.start()
-    for copy in small:
+    for copy in small + large:
         copy.wait()
     odd = lax.axis_index("c") == 1
     own = shared_ref[...]
@@ -162,8 +162,6 @@
     row12 = iota((12, 256), 0)
     zero16 = jnp.zeros((), BF16)
     lumped = None
-    for copy in large:
-        copy.wait()
     for block in range(ELEMS // 256):
         for n in range(4):
             span = slice(block * 256, block * 256 + 256)
@@ -174,8 +172,10 @@
                 column = mats_ref[j, :, span].astype(F32)
                 rows.append(jnp.where(mask, bf16_rows(column[j : j + 1, :], 16), zero16))
                 mats_ref[j, :, span] = jnp.where(row12 == j, 0.0, column).astype(BF16)
-            piece = times_one_hot(jnp.concatenate(rows, axis=0), nodes)
+            low = jnp.where(bf16_rows(nodes & 127, 128) == bf16_iota((128, 256)), jnp.ones((), BF16), zero16)
+            piece = lax.dot_general(low, jnp.concatenate(rows, axis=0), (((1,), (1,)), ((), ())), preferred_element_type=F32)
             lumped = piece if lumped is None else lumped + piece
+    lumped = lumped.T
     lumped_out[...] = lumped
     lump_a, lump_b = halos_of(lumped, lists)
     a_out[8:16, :] = lump_a
@@ -341,14 +341,10 @@
     return tuple(lax.axis_index(a) for a in AXES)
 
 
-def slab_slot(slab):
-    return (slab // 128) * 8 + slab % 8
-
-
 def fourth_kernel(
     past_ref, corner_ref, scale_ref, place_ref, diag_ref, lumped_ref, inverse_ref, lists_ref, conn_ref, mats_ref, near_b, near_a,
     sums0, sums1, sums2,
-    basis_out, image_out, message_out, sums_ref,
+    basis_out, image_out, message_out, own_out, sums_ref,
 ):
     halos = late_step(
         past_ref, corner_ref, scale_ref, place_ref, diag_ref, lumped_ref, inverse_ref, lists_ref, conn_ref, mats_ref, near_b, near_a,
@@ -363,47 +359,56 @@
             total = jnp.sum(jnp.broadcast_to(total, (8, 128)), axis=1, keepdims=True)
             moments = jnp.where(lane == 2 * k + t, total, moments)
     moments = jnp.where(sub == 6, moments, 0.0)
-    message_out[...] = jnp.broadcast_to(moments[None], (32, 8, 128))
+    message_out[...] = jnp.broadcast_to(moments[None], (16, 8, 128))
     x, z, y, c = place()
-    slab = ((x * 16 + z) * 4 + y) * 2 + c
     odd = c == 1
-    to_right = jnp.where(sub < 6, jnp.where(odd, halos[1], halos[0]), moments)
-    to_left = jnp.where(sub < 6, jnp.where(odd, halos[0], halos[1]), moments)
-
-    @pl.when(slab < 511)
+    to_right = jnp.where(odd, halos[1], halos[0])
+    to_left = jnp.where(odd, halos[0], halos[1])
+    own_out[0:8, :] = to_right
+    own_out[8:16, :] = to_left
+
+    @pl.when((y == 3) & (c == 1))
     def _():
-        message_out[slab_slot(jnp.minimum(slab + 1, 511))] = to_right
-
-    @pl.when(slab > 0)
+        message_out[(z + 1) % 16] = jnp.where(sub < 6, to_right, moments)
+
+    @pl.when((y == 0) & (c == 0))
     def _():
-        message_out[slab_slot(jnp.maximum(slab - 1, 0))] = to_left
-
-
-def relay_kernel(message_ref, message_out, direct_out):
+        message_out[(z + 15) % 16] = jnp.where(sub < 6, to_left, moments)
+
+
+def neighbour_slots():
+    x, z, y, c = place()
+    slot = x * 8 + y * 2 + c
+    first = (y == 0) & (c == 0)
+    last = (y == 3) & (c == 1)
+    before = jnp.where(first, jnp.where(z > 0, x * 8 + 7, x * 8 - 1), slot - 1)
+    after = jnp.where(last, jnp.where(z < 15, x * 8, x * 8 + 8), slot + 1)
+    return before, after
+
+
+def relay_kernel(message_ref, own_ref, message_out):
     x, z, y, c = place()
     slot = x * 8 + y * 2 + c
     first = (y == 0) & (c == 0)
     last = (y == 3) & (c == 1)
     sub = iota((8, 128), 0)
     moments = message_ref[0]
-    for i in range(1, 32):
+    for i in range(1, 16):
         moments = moments + message_ref[i]
     moments = jnp.where(sub == 6, moments, 0.0)
-    message_out[...] = jnp.broadcast_to(moments[None], (16, 8, 128))
-    source_r = jnp.where(first, jnp.where(z < 15, x * 8 + 7, jnp.maximum(x * 8 - 1, 0)), jnp.maximum(slot - 1, 0))
-    source_l = jnp.where(last, jnp.where(z > 0, x * 8, jnp.minimum(x * 8 + 8, 31)), jnp.minimum(slot + 1, 31))
-    from_left = message_ref[source_r]
-    from_right = message_ref[source_l]
-    direct_out[0:8, :] = from_left
-    direct_out[8:16, :] = from_right
-
-    @pl.when(first)
+    message_out[...] = jnp.broadcast_to(moments[None], (32, 8, 128))
+    to_right = jnp.where(last, message_ref[(z + 15) % 16], own_ref[0:8, :])
+    to_left = jnp.where(first, message_ref[(z + 1) % 16], own_ref[8:16, :])
+    right = jnp.where(last, jnp.where(z > 0, x * 8, x * 8 + 8), slot + 1)
+    left = jnp.where(first, jnp.where(z < 15, x * 8 + 7, x * 8 - 1), slot - 1)
+
+    @pl.when(right < 32)
     def _():
-        message_out[(z + 1) % 16] = jnp.where(sub < 6, from_left, moments)
-
-    @pl.when(last)
+        message_out[jnp.minimum(right, 31)] = jnp.where(sub < 6, to_right, moments)
+
+    @pl.when(left >= 0)
     def _():
-        message_out[(z + 15) % 16] = jnp.where(sub < 6, from_right, moments)
+        message_out[jnp.maximum(left, 0)] = jnp.where(sub < 6, to_left, moments)
 
 
 def coefficients(moment):
@@ -438,25 +443,20 @@
     return accel, resid, good
 
 
-def last_kernel(message_ref, direct_ref, image_ref, diag_ref, inverse_ref, b0, b1, b2, b3, accel_out, resid_out, flag_out):
-    x, z, y, c = place()
-    slab = ((x * 16 + z) * 4 + y) * 2 + c
-    first = (y == 0) & (c == 0)
-    last = (y == 3) & (c == 1)
+def last_kernel(message_ref, image_ref, diag_ref, inverse_ref, b0, b1, b2, b3, accel_out, resid_out, flag_out):
+    before, after = neighbour_slots()
+    odd = lax.axis_index("c") == 1
     lane = iota((8, 128), 1)
     total = message_ref[0]
-    for i in range(1, 16):
+    for i in range(1, 32):
         total = total + message_ref[i]
     total = jnp.broadcast_to(total[6:7, :], (8, 128))
     moment = [
         jnp.broadcast_to(jnp.sum(jnp.where(lane == k, total, 0.0), axis=1, keepdims=True), (8, 128)) for k in range(8)
     ]
     accel_coef, resid_coef, good = coefficients(moment)
-    from_left = jnp.where(first, message_ref[(z + 15) % 16], direct_ref[0:8, :])
-    from_right = jnp.where(last, message_ref[(z + 1) % 16], direct_ref[8:16, :])
-    from_left = jnp.where(slab > 0, from_left, 0.0)
-    from_right = jnp.where(slab < 511, from_right, 0.0)
-    odd = c == 1
+    from_left = jnp.where(before >= 0, message_ref[jnp.maximum(before, 0)], 0.0)
+    from_right = jnp.where(after < 32, message_ref[jnp.minimum(after, 31)], 0.0)
     near = [jnp.where(odd, from_left, from_right), jnp.where(odd, from_right, from_left)]
     diag = diag_ref[...]
     image = assembled(image_ref[...], inverse_ref[...], near)
@@ -589,20 +589,20 @@
             basis, image, total, a, b = call(middle_kernel, [field, field, sums, halo, halo], *args)
             bases.append(basis)
             totals.append(total)
-    basis, image, message = call(
+    basis, image, message, own = call(
         fourth_kernel,
-        [field, field, ((32, 8, 128), F32)],
+        [field, field, ((16, 8, 128), F32), sums],
         *args, *totals,
         scratch=[pltpu.VMEM((16, 128), F32)],
     )
     bases.append(basis)
+    message = lax.all_to_all(message, "z", 0, 0, tiled=True)
+    (message,) = call(relay_kernel, [((32, 8, 128), F32)], message, own)
     message = lax.all_to_all(message, GROUP, 0, 0, tiled=True)
-    message, direct = call(relay_kernel, [((16, 8, 128), F32), sums], message)
-    message = lax.all_to_all(message, "z", 0, 0, tiled=True)
     accel, residual, flag = call(
         last_kernel,
         [((3, NODES), F32), ((3, NODES), F32), ((1, 1), jnp.int32)],
-        message, direct, image, diag, inverse, *bases,
+        message, image, diag, inverse, *bases,
         smem_out=2,
     )
 

time: 84.1 us -> 84.5 us (level)
    all_to_all x1, blocking collectives: 16.4 us -> 31.8 us  [body(): message = lax.all_to_all(message, 'z', 0, 0, tiled=True)]
    all_to_all x1, blocking collectives: 30.1 us -> 15.2 us  [body(): message = lax.all_to_all(message, GROUP, 0, 0, tiled=True)]
where the time goes in v6:
time: 84.5 us; the launch traced here: 84.1 us
  blocking collectives  47 us (56%)
  starting transfers between devices  22.9 us (27%)
  Pallas kernels  11.6 us (14%)
  between operations  0.99 us (1%)
    all_to_all x1, blocking collectives, body(): message = lax.all_to_all(message, 'z', 0, 0, tiled=True)  31.8 us
    all_to_all x1, blocking collectives, body(): message = lax.all_to_all(message, GROUP, 0, 0, tiled=True)  15.2 us
    ppermute x4, starting transfers between devices, swap(): lax.ppermute(side_b, AXES, [(i, (i + 1 ^ 1) - 1) for i in range(1, count...  12.2 us
    pallas_call x11, Pallas kernels, call(): pl.pallas_call(kernel, out_shape=[jax.ShapeDtypeStruct(s, t) for s, t in...  11.6 us
    ppermute x4, starting transfers between devices, swap(): from_a = lax.ppermute(side_a, AXES, [(i, i ^ 1) for i in range(count)])  10.6 us
  transfers between devices with their start and end apart: 8, of which 3 were waited for; matrix products, arithmetic and copies ran while one was open for 0% of the time, Pallas kernels for 4%

profile of v6, /device:TPU:1, one launch (start us, length us, event | category | flops | bytes accessed | tf_op | source)
XLA Modules:
  0.0 84.1 jit_solution(10547484409494914912)
XLA Ops:
  0.6 2.2 %shard_map.59 = (f32[48,128]{1,0:T(8,128)S(1)}, f32[48,128]{1,0:T(8,128)S(1)}, bf16[12,12,2048]{2,1,0:T(8,128)(2,1)S(1)}, s32[4,2048]{1,0:T(4,128)S(1)}, s32[16,...) custom-call(f32[3,2048]{1,0:T(4,128)} %load_hbm.1, bf16[12,12,2048]{2,1,0:T(8,128)(2,1)} %mats_hbm.1, ...), custom_call_target="tpu_custom_call" | custom-call | tf_op jit(solution)/shard_map/pallas_call | solution.py:484
  2.9 4.6 %collective-permute-start.4 = (f32[16,128]{1,0:T(8,128)S(1)}, f32[16,128]{1,0:T(8,128)S(1)}, u32[]{:S(2)}, u32[]{:S(2)}) collective-permute-start(f32[16,128]{1,0:T(8,128)S(1)} %get-tuple-element.163), channel_id=1, source_target_pairs={{1,2},{2,1},{3,4},{4,3},{5,6},{6,5},{7,8},{8,7},{9,10},{10,9},{11,... | collective-permute-start | bytes 24584 | tf_op jit(solution)/shard_map/ppermute | solution.py:505
  7.5 4.9 %collective-permute-start.5 = (f32[16,128]{1,0:T(8,128)S(1)}, f32[16,128]{1,0:T(8,128)S(1)}, u32[]{:S(2)}, u32[]{:S(2)}) collective-permute-start(f32[16,128]{1,0:T(8,128)S(1)} %get-tuple-element.164), channel_id=1, source_target_pairs={{0,1},{1,0},{2,3},{3,2},{4,5},{5,4},{6,7},{7,6},{8,9},{9,8},{10,11... | collective-permute-start | bytes 24584 | tf_op jit(solution)/shard_map/ppermute | solution.py:506
  12.3 0.9 %shard_map.60 = (s32[16,2048]{1,0:T(8,128)S(1)}, s32[16,128]{1,0:T(8,128)S(1)}, s32[16,2048]{1,0:T(8,128)S(1)}) custom-call(s32[4,2048]{1,0:T(4,128)S(1)} %get-tuple-element.158.conn_ref, s32[16,128]{1,0:T(8,128)S(1)} %get-tuple-element.159.lists_ref), custom_call_target="tpu_custom_call" | custom-call | flops 2000000 | bytes 400000 | tf_op jit(solution)/shard_map/pallas_call | solution.py:484
  13.2 0.0 collective-permute-done.4.near_b
  13.2 0.0 collective-permute-done.5.near_a
  13.2 1.5 %shard_map.61 = (f32[48,128]{1,0:T(8,128)S(1)}, f32[48,128]{1,0:T(8,128)S(1)}, f32[48,128]{1,0:T(8,128)S(1)}, f32[16,128]{1,0:T(8,128)S(1)}, f32[8,128]{1,0:T(8,128)S(1)}, /*index=5*/f32[8,128]{1,0:T(8,128)S(1)}) custom-call(f32[48,128]{1,0:T(8,128)S(1)} %get-tuple-element.156.load_ref, f32[48,128]{1,0:T(8,128)S(1)} %get-tuple-element.157.lumped_ref, ...), custom_call_target="tpu_custom_call" | custom-call | tf_op jit(solution)/shard_map/pallas_call | solution.py:484
  14.7 1.9 %collective-permute-start.6 = (f32[8,128]{1,0:T(8,128)S(1)}, f32[8,128]{1,0:T(8,128)S(1)}, u32[]{:S(2)}, u32[]{:S(2)}) collective-permute-start(f32[8,128]{1,0:T(8,128)S(1)} %get-tuple-element.170), channel_id=1, source_target_pairs={{1,2},{2,1},{3,4},{4,3},{5,6},{6,5},{7,8},{8,7},{9,10},{10,9},{11,... | collective-permute-start | bytes 12296 | tf_op jit(solution)/shard_map/ppermute | solution.py:505
  16.6 1.9 %collective-permute-start.7 = (f32[8,128]{1,0:T(8,128)S(1)}, f32[8,128]{1,0:T(8,128)S(1)}, u32[]{:S(2)}, u32[]{:S(2)}) collective-permute-start(f32[8,128]{1,0:T(8,128)S(1)} %get-tuple-element.171), channel_id=1, source_target_pairs={{0,1},{1,0},{2,3},{3,2},{4,5},{5,4},{6,7},{7,6},{8,9},{9,8},{10,11... | collective-permute-start | bytes 12296 | tf_op jit(solution)/shard_map/ppermute | solution.py:506
  18.6 1.4 %shard_map.62 = (f32[16,2048]{1,0:T(8,128)S(1)}, f32[16,2048]{1,0:T(8,128)S(1)}) custom-call(f32[48,128]{1,0:T(8,128)S(1)} %get-tuple-element.165.past_ref, s32[16,2048]{1,0:T(8,128)S(1)} %get-tuple-element.161.index_ref, f32[48,128]{1,0:T(8,128)S(1)} %get-tuple-element.166.rest_0_.diag_ref), custom_call_target="tpu_custom_call" | custom-call | flops 2000000 | bytes 400000 | tf_op jit(solution)/shard_map/pallas_call | solution.py:484
  19.9 0.0 collective-permute-done.6.near_b
  19.9 0.0 collective-permute-done.7.near_a
  19.9 1.1 %shard_map.63 = (f32[48,128]{1,0:T(8,128)S(1)}, f32[48,128]{1,0:T(8,128)S(1)}, f32[16,128]{1,0:T(8,128)S(1)}, f32[8,128]{1,0:T(8,128)S(1)}, f32[8,128]{1,0:T(8,128)S(1)}) custom-call(f32[48,128]{1,0:T(8,128)S(1)} %get-tuple-element.165.past_ref, f32[16,2048]{1,0:T(8,128)S(1)} %get-tuple-element.167.corner_ref, f32[16,2048]{1,0:T(8,128)S(1)} %get-tuple-element.168.scale_ref, ...), custom_call_target="tpu_custom_call" | custom-call | tf_op jit(solution)/shard_map/pallas_call | solution.py:484
  21.1 3.6 %collective-permute-start.8 = (f32[8,128]{1,0:T(8,128)S(1)}, f32[8,128]{1,0:T(8,128)S(1)}, u32[]{:S(2)}, u32[]{:S(2)}) collective-permute-start(f32[8,128]{1,0:T(8,128)S(1)} %get-tuple-element.173), channel_id=1, source_target_pairs={{1,2},{2,1},{3,4},{4,3},{5,6},{6,5},{7,8},{8,7},{9,10},{10,9},{11,... | collective-permute-start | bytes 12296 | tf_op jit(solution)/shard_map/ppermute | solution.py:505
  24.7 1.9 %collective-permute-start.9 = (f32[8,128]{1,0:T(8,128)S(1)}, f32[8,128]{1,0:T(8,128)S(1)}, u32[]{:S(2)}, u32[]{:S(2)}) collective-permute-start(f32[8,128]{1,0:T(8,128)S(1)} %get-tuple-element.174), channel_id=1, source_target_pairs={{0,1},{1,0},{2,3},{3,2},{4,5},{5,4},{6,7},{7,6},{8,9},{9,8},{10,11... | collective-permute-start | bytes 12296 | tf_op jit(solution)/shard_map/ppermute | solution.py:506
  26.7 0.7 shard_map.64.corner_ref
  27.4 0.0 collective-permute-done.8.near_b
  27.4 0.4 collective-permute-done.9.near_a
  27.8 1.1 %shard_map.65 = (f32[48,128]{1,0:T(8,128)S(1)}, f32[48,128]{1,0:T(8,128)S(1)}, f32[16,128]{1,0:T(8,128)S(1)}, f32[8,128]{1,0:T(8,128)S(1)}, f32[8,128]{1,0:T(8,128)S(1)}) custom-call(f32[48,128]{1,0:T(8,128)S(1)} %get-tuple-element.172.past_ref, f32[16,2048]{1,0:T(8,128)S(1)} %shard_map.64.corner_ref, f32[16,2048]{1,0:T(8,128)S(1)} %get-tuple-element.168.scale_ref, ...), custom_call_target="tpu_custom_call" | custom-call | tf_op jit(solution)/shard_map/pallas_call | solution.py:484
  28.9 2.1 %collective-permute-start.10 = (f32[8,128]{1,0:T(8,128)S(1)}, f32[8,128]{1,0:T(8,128)S(1)}, u32[]{:S(2)}, u32[]{:S(2)}) collective-permute-start(f32[8,128]{1,0:T(8,128)S(1)} %get-tuple-element.176), channel_id=1, source_target_pairs={{1,2},{2,1},{3,4},{4,3},{5,6},{6,5},{7,8},{8,7},{9,10},{10,9},{11,... | collective-permute-start | bytes 12296 | tf_op jit(solution)/shard_map/ppermute | solution.py:505
  31.0 1.9 %collective-permute-start.11 = (f32[8,128]{1,0:T(8,128)S(1)}, f32[8,128]{1,0:T(8,128)S(1)}, u32[]{:S(2)}, u32[]{:S(2)}) collective-permute-start(f32[8,128]{1,0:T(8,128)S(1)} %get-tuple-element.177), channel_id=1, source_target_pairs={{0,1},{1,0},{2,3},{3,2},{4,5},{5,4},{6,7},{7,6},{8,9},{9,8},{10,11... | collective-permute-start | bytes 12296 | tf_op jit(solution)/shard_map/ppermute | solution.py:506
  32.9 0.7 shard_map.66.corner_ref
  33.6 0.2 collective-permute-done.10.near_b
  33.8 0.2 collective-permute-done.11.near_a
  34.1 1.1 %shard_map.67 = (f32[48,128]{1,0:T(8,128)S(1)}, f32[48,128]{1,0:T(8,128)S(1)}, f32[16,8,128]{2,1,0:T(8,128)S(1)}, f32[16,128]{1,0:T(8,128)S(1)}) custom-call(f32[48,128]{1,0:T(8,128)S(1)} %get-tuple-element.175.past_ref, f32[16,2048]{1,0:T(8,128)S(1)} %shard_map.66.corner_ref, f32[16,2048]{1,0:T(8,128)S(1)} %get-tuple-element.168.scale_ref, ...), custom_call_target="tpu_custom_call" | custom-call | tf_op jit(solution)/shard_map/pallas_call | solution.py:484
  35.2 31.8 %all_to_all.10.message_ref = f32[16,8,128]{2,1,0:T(8,128)S(1)} all-to-all(f32[16,8,128]{2,1,0:T(8,128)S(1)} %get-tuple-element.181), channel_id=1, replica_groups=mesh['x'=4,'z'=16,'y'=4,'c'=2] {'z'}, dimensions={0} | all-to-all | bytes 131072 | tf_op jit(solution)/shard_map/all_to_all | solution.py:599
  67.0 15.2 %all_to_all.11.message_ref = f32[32,8,128]{2,1,0:T(8,128)S(1)} all-to-all(f32[32,8,128]{2,1,0:T(8,128)S(1)} %shard_map.68), channel_id=1, replica_groups=mesh['x'=4,'z'=16,'y'=4,'c'=2] {'x','y','c'}, dimensions={0} | all-to-all | bytes 262144 | tf_op jit(solution)/shard_map/all_to_all | solution.py:601
  82.2 0.9 %shard_map.69 = (f32[3,2048]{1,0:T(4,128)}, f32[3,2048]{1,0:T(4,128)}, s32[1,1]{1,0:T(1,128)}) custom-call(f32[32,8,128]{2,1,0:T(8,128)S(1)} %all_to_all.11.message_ref, f32[48,128]{1,0:T(8,128)S(1)} %get-tuple-element.183.image_ref, f32[48,128]{1,0:T(8,128)S(1)} %get-tuple-element.166.rest_0_.diag_ref, s32[16,128]{1,0:T(8,128)S(1)} %get-tuple-element.160.inverse_ref, ...), custom_call_target="tpu_custom_call" | custom-call | tf_op jit(solution)/shard_map/pallas_call | solution.py:484
  83.1 0.8 while.28
  (1 shorter events, 0.0 us)
Async XLA Ops:
  2.9 10.4 %collective-permute-start.4 = (f32[16,128]{1,0:T(8,128)S(1)}, f32[16,128]{1,0:T(8,128)S(1)}, u32[]{:S(2)}, u32[]{:S(2)}) collective-permute-start(f32[16,128]{1,0:T(8,128)S(1)} %get-tuple-element.163), channel_id=1, source_target_pairs={{1,2},{2,1},{3,4},{4,3},{5,6},{6,5},{7,8},{8,7},{9,10},{10,9},{11,... | collective-permute-start | bytes 24584 | tf_op jit(solution)/shard_map/ppermute | solution.py:505
  7.5 5.8 %collective-permute-start.5 = (f32[16,128]{1,0:T(8,128)S(1)}, f32[16,128]{1,0:T(8,128)S(1)}, u32[]{:S(2)}, u32[]{:S(2)}) collective-permute-start(f32[16,128]{1,0:T(8,128)S(1)} %get-tuple-element.164), channel_id=1, source_target_pairs={{0,1},{1,0},{2,3},{3,2},{4,5},{5,4},{6,7},{7,6},{8,9},{9,8},{10,11... | collective-permute-start | bytes 24584 | tf_op jit(solution)/shard_map/ppermute | solution.py:506
  14.7 5.2 %collective-permute-start.6 = (f32[8,128]{1,0:T(8,128)S(1)}, f32[8,128]{1,0:T(8,128)S(1)}, u32[]{:S(2)}, u32[]{:S(2)}) collective-permute-start(f32[8,128]{1,0:T(8,128)S(1)} %get-tuple-element.170), channel_id=1, source_target_pairs={{1,2},{2,1},{3,4},{4,3},{5,6},{6,5},{7,8},{8,7},{9,10},{10,9},{11,... | collective-permute-start | bytes 12296 | tf_op jit(solution)/shard_map/ppermute | solution.py:505
  16.6 3.3 %collective-permute-start.7 = (f32[8,128]{1,0:T(8,128)S(1)}, f32[8,128]{1,0:T(8,128)S(1)}, u32[]{:S(2)}, u32[]{:S(2)}) collective-permute-start(f32[8,128]{1,0:T(8,128)S(1)} %get-tuple-element.171), channel_id=1, source_target_pairs={{0,1},{1,0},{2,3},{3,2},{4,5},{5,4},{6,7},{7,6},{8,9},{9,8},{10,11... | collective-permute-start | bytes 12296 | tf_op jit(solution)/shard_map/ppermute | solution.py:506
  21.1 6.3 %collective-permute-start.8 = (f32[8,128]{1,0:T(8,128)S(1)}, f32[8,128]{1,0:T(8,128)S(1)}, u32[]{:S(2)}, u32[]{:S(2)}) collective-permute-start(f32[8,128]{1,0:T(8,128)S(1)} %get-tuple-element.173), channel_id=1, source_target_pairs={{1,2},{2,1},{3,4},{4,3},{5,6},{6,5},{7,8},{8,7},{9,10},{10,9},{11,... | collective-permute-start | bytes 12296 | tf_op jit(solution)/shard_map/ppermute | solution.py:505
  24.7 3.1 %collective-permute-start.9 = (f32[8,128]{1,0:T(8,128)S(1)}, f32[8,128]{1,0:T(8,128)S(1)}, u32[]{:S(2)}, u32[]{:S(2)}) collective-permute-start(f32[8,128]{1,0:T(8,128)S(1)} %get-tuple-element.174), channel_id=1, source_target_pairs={{0,1},{1,0},{2,3},{3,2},{4,5},{5,4},{6,7},{7,6},{8,9},{9,8},{10,11... | collective-permute-start | bytes 12296 | tf_op jit(solution)/shard_map/ppermute | solution.py:506
  28.9 4.9 %collective-permute-start.10 = (f32[8,128]{1,0:T(8,128)S(1)}, f32[8,128]{1,0:T(8,128)S(1)}, u32[]{:S(2)}, u32[]{:S(2)}) collective-permute-start(f32[8,128]{1,0:T(8,128)S(1)} %get-tuple-element.176), channel_id=1, source_target_pairs={{1,2},{2,1},{3,4},{4,3},{5,6},{6,5},{7,8},{8,7},{9,10},{10,9},{11,... | collective-permute-start | bytes 12296 | tf_op jit(solution)/shard_map/ppermute | solution.py:505
  31.0 3.1 %collective-permute-start.11 = (f32[8,128]{1,0:T(8,128)S(1)}, f32[8,128]{1,0:T(8,128)S(1)}, u32[]{:S(2)}, u32[]{:S(2)}) collective-permute-start(f32[8,128]{1,0:T(8,128)S(1)} %get-tuple-element.177), channel_id=1, source_target_pairs={{0,1},{1,0},{2,3},{3,2},{4,5},{5,4},{6,7},{7,6},{8,9},{9,8},{10,11... | collective-permute-start | bytes 12296 | tf_op jit(solution)/shard_map/ppermute | solution.py:506

commit v7 on v4

--- a/solution.py
+++ b/solution.py
@@ -135,7 +135,7 @@
     ]
     for copy in small[:2] + large + small[2:]:
         copy.start()
-    for copy in small:
+    for copy in small + large:
         copy.wait()
     odd = lax.axis_index("c") == 1
     own = shared_ref[...]
@@ -162,8 +162,6 @@
     row12 = iota((12, 256), 0)
     zero16 = jnp.zeros((), BF16)
     lumped = None
-    for copy in large:
-        copy.wait()
     for block in range(ELEMS // 256):
         for n in range(4):
             span = slice(block * 256, block * 256 + 256)
@@ -174,8 +172,10 @@
                 column = mats_ref[j, :, span].astype(F32)
                 rows.append(jnp.where(mask, bf16_rows(column[j : j + 1, :], 16), zero16))
                 mats_ref[j, :, span] = jnp.where(row12 == j, 0.0, column).astype(BF16)
-            piece = times_one_hot(jnp.concatenate(rows, axis=0), nodes)
+            low = jnp.where(bf16_rows(nodes & 127, 128) == bf16_iota((128, 256)), jnp.ones((), BF16), zero16)
+            piece = lax.dot_general(low, jnp.concatenate(rows, axis=0), (((1,), (1,)), ((), ())), preferred_element_type=F32)
             lumped = piece if lumped is None else lumped + piece
+    lumped = lumped.T
     lumped_out[...] = lumped
     lump_a, lump_b = halos_of(lumped, lists)
     a_out[8:16, :] = lump_a

time: 84.1 us -> 84 us (level)
  no operation moved by 1% of the time
where the time goes in v7:
time: 84 us; the launch traced here: 83.6 us
  blocking collectives  46.5 us (55%)
  starting transfers between devices  22.9 us (27%)
  Pallas kernels  11.6 us (14%)
  between operations  0.99 us (1%)
    all_to_all x1, blocking collectives, body(): message = lax.all_to_all(message, GROUP, 0, 0, tiled=True)  30.1 us
    all_to_all x1, blocking collectives, body(): message = lax.all_to_all(message, 'z', 0, 0, tiled=True)  16.4 us
    ppermute x4, starting transfers between devices, swap(): lax.ppermute(side_b, AXES, [(i, (i + 1 ^ 1) - 1) for i in range(1, count...  12.2 us
    pallas_call x11, Pallas kernels, call(): pl.pallas_call(kernel, out_shape=[jax.ShapeDtypeStruct(s, t) for s, t in...  11.6 us
    ppermute x4, starting transfers between devices, swap(): from_a = lax.ppermute(side_a, AXES, [(i, i ^ 1) for i in range(count)])  10.6 us
  transfers between devices with their start and end apart: 8, of which 3 were waited for; matrix products, arithmetic and copies ran while one was open for 0% of the time, Pallas kernels for 4%

profile of v7, /device:TPU:1, one launch (start us, length us, event | category | flops | bytes accessed | tf_op | source)
XLA Modules:
  0.0 83.6 jit_solution(1204320435748392507)
XLA Ops:
  0.6 2.2 %shard_map.59 = (f32[48,128]{1,0:T(8,128)S(1)}, f32[48,128]{1,0:T(8,128)S(1)}, bf16[12,12,2048]{2,1,0:T(8,128)(2,1)S(1)}, s32[4,2048]{1,0:T(4,128)S(1)}, s32[16,...) custom-call(f32[3,2048]{1,0:T(4,128)} %load_hbm.1, bf16[12,12,2048]{2,1,0:T(8,128)(2,1)} %mats_hbm.1, ...), custom_call_target="tpu_custom_call" | custom-call | tf_op jit(solution)/shard_map/pallas_call | solution.py:484
  2.9 4.6 %collective-permute-start.4 = (f32[16,128]{1,0:T(8,128)S(1)}, f32[16,128]{1,0:T(8,128)S(1)}, u32[]{:S(2)}, u32[]{:S(2)}) collective-permute-start(f32[16,128]{1,0:T(8,128)S(1)} %get-tuple-element.164), channel_id=1, source_target_pairs={{1,2},{2,1},{3,4},{4,3},{5,6},{6,5},{7,8},{8,7},{9,10},{10,9},{11,... | collective-permute-start | bytes 24584 | tf_op jit(solution)/shard_map/ppermute | solution.py:505
  7.5 4.9 %collective-permute-start.5 = (f32[16,128]{1,0:T(8,128)S(1)}, f32[16,128]{1,0:T(8,128)S(1)}, u32[]{:S(2)}, u32[]{:S(2)}) collective-permute-start(f32[16,128]{1,0:T(8,128)S(1)} %get-tuple-element.165), channel_id=1, source_target_pairs={{0,1},{1,0},{2,3},{3,2},{4,5},{5,4},{6,7},{7,6},{8,9},{9,8},{10,11... | collective-permute-start | bytes 24584 | tf_op jit(solution)/shard_map/ppermute | solution.py:506
  12.3 0.9 %shard_map.60 = (s32[16,2048]{1,0:T(8,128)S(1)}, s32[16,128]{1,0:T(8,128)S(1)}, s32[16,2048]{1,0:T(8,128)S(1)}) custom-call(s32[4,2048]{1,0:T(4,128)S(1)} %get-tuple-element.159.conn_ref, s32[16,128]{1,0:T(8,128)S(1)} %get-tuple-element.160.lists_ref), custom_call_target="tpu_custom_call" | custom-call | flops 2000000 | bytes 400000 | tf_op jit(solution)/shard_map/pallas_call | solution.py:484
  13.2 0.0 collective-permute-done.4.near_b
  13.2 0.0 collective-permute-done.5.near_a
  13.2 1.5 %shard_map.61 = (f32[48,128]{1,0:T(8,128)S(1)}, f32[48,128]{1,0:T(8,128)S(1)}, f32[48,128]{1,0:T(8,128)S(1)}, f32[16,128]{1,0:T(8,128)S(1)}, f32[8,128]{1,0:T(8,128)S(1)}, /*index=5*/f32[8,128]{1,0:T(8,128)S(1)}) custom-call(f32[48,128]{1,0:T(8,128)S(1)} %get-tuple-element.157.load_ref, f32[48,128]{1,0:T(8,128)S(1)} %get-tuple-element.158.lumped_ref, ...), custom_call_target="tpu_custom_call" | custom-call | tf_op jit(solution)/shard_map/pallas_call | solution.py:484
  14.7 1.9 %collective-permute-start.6 = (f32[8,128]{1,0:T(8,128)S(1)}, f32[8,128]{1,0:T(8,128)S(1)}, u32[]{:S(2)}, u32[]{:S(2)}) collective-permute-start(f32[8,128]{1,0:T(8,128)S(1)} %get-tuple-element.171), channel_id=1, source_target_pairs={{1,2},{2,1},{3,4},{4,3},{5,6},{6,5},{7,8},{8,7},{9,10},{10,9},{11,... | collective-permute-start | bytes 12296 | tf_op jit(solution)/shard_map/ppermute | solution.py:505
  16.6 1.9 %collective-permute-start.7 = (f32[8,128]{1,0:T(8,128)S(1)}, f32[8,128]{1,0:T(8,128)S(1)}, u32[]{:S(2)}, u32[]{:S(2)}) collective-permute-start(f32[8,128]{1,0:T(8,128)S(1)} %get-tuple-element.172), channel_id=1, source_target_pairs={{0,1},{1,0},{2,3},{3,2},{4,5},{5,4},{6,7},{7,6},{8,9},{9,8},{10,11... | collective-permute-start | bytes 12296 | tf_op jit(solution)/shard_map/ppermute | solution.py:506
  18.6 1.4 %shard_map.62 = (f32[16,2048]{1,0:T(8,128)S(1)}, f32[16,2048]{1,0:T(8,128)S(1)}) custom-call(f32[48,128]{1,0:T(8,128)S(1)} %get-tuple-element.166.past_ref, s32[16,2048]{1,0:T(8,128)S(1)} %get-tuple-element.162.index_ref, f32[48,128]{1,0:T(8,128)S(1)} %get-tuple-element.167.rest_0_.diag_ref), custom_call_target="tpu_custom_call" | custom-call | flops 2000000 | bytes 400000 | tf_op jit(solution)/shard_map/pallas_call | solution.py:484
  19.9 0.0 collective-permute-done.6.near_b
  19.9 0.0 collective-permute-done.7.near_a
  19.9 1.1 %shard_map.63 = (f32[48,128]{1,0:T(8,128)S(1)}, f32[48,128]{1,0:T(8,128)S(1)}, f32[16,128]{1,0:T(8,128)S(1)}, f32[8,128]{1,0:T(8,128)S(1)}, f32[8,128]{1,0:T(8,128)S(1)}) custom-call(f32[48,128]{1,0:T(8,128)S(1)} %get-tuple-element.166.past_ref, f32[16,2048]{1,0:T(8,128)S(1)} %get-tuple-element.168.corner_ref, f32[16,2048]{1,0:T(8,128)S(1)} %get-tuple-element.169.scale_ref, ...), custom_call_target="tpu_custom_call" | custom-call | tf_op jit(solution)/shard_map/pallas_call | solution.py:484
  21.1 3.6 %collective-permute-start.8 = (f32[8,128]{1,0:T(8,128)S(1)}, f32[8,128]{1,0:T(8,128)S(1)}, u32[]{:S(2)}, u32[]{:S(2)}) collective-permute-start(f32[8,128]{1,0:T(8,128)S(1)} %get-tuple-element.174), channel_id=1, source_target_pairs={{1,2},{2,1},{3,4},{4,3},{5,6},{6,5},{7,8},{8,7},{9,10},{10,9},{11,... | collective-permute-start | bytes 12296 | tf_op jit(solution)/shard_map/ppermute | solution.py:505
  24.7 1.9 %collective-permute-start.9 = (f32[8,128]{1,0:T(8,128)S(1)}, f32[8,128]{1,0:T(8,128)S(1)}, u32[]{:S(2)}, u32[]{:S(2)}) collective-permute-start(f32[8,128]{1,0:T(8,128)S(1)} %get-tuple-element.175), channel_id=1, source_target_pairs={{0,1},{1,0},{2,3},{3,2},{4,5},{5,4},{6,7},{7,6},{8,9},{9,8},{10,11... | collective-permute-start | bytes 12296 | tf_op jit(solution)/shard_map/ppermute | solution.py:506
  26.7 0.7 shard_map.64.corner_ref
  27.4 0.0 collective-permute-done.8.near_b
  27.4 0.4 collective-permute-done.9.near_a
  27.8 1.1 %shard_map.65 = (f32[48,128]{1,0:T(8,128)S(1)}, f32[48,128]{1,0:T(8,128)S(1)}, f32[16,128]{1,0:T(8,128)S(1)}, f32[8,128]{1,0:T(8,128)S(1)}, f32[8,128]{1,0:T(8,128)S(1)}) custom-call(f32[48,128]{1,0:T(8,128)S(1)} %get-tuple-element.173.past_ref, f32[16,2048]{1,0:T(8,128)S(1)} %shard_map.64.corner_ref, f32[16,2048]{1,0:T(8,128)S(1)} %get-tuple-element.169.scale_ref, ...), custom_call_target="tpu_custom_call" | custom-call | tf_op jit(solution)/shard_map/pallas_call | solution.py:484
  28.9 2.1 %collective-permute-start.10 = (f32[8,128]{1,0:T(8,128)S(1)}, f32[8,128]{1,0:T(8,128)S(1)}, u32[]{:S(2)}, u32[]{:S(2)}) collective-permute-start(f32[8,128]{1,0:T(8,128)S(1)} %get-tuple-element.177), channel_id=1, source_target_pairs={{1,2},{2,1},{3,4},{4,3},{5,6},{6,5},{7,8},{8,7},{9,10},{10,9},{11,... | collective-permute-start | bytes 12296 | tf_op jit(solution)/shard_map/ppermute | solution.py:505
  31.0 1.9 %collective-permute-start.11 = (f32[8,128]{1,0:T(8,128)S(1)}, f32[8,128]{1,0:T(8,128)S(1)}, u32[]{:S(2)}, u32[]{:S(2)}) collective-permute-start(f32[8,128]{1,0:T(8,128)S(1)} %get-tuple-element.178), channel_id=1, source_target_pairs={{0,1},{1,0},{2,3},{3,2},{4,5},{5,4},{6,7},{7,6},{8,9},{9,8},{10,11... | collective-permute-start | bytes 12296 | tf_op jit(solution)/shard_map/ppermute | solution.py:506
  32.9 0.7 shard_map.66.corner_ref
  33.6 0.2 collective-permute-done.10.near_b
  33.8 0.2 collective-permute-done.11.near_a
  34.1 1.2 %shard_map.67 = (f32[48,128]{1,0:T(8,128)S(1)}, f32[48,128]{1,0:T(8,128)S(1)}, f32[32,8,128]{2,1,0:T(8,128)S(1)}) custom-call(f32[48,128]{1,0:T(8,128)S(1)} %get-tuple-element.176.past_ref, f32[16,2048]{1,0:T(8,128)S(1)} %shard_map.66.corner_ref, f32[16,2048]{1,0:T(8,128)S(1)} %get-tuple-element.169.scale_ref, s32[16,2048]{1,0:T(8,128)S(1)} %get-tuple-element.170.place_ref, ...), custom_call_target="tpu_custom_call" | custom-call | tf_op jit(solution)/shard_map/pallas_call | solution.py:484
  35.2 30.1 %all_to_all.10.message_ref = f32[32,8,128]{2,1,0:T(8,128)S(1)} all-to-all(f32[32,8,128]{2,1,0:T(8,128)S(1)} %get-tuple-element.182), channel_id=1, replica_groups=mesh['x'=4,'z'=16,'y'=4,'c'=2] {'x','y','c'}, dimensions={0} | all-to-all | bytes 262144 | tf_op jit(solution)/shard_map/all_to_all | solution.py:599
  65.3 16.4 %all_to_all.11.message_ref = f32[16,8,128]{2,1,0:T(8,128)S(1)} all-to-all(f32[16,8,128]{2,1,0:T(8,128)S(1)} %get-tuple-element.183), channel_id=1, replica_groups=mesh['x'=4,'z'=16,'y'=4,'c'=2] {'z'}, dimensions={0} | all-to-all | bytes 131072 | tf_op jit(solution)/shard_map/all_to_all | solution.py:601
  81.8 0.8 %shard_map.69 = (f32[3,2048]{1,0:T(4,128)}, f32[3,2048]{1,0:T(4,128)}, s32[1,1]{1,0:T(1,128)}) custom-call(f32[16,8,128]{2,1,0:T(8,128)S(1)} %all_to_all.11.message_ref, f32[16,128]{1,0:T(8,128)S(1)} %get-tuple-element.184.direct_ref, f32[48,128]{1,0:T(8,128)S(1)} %get-tuple-element.185.image_ref, f32[48,128]{1,0:T(8,128)S(1)} %get-tuple-element.167.rest_0_.diag_ref, ...), custom_call_target="tpu_custom_call" | custom-call | tf_op jit(solution)/shard_map/pallas_call | solution.py:484
  82.6 0.8 while.28
  (1 shorter events, 0.0 us)
Async XLA Ops:
  2.9 10.4 %collective-permute-start.4 = (f32[16,128]{1,0:T(8,128)S(1)}, f32[16,128]{1,0:T(8,128)S(1)}, u32[]{:S(2)}, u32[]{:S(2)}) collective-permute-start(f32[16,128]{1,0:T(8,128)S(1)} %get-tuple-element.164), channel_id=1, source_target_pairs={{1,2},{2,1},{3,4},{4,3},{5,6},{6,5},{7,8},{8,7},{9,10},{10,9},{11,... | collective-permute-start | bytes 24584 | tf_op jit(solution)/shard_map/ppermute | solution.py:505
  7.5 5.8 %collective-permute-start.5 = (f32[16,128]{1,0:T(8,128)S(1)}, f32[16,128]{1,0:T(8,128)S(1)}, u32[]{:S(2)}, u32[]{:S(2)}) collective-permute-start(f32[16,128]{1,0:T(8,128)S(1)} %get-tuple-element.165), channel_id=1, source_target_pairs={{0,1},{1,0},{2,3},{3,2},{4,5},{5,4},{6,7},{7,6},{8,9},{9,8},{10,11... | collective-permute-start | bytes 24584 | tf_op jit(solution)/shard_map/ppermute | solution.py:506
  14.7 5.2 %collective-permute-start.6 = (f32[8,128]{1,0:T(8,128)S(1)}, f32[8,128]{1,0:T(8,128)S(1)}, u32[]{:S(2)}, u32[]{:S(2)}) collective-permute-start(f32[8,128]{1,0:T(8,128)S(1)} %get-tuple-element.171), channel_id=1, source_target_pairs={{1,2},{2,1},{3,4},{4,3},{5,6},{6,5},{7,8},{8,7},{9,10},{10,9},{11,... | collective-permute-start | bytes 12296 | tf_op jit(solution)/shard_map/ppermute | solution.py:505
  16.6 3.3 %collective-permute-start.7 = (f32[8,128]{1,0:T(8,128)S(1)}, f32[8,128]{1,0:T(8,128)S(1)}, u32[]{:S(2)}, u32[]{:S(2)}) collective-permute-start(f32[8,128]{1,0:T(8,128)S(1)} %get-tuple-element.172), channel_id=1, source_target_pairs={{0,1},{1,0},{2,3},{3,2},{4,5},{5,4},{6,7},{7,6},{8,9},{9,8},{10,11... | collective-permute-start | bytes 12296 | tf_op jit(solution)/shard_map/ppermute | solution.py:506
  21.1 6.3 %collective-permute-start.8 = (f32[8,128]{1,0:T(8,128)S(1)}, f32[8,128]{1,0:T(8,128)S(1)}, u32[]{:S(2)}, u32[]{:S(2)}) collective-permute-start(f32[8,128]{1,0:T(8,128)S(1)} %get-tuple-element.174), channel_id=1, source_target_pairs={{1,2},{2,1},{3,4},{4,3},{5,6},{6,5},{7,8},{8,7},{9,10},{10,9},{11,... | collective-permute-start | bytes 12296 | tf_op jit(solution)/shard_map/ppermute | solution.py:505
  24.7 3.1 %collective-permute-start.9 = (f32[8,128]{1,0:T(8,128)S(1)}, f32[8,128]{1,0:T(8,128)S(1)}, u32[]{:S(2)}, u32[]{:S(2)}) collective-permute-start(f32[8,128]{1,0:T(8,128)S(1)} %get-tuple-element.175), channel_id=1, source_target_pairs={{0,1},{1,0},{2,3},{3,2},{4,5},{5,4},{6,7},{7,6},{8,9},{9,8},{10,11... | collective-permute-start | bytes 12296 | tf_op jit(solution)/shard_map/ppermute | solution.py:506
  28.9 4.9 %collective-permute-start.10 = (f32[8,128]{1,0:T(8,128)S(1)}, f32[8,128]{1,0:T(8,128)S(1)}, u32[]{:S(2)}, u32[]{:S(2)}) collective-permute-start(f32[8,128]{1,0:T(8,128)S(1)} %get-tuple-element.177), channel_id=1, source_target_pairs={{1,2},{2,1},{3,4},{4,3},{5,6},{6,5},{7,8},{8,7},{9,10},{10,9},{11,... | collective-permute-start | bytes 12296 | tf_op jit(solution)/shard_map/ppermute | solution.py:505
  31.0 3.1 %collective-permute-start.11 = (f32[8,128]{1,0:T(8,128)S(1)}, f32[8,128]{1,0:T(8,128)S(1)}, u32[]{:S(2)}, u32[]{:S(2)}) collective-permute-start(f32[8,128]{1,0:T(8,128)S(1)} %get-tuple-element.178), channel_id=1, source_target_pairs={{0,1},{1,0},{2,3},{3,2},{4,5},{5,4},{6,7},{7,6},{8,9},{9,8},{10,11... | collective-permute-start | bytes 12296 | tf_op jit(solution)/shard_map/ppermute | solution.py:506
